TPU v7x, 32 devices: a whole 2x2x4 slice. The times are simulated.
32 devices in a mesh: dp: 16 (over z, x, core), mp: 2 (over y).
Axes of the slice: x: 2, y: 2, z: 4, core: 2. Of those that a mesh axis runs over, the one named last changes fastest.
Arguments:
- block_input: bfloat16 [16384, 1152], P(('dp', 'mp')), may hold values from -6 to 6
- out_grad: bfloat16 [16384, 1152], P(('dp', 'mp')), may hold values from -6 to 6
- time_table: bfloat16 [1000, 1152], replicated, may hold values from -6 to 6
- class_table: bfloat16 [1001, 1152], replicated, may hold values from -6 to 6
- time_ids: int32 [64], P('dp'), may hold values from 0 to 999
- class_ids: int32 [64], P('dp'), may hold values from 0 to 1000
- image_patches: int32 [16], P('dp'), may hold values from 256 to 1024, as said below
- ada_weight: bfloat16 [1152, 6912], P(None, 'dp'), may hold values from -0.1875 to 0.1875
- ada_bias: bfloat16 [6912], P('dp'), may hold values from -3 to 3
- proj_weight: bfloat16 [4, 1152, 1152], P(None, 'dp', 'mp'), may hold values from -0.1875 to 0.1875
- decay_down: bfloat16 [1152, 16], replicated, may hold values from -0.1875 to 0.1875
- decay_up: bfloat16 [16, 1152], replicated, may hold values from -1.5 to 1.5
- decay_bias: bfloat16 [1152], replicated, may hold values from 0.5 to 7
- head_gain: bfloat16 [72], replicated, may hold values from 0.25 to 1.75
- conv_taps: bfloat16 [9, 1152], replicated, may hold values from -1.75 to 1.75
- out_weight: bfloat16 [1152, 1152], P('mp', 'dp'), may hold values from -0.1875 to 0.1875
- fc1_weight: bfloat16 [1152, 4608], P('dp', 'mp'), may hold values from -0.1875 to 0.1875
- fc2_weight: bfloat16 [4608, 1152], P('mp', 'dp'), may hold values from -0.09375 to 0.09375
Outputs:
- block_out: bfloat16 [16384, 1152], P(('dp', 'mp'))
- input_grad: float32 [16384, 1152], P(('dp', 'mp'))
- cond_grad: float32 [64, 1152], P('dp')
- ada_weight_grad: float32 [1152, 6912], P(None, 'dp')
- ada_bias_grad: float32 [6912], P('dp')
- proj_grad: float32 [4, 1152, 1152], P(None, 'dp', 'mp')
- decay_down_grad: float32 [1152, 16], replicated
- decay_up_grad: float32 [16, 1152], replicated
- decay_bias_grad: float32 [1152], replicated
- gain_grad: float32 [72], replicated
- conv_grad: float32 [9, 1152], replicated
- out_weight_grad: float32 [1152, 1152], P('mp', 'dp')
- fc1_grad: float32 [1152, 4608], P('dp', 'mp')
- fc2_grad: float32 [4608, 1152], P('mp', 'dp')
Inputs may be any that keep to these rules, and one draw needn't show every extreme that they name: `image_patches`: each unit holds images of one size: its value is 16 * 16 (four small images) or 4 * 16 * 16 (one large image); half of all units, rounded down, hold a large image.
All inputs are finite; a program needn't handle non-finite values.
Results may differ from a plain program's by a relative error of at most 0.0095.
The roundings to bfloat16 on the way count: a program that leaves them out, or rounds other values in their place, can miss the bound.
Values may be sent and summed in bfloat16 or wider, within the bound.
No kernel may reach another device: no remote copies, remote signals or barrier semaphores. Data moves between devices by JAX's collectives and lax.ppermute only.
A program may use at most 320 MiB of HBM per device.

v0:
```python
from functools import partial

import jax
import jax.numpy as jnp
from jax import lax
from jax.sharding import PartitionSpec as P

HDIM = 72
BLOCK_LEN = 64
SIDE = 16


maximum_precision = lax.Precision.HIGHEST
norm_eps = 1e-06
head_eps = 1e-05
gate_norm = 16.0


def shifted(unit_grid, offset):
    row_total = unit_grid.shape[1]
    margin = abs(offset)
    padded = jnp.pad(unit_grid, ((0, 0), (margin, margin), (0, 0)))
    return lax.slice_in_dim(padded, margin + offset, margin + offset + row_total, axis=1)


def depthwise(big_unit, value_matrix, conv_taps):
    row_total, channels = value_matrix.shape
    unit_count = big_unit.shape[0]
    unit_rows = row_total // unit_count
    unit_grid = value_matrix.reshape(unit_count, unit_rows, channels)
    positions = jnp.arange(unit_rows)
    small_pos = positions % (SIDE * SIDE)
    small_row = small_pos // SIDE
    small_col = small_pos % SIDE
    big_row = positions // (2 * SIDE)
    big_col = positions % (2 * SIDE)
    summed = jnp.zeros_like(unit_grid)
    tap_index = 0
    for row_step in (-1, 0, 1):
        for col_step in (-1, 0, 1):
            small_ok = (
                (small_row + row_step >= 0)
                & (small_row + row_step < SIDE)
                & (small_col + col_step >= 0)
                & (small_col + col_step < SIDE)
            ).astype(jnp.float32)
            big_ok = (
                (big_row + row_step >= 0)
                & (big_row + row_step < 2 * SIDE)
                & (big_col + col_step >= 0)
                & (big_col + col_step < 2 * SIDE)
            ).astype(jnp.float32)
            small_val = shifted(unit_grid, row_step * SIDE + col_step) * small_ok[None, :, None]
            big_val = shifted(unit_grid, row_step * 2 * SIDE + col_step) * big_ok[None, :, None]
            chosen = jnp.where(big_unit[:, None, None], big_val, small_val)
            summed = summed + chosen * conv_taps[tap_index]
            tap_index = tap_index + 1
    return summed.reshape(row_total, channels)


def block_step(running_state, inputs):
    query_rows, key_matrix, value_matrix, log_decay, start = inputs
    running_state = jnp.where(start, jnp.zeros_like(running_state), running_state)
    length = query_rows.shape[1]
    prefix_decay = jnp.cumsum(log_decay, axis=1)
    final_decay = prefix_decay[:, -1, :]
    causal = jnp.arange(length)[:, None] >= jnp.arange(length)[None, :]
    spread = prefix_decay[:, :, None, :] - prefix_decay[:, None, :, :]
    spread = jnp.where(causal[None, :, :, None], spread, -1e30)
    scores = jnp.einsum(
        "hik,hjk,hijk->hij", query_rows, key_matrix, jnp.exp(spread), precision=maximum_precision
    )
    inside = jnp.einsum("hij,hjv->hiv", scores, value_matrix, precision=maximum_precision)
    incoming_state = jnp.einsum(
        "rqo,rol->rql",
        query_rows * jnp.exp(prefix_decay),
        running_state,
        precision=maximum_precision,
    )
    fresh_contributions = jnp.einsum(
        "rig,ril->rgl",
        key_matrix * jnp.exp(final_decay[:, None, :] - prefix_decay),
        value_matrix,
        precision=maximum_precision,
    )
    running_state = running_state * jnp.exp(final_decay)[:, :, None] + fresh_contributions
    return (running_state, inside + incoming_state)


def gla_mixer(
    big_unit, query_rows, key_matrix, value_matrix, gate_rows, decay_pre, head_gain, conv_taps
):
    row_total, channels = query_rows.shape
    head_count = channels // HDIM
    blocks = row_total // BLOCK_LEN

    def to_blocks(values):
        return values.reshape(blocks, BLOCK_LEN, head_count, HDIM).transpose(0, 2, 1, 3)

    per_unit = blocks // big_unit.shape[0]
    period = SIDE * SIDE // BLOCK_LEN
    block_ids = jnp.arange(blocks)
    position = block_ids % per_unit
    starts = jnp.where(big_unit[block_ids // per_unit], position == 0, position % period == 0)
    log_decay = jax.nn.log_sigmoid(decay_pre) / gate_norm
    scaled = query_rows * HDIM ** (-0.5)
    initial = jnp.zeros((head_count, HDIM, HDIM), jnp.float32)
    _, outputs = lax.scan(
        jax.checkpoint(block_step),
        initial,
        (
            to_blocks(scaled),
            to_blocks(key_matrix),
            to_blocks(value_matrix),
            to_blocks(log_decay),
            starts,
        ),
    )
    outputs = outputs.transpose(0, 2, 1, 3).reshape(row_total, head_count, HDIM)
    local_term = depthwise(big_unit, value_matrix, conv_taps)
    combined = outputs + local_term.reshape(row_total, head_count, HDIM)
    normed = (
        combined
        * lax.rsqrt(jnp.mean(combined * combined, axis=-1, keepdims=True) + head_eps)
        * head_gain
    )
    return normed.reshape(row_total, channels) * jax.nn.silu(gate_rows)


def modulate(row_slots, shift, scale):
    center = row_slots - jnp.mean(row_slots, axis=-1, keepdims=True)
    normed = center * lax.rsqrt(jnp.mean(center * center, axis=-1, keepdims=True) + norm_eps)
    return normed * (1.0 + scale[:, None, :]) + shift[:, None, :]


def effective(big_unit, modulation):
    unit_count = big_unit.shape[0]
    grouped = modulation.reshape(unit_count, 4, modulation.shape[-1])
    leading = jnp.broadcast_to(grouped[:, :1], grouped.shape)
    return jnp.where(big_unit[:, None, None], leading, grouped).reshape(modulation.shape)


def contract(left, right, left_axis, right_axis):
    return lax.dot_general(
        left, right, (((left_axis,), (right_axis,)), ((), ())), preferred_element_type=jnp.float32
    )


def arrange(values, split_dim, divisions):
    dims_in = values.shape
    pieces = values.reshape(
        dims_in[:split_dim]
        + (divisions, dims_in[split_dim] // divisions)
        + dims_in[split_dim + 1 :]
    )
    reordered = jnp.moveaxis(pieces, split_dim, 0)
    return (reordered.reshape(-1, reordered.shape[-1]), reordered.shape)


def settle(received, reordered_dims):
    return jnp.sum(received.reshape(reordered_dims), axis=0)


def gather_rows(values):
    return lax.all_gather(values, "mp", axis=0, tiled=True)


def scatter_rows(values):
    return lax.psum_scatter(values, "mp", scatter_dimension=0, tiled=True)


def fetch_weights(proj_weight, out_weight, fc1_weight, fc2_weight):
    return (
        lax.all_gather(proj_weight, "dp", axis=1, tiled=True),
        lax.all_gather(out_weight, "dp", axis=1, tiled=True),
        lax.all_gather(fc1_weight, "dp", axis=0, tiled=True),
        lax.all_gather(fc2_weight, "dp", axis=1, tiled=True),
    )


def forward_pass(block_input, own_mod, weights, local_params, big_unit):
    proj_full, out_full, fc1_full, fc2_full = weights
    decay_down, up_local, bias_local, head_gain, taps_local = local_params
    own_rows, model_width = block_input.shape
    slot_rows = SIDE * SIDE
    own_slots = own_rows // slot_rows
    pieces = [
        own_mod[:, part_index * model_width : (part_index + 1) * model_width]
        for part_index in range(6)
    ]
    residual = block_input.astype(jnp.float32).reshape(own_slots, slot_rows, model_width)
    hidden, norm_back_one = jax.vjp(modulate, residual, pieces[0], pieces[1])
    hidden_all = gather_rows(hidden.reshape(own_rows, model_width).astype(jnp.bfloat16))
    projected = jnp.einsum("rd,gde->gre", hidden_all, proj_full, preferred_element_type=jnp.float32)
    latent = jnp.dot(hidden_all, decay_down, preferred_element_type=jnp.float32)
    decay_pre = jnp.dot(
        latent,
        up_local.astype(jnp.float32),
        precision=maximum_precision,
        preferred_element_type=jnp.float32,
    ) + bias_local.astype(jnp.float32)
    mixed, mixer_back = jax.vjp(
        partial(gla_mixer, big_unit),
        projected[0],
        projected[1],
        projected[2],
        projected[3],
        decay_pre,
        head_gain.astype(jnp.float32),
        taps_local.astype(jnp.float32),
    )
    mixed_low = mixed.astype(jnp.bfloat16)
    attention = scatter_rows(
        jnp.dot(mixed_low, out_full, preferred_element_type=jnp.float32)
    ).reshape(own_slots, slot_rows, model_width)
    after_attn = residual + pieces[2][:, None, :] * attention
    hidden_two, norm_back_two = jax.vjp(modulate, after_attn, pieces[3], pieces[4])
    hidden_two_all = gather_rows(hidden_two.reshape(own_rows, model_width).astype(jnp.bfloat16))
    up_proj = jnp.dot(hidden_two_all, fc1_full, preferred_element_type=jnp.float32)
    active, gelu_back = jax.vjp(partial(jax.nn.gelu, approximate=True), up_proj)
    active_low = active.astype(jnp.bfloat16)
    feed_out = scatter_rows(
        jnp.dot(active_low, fc2_full, preferred_element_type=jnp.float32)
    ).reshape(own_slots, slot_rows, model_width)
    result = after_attn + pieces[5][:, None, :] * feed_out
    return (
        result,
        pieces,
        hidden_all,
        latent,
        mixed_low,
        attention,
        hidden_two_all,
        active_low,
        feed_out,
        norm_back_one,
        norm_back_two,
        mixer_back,
        gelu_back,
    )


def on_device(
    block_input,
    out_grad,
    time_table,
    class_table,
    time_ids,
    class_ids,
    image_patches,
    ada_weight,
    ada_bias,
    proj_weight,
    decay_down,
    decay_up,
    decay_bias,
    head_gain,
    conv_taps,
    out_weight,
    fc1_weight,
    fc2_weight,
):
    own_rows, model_width = block_input.shape
    local_width = proj_weight.shape[2]
    mp_rank = lax.axis_index("mp")
    dp_count = lax.axis_size("dp")
    slot_rows = SIDE * SIDE
    own_slots = own_rows // slot_rows
    slot_count = 4 * image_patches.shape[0]
    big_unit = image_patches == 4 * SIDE * SIDE
    condition = time_table[time_ids].astype(jnp.float32) + class_table[class_ids].astype(
        jnp.float32
    )
    silu_cond, silu_back = jax.vjp(jax.nn.silu, condition)
    silu_all = lax.all_gather(silu_cond.astype(jnp.bfloat16), "dp", axis=0, tiled=True)
    mod_columns = jnp.dot(
        silu_all, ada_weight, preferred_element_type=jnp.float32
    ) + ada_bias.astype(jnp.float32)
    modulation_all = lax.all_to_all(mod_columns, "dp", split_axis=0, concat_axis=1, tiled=True)
    modulation, effective_back = jax.vjp(partial(effective, big_unit), modulation_all)
    own_mod = lax.dynamic_slice_in_dim(modulation, mp_rank * own_slots, own_slots, 0)
    column_start = mp_rank * local_width
    up_local = lax.dynamic_slice_in_dim(decay_up, column_start, local_width, 1)
    local_params = (
        decay_down,
        up_local,
        lax.dynamic_slice_in_dim(decay_bias, column_start, local_width, 0),
        head_gain,
        lax.dynamic_slice_in_dim(conv_taps, column_start, local_width, 1),
    )
    weights = fetch_weights(proj_weight, out_weight, fc1_weight, fc2_weight)
    first_pass = forward_pass(block_input, own_mod, weights, local_params, big_unit)
    weights_again = fetch_weights(proj_weight, out_weight, fc1_weight, fc2_weight)
    kept_values = forward_pass(block_input, own_mod, weights_again, local_params, big_unit)
    block_out = first_pass[0].reshape(own_rows, model_width).astype(jnp.bfloat16)
    proj_full, out_full, fc1_full, fc2_full = weights_again
    (
        result_again,
        pieces,
        hidden_all,
        latent,
        mixed_low,
        attention,
        hidden_two_all,
        active_low,
        feed_out,
        norm_back_one,
        norm_back_two,
        mixer_back,
        gelu_back,
    ) = kept_values
    grad_rows = out_grad.astype(jnp.float32).reshape(own_slots, slot_rows, model_width)
    grad_gate_two = jnp.sum(grad_rows * feed_out, axis=1)
    grad_feed = (
        (grad_rows * pieces[5][:, None, :]).astype(jnp.bfloat16).reshape(own_rows, model_width)
    )
    grad_feed_all = gather_rows(grad_feed)
    grad_active = contract(grad_feed_all, fc2_full, 1, 1)
    grad_fc2 = contract(active_low, grad_feed_all, 0, 0)
    grad_up = gelu_back(grad_active)[0].astype(jnp.bfloat16)
    grad_fc1 = contract(hidden_two_all, grad_up, 0, 0)
    grad_hidden_two = scatter_rows(contract(grad_up, fc1_full, 1, 1))
    grad_after, grad_shift_two, grad_scale_two = norm_back_two(
        grad_hidden_two.reshape(own_slots, slot_rows, model_width)
    )
    grad_after = grad_after + grad_rows
    grad_gate_one = jnp.sum(grad_after * attention, axis=1)
    grad_attn = (
        (grad_after * pieces[2][:, None, :]).astype(jnp.bfloat16).reshape(own_rows, model_width)
    )
    grad_attn_all = gather_rows(grad_attn)
    grad_mixed = contract(grad_attn_all, out_full, 1, 1)
    grad_out_weight = contract(mixed_low, grad_attn_all, 0, 0)
    grad_query, grad_key, grad_value, grad_gate, grad_pre, grad_gain, grad_taps = mixer_back(
        grad_mixed
    )
    grad_proj_out = jnp.stack([grad_query, grad_key, grad_value, grad_gate]).astype(jnp.bfloat16)
    grad_proj = jnp.einsum(
        "rd,gre->gde", hidden_all, grad_proj_out, preferred_element_type=jnp.float32
    )
    grad_latent = jnp.dot(
        grad_pre,
        up_local.astype(jnp.float32).T,
        precision=maximum_precision,
        preferred_element_type=jnp.float32,
    )
    grad_up_local = jnp.dot(
        latent.T, grad_pre, precision=maximum_precision, preferred_element_type=jnp.float32
    )
    grad_bias_local = jnp.sum(grad_pre, axis=0)
    grad_down = jnp.dot(
        hidden_all.T, grad_latent, precision=maximum_precision, preferred_element_type=jnp.float32
    )
    grad_hidden_part = jnp.einsum(
        "gre,gde->rd", grad_proj_out, proj_full, preferred_element_type=jnp.float32
    ) + jnp.dot(
        grad_latent, decay_down.T, precision=maximum_precision, preferred_element_type=jnp.float32
    )
    grad_hidden = scatter_rows(grad_hidden_part)
    grad_residual, grad_shift_one, grad_scale_one = norm_back_one(
        grad_hidden.reshape(own_slots, slot_rows, model_width)
    )
    input_grad = (grad_residual + grad_after).reshape(own_rows, model_width)
    grad_up_full = lax.dynamic_update_slice_in_dim(
        jnp.zeros(decay_up.shape, jnp.float32), grad_up_local, column_start, 1
    )
    grad_bias_full = lax.dynamic_update_slice_in_dim(
        jnp.zeros(decay_bias.shape, jnp.float32), grad_bias_local, column_start, 0
    )
    grad_taps_full = lax.dynamic_update_slice_in_dim(
        jnp.zeros(conv_taps.shape, jnp.float32), grad_taps, column_start, 1
    )
    down_sum, up_sum, bias_sum, gain_sum, taps_sum = lax.psum(
        (grad_down, grad_up_full, grad_bias_full, grad_gain, grad_taps_full), ("dp", "mp")
    )
    flat_proj, dims_proj = arrange(grad_proj, 1, dp_count)
    flat_out, dims_out = arrange(grad_out_weight, 1, dp_count)
    flat_fc1, dims_fc1 = arrange(grad_fc1, 0, dp_count)
    flat_fc2, dims_fc2 = arrange(grad_fc2, 1, dp_count)
    got_proj, got_out, got_fc1, got_fc2 = (
        lax.all_to_all(
            flat_proj.astype(jnp.bfloat16), "dp", split_axis=0, concat_axis=0, tiled=True
        ).astype(flat_proj.dtype),
        lax.all_to_all(
            flat_out.astype(jnp.bfloat16), "dp", split_axis=0, concat_axis=0, tiled=True
        ).astype(flat_out.dtype),
        lax.all_to_all(
            flat_fc1.astype(jnp.bfloat16), "dp", split_axis=0, concat_axis=0, tiled=True
        ).astype(flat_fc1.dtype),
        lax.all_to_all(
            flat_fc2.astype(jnp.bfloat16), "dp", split_axis=0, concat_axis=0, tiled=True
        ).astype(flat_fc2.dtype),
    )
    proj_grad = settle(got_proj, dims_proj)
    out_weight_grad = settle(got_out, dims_out)
    fc1_grad = settle(got_fc1, dims_fc1)
    fc2_grad = settle(got_fc2, dims_fc2)
    grad_mod = jnp.concatenate(
        [
            grad_shift_one,
            grad_scale_one,
            grad_gate_one,
            grad_shift_two,
            grad_scale_two,
            grad_gate_two,
        ],
        axis=1,
    )
    placed = lax.dynamic_update_slice_in_dim(
        jnp.zeros((slot_count, 6 * model_width), jnp.float32), grad_mod, mp_rank * own_slots, 0
    )
    folded = effective_back(placed)[0]
    summed_mod = lax.psum(folded.astype(jnp.bfloat16), "mp").astype(jnp.float32)
    mod_grad_all = lax.all_to_all(
        summed_mod.astype(jnp.bfloat16), "dp", split_axis=1, concat_axis=0, tiled=True
    ).astype(summed_mod.dtype)
    ada_bias_grad = jnp.sum(mod_grad_all, axis=0)
    ada_weight_grad = jnp.dot(
        silu_all.T, mod_grad_all, precision=maximum_precision, preferred_element_type=jnp.float32
    )
    grad_silu = lax.psum_scatter(
        jnp.dot(
            mod_grad_all,
            ada_weight.T,
            precision=maximum_precision,
            preferred_element_type=jnp.float32,
        ),
        "dp",
        scatter_dimension=0,
        tiled=True,
    )
    cond_grad = silu_back(grad_silu)[0]
    return (
        block_out,
        input_grad,
        cond_grad,
        ada_weight_grad,
        ada_bias_grad,
        proj_grad,
        down_sum,
        up_sum,
        bias_sum,
        gain_sum,
        taps_sum,
        out_weight_grad,
        fc1_grad,
        fc2_grad,
    )


def solution(mesh):
    return jax.shard_map(
        on_device,
        mesh=mesh,
        in_specs=(
            P(("dp", "mp"), None),
            P(("dp", "mp"), None),
            P(),
            P(),
            P("dp"),
            P("dp"),
            P("dp"),
            P(None, "dp"),
            P("dp"),
            P(None, "dp", "mp"),
            P(),
            P(),
            P(),
            P(),
            P(),
            P("mp", "dp"),
            P("dp", "mp"),
            P("mp", "dp"),
        ),
        out_specs=(
            P(("dp", "mp"), None),
            P(("dp", "mp"), None),
            P("dp", None),
            P(None, "dp"),
            P("dp"),
            P(None, "dp", "mp"),
            P(),
            P(),
            P(),
            P(),
            P(),
            P("mp", "dp"),
            P("dp", "mp"),
            P("mp", "dp"),
        ),
        check_vma=False,
    )
```

profile of v0, /device:TPU:1, one launch (start us, length us, event | category | flops | bytes accessed | tf_op | source)
XLA Modules:
  0.0 3038.2 jit_solution(18284514030943257621)
XLA Ops:
  12.1 23.4 all-gather
  61.3 24.8 all-gather.11.cloned.1.call-done
  101.0 47.2 %all-gather.13.cloned.1.call-done = bf16[4,1152,576]{2,1,0:T(8,128)(2,1)} async-done(((bf16[4,72,576]{2,1,0:T(8,128)(2,1)}), bf16[4,1152,576]{2,1,0:T(8,128)(2,1)}) %all-gather.13.cloned.1.call-update) | async-done | bytes 5308432 | tf_op jit(solution)/shard_map/all_gather | solution.py:174
  195.6 495.8 %while.54 = (s32[]{:T(128)}, f32[8,72,72]{2,1,0:T(8,128)}, f32[16,8,64,72]{3,2,1,0:T(8,128)}, f32[16,8,72,72]{3,2,1,0:T(8,128)}, pred[16]{0:T(512)(128)(4,1)}, /...) while((s32[]{:T(128)}, f32[8,72,72]{2,1,0:T(8,128)}, ...), condition=%wide.region_12.13_spmd.clone, body=%wide.region_10.12_spmd.clone.sunk | while | flops 106536448 | bytes 24941224 | solution.py:108
  204.4 14.1 fusion.354
  234.5 14.1 fusion.354
  265.5 14.1 fusion.354
  296.6 14.1 fusion.354
  358.8 14.1 fusion.354
  389.9 14.1 fusion.354
  421.0 14.1 fusion.354
  452.1 14.1 fusion.354
  483.2 14.1 fusion.354
  514.3 14.1 fusion.354
  545.4 14.1 fusion.354
  576.5 14.1 fusion.354
  607.6 14.1 fusion.354
  638.7 14.1 fusion.354
  669.8 14.1 fusion.354
  764.8 54.5 %reduce-scatter.11.cloned.1.call-done = f32[512,1152]{1,0:T(8,128)} async-done(((f32[1024,1152]{1,0:T(8,128)}), f32[512,1152]{1,0:T(8,128)}) %reduce-scatter.11.cloned.1.call-update) | async-done | bytes 2359312 | tf_op jit(solution)/shard_map/reduce_scatter | solution.py:169
  824.1 33.4 %all-gather.23.cloned.1.call-done = bf16[1024,1152]{1,0:T(8,128)(2,1)} async-done(((bf16[512,1152]{1,0:T(8,128)(2,1)}), bf16[1024,1152]{1,0:T(8,128)(2,1)}) %all-gather.23.cloned.1.call-update) | async-done | bytes 2359312 | tf_op jit(solution)/shard_map/all_gather | solution.py:165
  857.5 59.1 %all-gather.21.cloned.1.call-done = bf16[2304,1152]{0,1:T(8,128)(2,1)} async-done(((bf16[2304,72]{0,1:T(8,128)(2,1)}), bf16[2304,1152]{0,1:T(8,128)(2,1)}) %all-gather.21.cloned.1.call-update) | async-done | bytes 5308432 | tf_op jit(solution)/shard_map/all_gather | solution.py:177
  928.2 45.7 %all-gather.19.cloned.1.call-done = bf16[1152,2304]{1,0:T(8,128)(2,1)} async-done(((bf16[72,2304]{1,0:T(8,128)(2,1)}), bf16[1152,2304]{1,0:T(8,128)(2,1)}) %all-gather.19.cloned.1.call-update) | async-done | bytes 5308432 | tf_op jit(solution)/shard_map/all_gather | solution.py:176
  973.9 36.4 %all-gather.25.cloned.1.call-done = bf16[1024,1152]{1,0:T(8,128)(2,1)} async-done(((bf16[512,1152]{1,0:T(8,128)(2,1)}), bf16[1024,1152]{1,0:T(8,128)(2,1)}) %all-gather.25.cloned.1.call-update) | async-done | bytes 2359312 | tf_op jit(solution)/shard_map/all_gather | solution.py:165
  1010.3 16.8 fusion.77
  1039.8 57.7 %reduce-scatter.13.cloned.1.call-done = f32[512,1152]{1,0:T(8,128)} async-done(((f32[1024,1152]{1,0:T(8,128)}), f32[512,1152]{1,0:T(8,128)}) %reduce-scatter.13.cloned.1.call-update) | async-done | bytes 2359312 | tf_op jit(solution)/shard_map/reduce_scatter | solution.py:169
  1106.5 436.2 %while.53 = (s32[]{:T(128)}, f32[8,72,72]{2,1,0:T(8,128)S(1)}, f32[16,8,64,72]{3,1,2,0:T(8,128)}, pred[16]{0:T(512)(128)(4,1)S(1)}, f32[16,8,64,72]{3,1,2,0:T(8,...) while((s32[]{:T(128)}, f32[8,72,72]{2,1,0:T(8,128)S(1)}, ...), condition=%wide.region_4.5_spmd.clone, body=%wide.region_2.4_spmd.clone.sunk | while | flops 106494976 | bytes 24387744 | solution.py:108
  1114.1 14.1 fusion.343
  1141.3 14.1 fusion.343
  1168.6 14.1 fusion.343
  1223.1 14.1 fusion.343
  1250.3 14.1 fusion.343
  1277.5 14.1 fusion.343
  1304.8 14.1 fusion.343
  1332.0 14.1 fusion.343
  1359.2 14.1 fusion.343
  1386.4 14.1 fusion.343
  1604.3 765.2 %while.55 = (s32[]{:T(128)}, f32[8,72,72]{2,1,0:T(8,128)S(1)}, f32[16,8,64,72]{3,2,1,0:T(8,128)}, bf16[16,8,64,72]{3,2,1,0:T(8,128)(2,1)}, f32[16,8,64,72]{3,2,1...) while((s32[]{:T(128)}, f32[8,72,72]{2,1,0:T(8,128)S(1)}, ...), condition=%wide.region_28.29_spmd.clone, body=%wide.region_21.28_spmd.clone.sunk | while | flops 236896256 | bytes 12708060 | solution.py:108
  1633.8 14.5 fusion.377
  1681.7 14.5 fusion.377
  1729.5 14.5 fusion.377
  1777.3 14.5 fusion.377
  1825.1 14.5 fusion.377
  1872.9 14.5 fusion.377
  1920.7 14.5 fusion.377
  1968.6 14.5 fusion.377
  2016.4 14.5 fusion.377
  2064.2 14.5 fusion.377
  2112.0 14.5 fusion.377
  2159.8 14.5 fusion.377
  2207.6 14.5 fusion.377
  2255.4 14.5 fusion.377
  2303.2 14.5 fusion.377
  2351.0 14.5 fusion.377
  2411.4 15.1 multiply_bitcast_fusion.15
  2443.4 14.4 fusion.156
  2500.3 32.1 %reduce-scatter.15.cloned.1.call-done = f32[512,1152]{1,0:T(8,128)} async-done(((f32[1024,1152]{1,0:T(8,128)}), f32[512,1152]{1,0:T(8,128)}) %reduce-scatter.15.cloned.1.call-update) | async-done | bytes 2359312 | tf_op jit(solution)/shard_map/reduce_scatter | solution.py:169
  2551.3 35.5 %all-to-all-done.4 = bf16[16,72,2304]{2,1,0:T(8,128)(2,1)} async-done(((bf16[16,72,2304]{2,1,0:T(8,128)(2,1)}), bf16[16,72,2304]{2,1,0:T(8,128)(2,1)}, u32[]{:S(2)}, u32[]{:S(2)}) %all-to-all-start.4) | async-done | bytes 5308448 | tf_op jit(solution)/shard_map/all_to_all | solution.py:387
  2586.8 23.8 all-to-all-start.1
  2667.7 59.4 %all-to-all-done.5 = bf16[16,2304,72]{1,2,0:T(8,128)(2,1)} async-done(((bf16[16,2304,72]{1,2,0:T(8,128)(2,1)}), bf16[16,2304,72]{1,2,0:T(8,128)(2,1)}, u32[]{:S(2)}, u32[]{:S(2)}) %all-to-all-start.5) | async-done | bytes 5308448 | tf_op jit(solution)/shard_map/all_to_all | solution.py:390
  2727.2 24.2 all-to-all-start.3
  2751.6 19.5 fusion.86
  2867.5 85.4 %all-reduce.35 = (f32[1152]{0:T(1024)}, f32[72]{0:T(128)}, f32[9,1152]{1,0:T(8,128)}) all-reduce(f32[1152]{0:T(1024)S(1)} %negate_dynamic-update-slice_fusion, f32[72]{0:T(128)} %reduce_sum.527, f32[9,1152]{1,0:T(8,128)} %dynamic_update_slice.69), channel_id=1, replica_groups=mesh['dp'=16,'mp'=2] {'dp','mp'}, use_global_device_ids=true, to_apply=%region_47.48 | all-reduce | flops 11592 | bytes 92736 | tf_op jit(solution)/shard_map/psum | solution.py:373
  2969.4 58.8 %all-reduce.42.cloned.1.call-done = (f32[1152,16]{0,1:T(8,128)}, f32[16,1152]{1,0:T(8,128)}) async-done(((f32[1152,16]{0,1:T(8,128)}, f32[16,1152]{1,0:T(8,128)}), (f32[1152,16]{0,1:T(8,128)}, f32[16,1152]{1,0:T(8,128)})) %all-reduce.42.cloned.1.call-update) | async-done | bytes 147472 | tf_op jit(solution)/shard_map/psum | solution.py:373
  (1375 shorter events, 1663.5 us)
Async XLA Ops:
  7.2 34.9 %copy-start.4 = (bf16[512,1152]{1,0:T(8,128)(2,1)S(1)}, bf16[512,1152]{1,0:T(8,128)(2,1)}, u32[]{:S(2)}) copy-start(bf16[512,1152]{1,0:T(8,128)(2,1)} %param.24) | copy-start | bytes 3538948
  11.5 31.3 %copy-start.90 = (bf16[4,1152]{1,0:T(4,128)(2,1)}, bf16[4,1152]{1,0:T(4,128)(2,1)S(1)}, u32[]{:S(2)}) copy-start(bf16[4,1152]{1,0:T(4,128)(2,1)S(1)} %gather_fusion) | copy-start | bytes 27652
  12.1 36.3 %copy-start.92 = (bf16[4,1152]{1,0:T(4,128)(2,1)}, bf16[4,1152]{1,0:T(4,128)(2,1)S(1)}, u32[]{:S(2)}) copy-start(bf16[4,1152]{1,0:T(4,128)(2,1)S(1)} %gather_fusion.1) | copy-start | bytes 27652
  35.5 13.2 copy-start.22
  37.9 10.4 all-to-all-start
  41.4 44.7 %all-gather.11.cloned.1.call-start = ((), (), s32[]{:S(2)}) async-start(), calls=%async_computation.12 | async-start | bytes 3538944 | tf_op jit(solution)/shard_map/all_gather | solution.py:165
  48.4 10.8 copy-start.114
  48.4 11.5 copy-start.113
  48.4 12.1 copy-start.111
  48.4 37.7 %copy-start.83 = (bf16[1152,16]{0,1:T(8,128)(2,1)S(1)}, bf16[1152,16]{0,1:T(8,128)(2,1)}, u32[]{:S(2)}) copy-start(bf16[1152,16]{0,1:T(8,128)(2,1)} %param.34) | copy-start | bytes 110596
  51.7 96.6 %all-gather.13.cloned.1.call-start = ((), (), s32[]{:S(2)}) async-start(), calls=%async_computation.13 | async-start | bytes 6266880 | tf_op jit(solution)/shard_map/all_gather | solution.py:174
  52.4 700.9 %all-gather.15.cloned.1.call-start = ((), (), s32[]{:S(2)}) async-start(), calls=%async_computation.14 | async-start | bytes 1566720 | tf_op jit(solution)/shard_map/all_gather | solution.py:175
  53.2 766.1 %reduce-scatter.11.cloned.1.call-start = ((), (), s32[]{:S(2)}) async-start(), calls=%async_computation.21 | async-start | bytes 7077888 | tf_op jit(solution)/shard_map/reduce_scatter | solution.py:169
  59.2 681.0 %copy-start.37 = (f32[1024]{0:T(1024)}, f32[1024]{0:T(1024)S(1)}, u32[]{:S(2)}) copy-start(f32[1024]{0:T(1024)S(1)} %get-tuple-element.947) | copy-start | bytes 12292
  61.3 678.9 %copy-start.39 = (f32[576]{0:T(1024)}, f32[576]{0:T(1024)S(1)}, u32[]{:S(2)}) copy-start(f32[576]{0:T(1024)S(1)} %get-tuple-element.792) | copy-start | bytes 6916
  95.5 52.7 %copy-start.19 = (bf16[1024,1152]{1,0:T(8,128)(2,1)S(1)}, bf16[1024,1152]{1,0:T(8,128)(2,1)}, u32[]{:S(2)}) copy-start(bf16[1024,1152]{1,0:T(8,128)(2,1)} %all-gather.11.cloned.1.call-done) | copy-start | bytes 7077892
  162.6 577.6 %copy-start.2 = (f32[1,1024,576]{1,2,0:T(8,128)}, f32[1,1024,576]{1,2,0:T(8,128)S(1)}, u32[]{:S(2)}) copy-start(f32[1,1024,576]{1,2,0:T(8,128)S(1)} %get-tuple-element.897) | copy-start | bytes 7077892
  760.9 96.5 %all-gather.23.cloned.1.call-start = ((), (), s32[]{:S(2)}) async-start(), calls=%async_computation.20 | async-start | bytes 3538944 | tf_op jit(solution)/shard_map/all_gather | solution.py:165
  763.4 153.1 %all-gather.21.cloned.1.call-start = ((), (), s32[]{:S(2)}) async-start(), calls=%async_computation.18 | async-start | bytes 5640192 | tf_op jit(solution)/shard_map/all_gather | solution.py:177
  764.0 209.9 %all-gather.19.cloned.1.call-start = ((), (), s32[]{:S(2)}) async-start(), calls=%async_computation.17 | async-start | bytes 5640192 | tf_op jit(solution)/shard_map/all_gather | solution.py:176
  764.8 245.6 %all-gather.25.cloned.1.call-start = ((), (), s32[]{:S(2)}) async-start(), calls=%async_computation.22 | async-start | bytes 3538944 | tf_op jit(solution)/shard_map/all_gather | solution.py:165
  821.4 279.0 %copy-start.96 = (f32[512]{0:T(512)}, f32[512]{0:T(512)S(1)}, u32[]{:S(2)}) copy-start(f32[512]{0:T(512)S(1)} %broadcast_multiply_fusion) | copy-start | bytes 6148
  824.1 273.5 %reduce-scatter.13.cloned.1.call-start = ((), (), s32[]{:S(2)}) async-start(), calls=%async_computation.23 | async-start | bytes 7077888 | tf_op jit(solution)/shard_map/reduce_scatter | solution.py:169
  1010.3 19.1 copy-start.116
  1037.3 524.7 %all-gather.27.cloned.1.call-start = ((), (), s32[]{:S(2)}) async-start(), calls=%async_computation.24 | async-start | bytes 3538944 | tf_op jit(solution)/shard_map/all_gather | solution.py:165
  1038.0 550.3 %copy-start.112 = (f32[72]{0:T(128)}, f32[72]{0:T(128)S(1)}, u32[]{:S(2)}) copy-start(f32[72]{0:T(128)S(1)} %convert_element_type.392) | copy-start | bytes 868
  1104.0 1396.3 %reduce-scatter.17.cloned.1.call-start = ((), (), s32[]{:S(2)}) async-start(), calls=%async_computation.26 | async-start | bytes 7077888 | tf_op jit(solution)/shard_map/reduce_scatter | solution.py:169
  1561.8 970.6 %reduce-scatter.15.cloned.1.call-start = ((), (), s32[]{:S(2)}) async-start(), calls=%async_computation.25 | async-start | bytes 7077888 | tf_op jit(solution)/shard_map/reduce_scatter | solution.py:169
  2411.3 15.2 copy-start.32
  2411.3 15.2 copy-start.21
  2411.3 15.2 copy-start.108
  2432.0 36.0 %copy-start.28 = (f32[1024,16]{0,1:T(8,128)}, f32[1024,16]{0,1:T(8,128)S(1)}, u32[]{:S(2)}) copy-start(f32[1024,16]{0,1:T(8,128)S(1)} %fusion.159) | copy-start | bytes 196612
  2433.2 10.1 copy-start.18
  2433.3 10.1 copy-start.45
  2433.3 10.1 copy-start.47
  2443.4 14.5 copy-start.24
  2443.4 14.5 copy-start.25
  2443.4 14.5 copy-start.119
  2457.8 10.2 copy-start.23
  2457.9 10.2 copy-start.84
  2482.9 103.9 %all-to-all-start.4 = ((bf16[16,72,2304]{2,1,0:T(8,128)(2,1)}), bf16[16,72,2304]{2,1,0:T(8,128)(2,1)}, u32[]{:S(2)}, u32[]{:S(2)}) async-start(bf16[16,72,2304]{2,1,0:T(8,128)(2,1)} %bitcast.595), calls=%async_computation.10 | async-start | bytes 10616832 | tf_op jit(solution)/shard_map/all_to_all | solution.py:387
  2489.3 139.1 %reduce-scatter.7.cloned.1.call-start = ((), (), s32[]{:S(2)}) async-start(), calls=%async_computation.15 | async-start | bytes 7077888 | tf_op jit(solution)/shard_map/reduce_scatter | solution.py:169
  2500.2 32.2 %copy-start.5 = (bf16[512,1152]{1,0:T(8,128)(2,1)S(1)}, bf16[512,1152]{1,0:T(8,128)(2,1)}, u32[]{:S(2)}) copy-start(bf16[512,1152]{1,0:T(8,128)(2,1)} %param.24) | copy-start | bytes 3538948
  2500.2 32.2 %copy-start.27 = (f32[2,1152]{1,0:T(2,128)S(1)}, f32[2,1152]{1,0:T(2,128)}, u32[]{:S(2)}) copy-start(f32[2,1152]{1,0:T(2,128)} %get-tuple-element.935) | copy-start | bytes 27652
  2586.8 35.2 %all-to-all-start.1 = ((bf16[4,16,432]{2,0,1:T(4,128)(2,1)}), bf16[4,16,432]{2,0,1:T(4,128)(2,1)}, u32[]{:S(2)}, u32[]{:S(2)}) async-start(bf16[4,16,432]{2,0,1:T(4,128)(2,1)} %psum.42), calls=%async_computation.7 | async-start | bytes 131072 | tf_op jit(solution)/shard_map/all_to_all | solution.py:414
  2622.0 105.2 %all-to-all-start.5 = ((bf16[16,2304,72]{1,2,0:T(8,128)(2,1)}), bf16[16,2304,72]{1,2,0:T(8,128)(2,1)}, u32[]{:S(2)}, u32[]{:S(2)}) async-start(bf16[16,2304,72]{1,2,0:T(8,128)(2,1)} %bitcast.596), calls=%async_computation.11 | async-start | bytes 10616832 | tf_op jit(solution)/shard_map/all_to_all | solution.py:390
  2628.0 123.6 %all-gather.17.cloned.1.call-start = ((), (), s32[]{:S(2)}) async-start(), calls=%async_computation.16 | async-start | bytes 3538944 | tf_op jit(solution)/shard_map/all_gather | solution.py:165
  2638.2 321.2 %all-reduce.40.cloned.1.call-start = ((), (), s32[]{:S(2)}) async-start(), calls=%async_computation.27 | async-start | bytes 589824
  2727.2 69.0 %all-to-all-start.3 = ((bf16[16,576,72]{1,2,0:T(8,128)(2,1)}), bf16[16,576,72]{1,2,0:T(8,128)(2,1)}, u32[]{:S(2)}, u32[]{:S(2)}) async-start(bf16[16,576,72]{1,2,0:T(8,128)(2,1)} %fusion.162), calls=%async_computation.9 | async-start | bytes 2949120 | tf_op jit(solution)/shard_map/all_to_all | solution.py:384
  2751.4 214.2 %reduce-scatter.9.cloned.1.call-start = ((), (), s32[]{:S(2)}) async-start(), calls=%async_computation.19 | async-start | bytes 7077888 | tf_op jit(solution)/shard_map/reduce_scatter | solution.py:169
  2796.1 164.6 %all-to-all-start.2 = ((bf16[16,288,576]{2,1,0:T(8,128)(2,1)}), bf16[16,288,576]{2,1,0:T(8,128)(2,1)}, u32[]{:S(2)}, u32[]{:S(2)}) async-start(bf16[16,288,576]{2,1,0:T(8,128)(2,1)} %bitcast.587), calls=%async_computation.8 | async-start | bytes 11796480 | tf_op jit(solution)/shard_map/all_to_all | solution.py:381
  2802.1 226.0 %all-reduce.42.cloned.1.call-start = ((), (), s32[]{:S(2)}) async-start(), calls=%async_computation.28 | async-start | bytes 294912 | tf_op jit(solution)/shard_map/psum | solution.py:373
  2822.3 14.0 copy-start.62
  2822.3 14.0 copy-start.64
  2822.3 14.0 copy-start.66
  2822.3 14.0 copy-start.68
  2822.3 14.0 copy-start.70
  2822.3 14.0 copy-start.72
  2822.3 14.0 copy-start.74
  2843.0 11.1 copy-start.109
  2849.4 15.4 copy-start.20
  2867.3 92.0 %copy-start.91 = (bf16[4,1152]{1,0:T(4,128)(2,1)S(1)}, bf16[4,1152]{1,0:T(4,128)(2,1)}, u32[]{:S(2)}) copy-start(bf16[4,1152]{1,0:T(4,128)(2,1)} %copy-done.90) | copy-start | bytes 27652
  2867.4 92.0 %copy-start.93 = (bf16[4,1152]{1,0:T(4,128)(2,1)S(1)}, bf16[4,1152]{1,0:T(4,128)(2,1)}, u32[]{:S(2)}) copy-start(bf16[4,1152]{1,0:T(4,128)(2,1)} %copy-done.92) | copy-start | bytes 27652
  2960.8 70.4 %copy-start.1 = (bf16[1001,1152]{1,0:T(8,128)(2,1)S(1)}, bf16[1001,1152]{1,0:T(8,128)(2,1)}, u32[]{:S(2)}) copy-start(bf16[1001,1152]{1,0:T(8,128)(2,1)} %param.27) | copy-start | bytes 6918916
  (79 other events, 276.1 us)
Sparse Core Ops, SparseCore 0:
  51.8 34.2 all-gather.10
  88.3 59.9 all-gather.12
  150.4 37.9 all-gather.14
  761.1 58.2 reduce-scatter.10
  821.4 36.0 all-gather.22
  859.7 56.7 all-gather.20
  918.9 54.9 all-gather.18
  976.1 34.2 all-gather.24
  1037.5 59.9 reduce-scatter.12
  1104.1 36.0 all-gather.26
  1561.9 59.9 reduce-scatter.16
  2472.4 60.0 reduce-scatter.14
  2534.7 61.3 reduce-scatter.6
  2638.3 35.8 all-gather.16
  2678.4 128.0 all-reduce.39
  2808.8 89.6 reduce-scatter.8
  2904.5 123.5 all-reduce.41
where the time goes:
time: 3060 us; the launch traced here: 3040 us
  other arithmetic  1420 us (46%)
  waiting for transfers between devices  553 us (18%)
  matrix products  471 us (15%)
  local copies, waits for them, and re-layouts  380 us (12%)
  blocking collectives  118 us (4%)
  starting transfers between devices  71.2 us (2%)
    dot_general x64, other arithmetic, block_step(): jnp.einsum('hik,hjk,hijk->hij', query_rows, key_matrix, jnp.exp(spread),...  653 us
    reduce_sum x16, other arithmetic, block_step(): spread = prefix_decay[:, :, None, :] - prefix_decay[:, None, :, :]  232 us
    another operation x80, other arithmetic, block_step(): prefix_decay = jnp.cumsum(log_decay, axis=1)  154 us
    reduce_scatter x6, waiting for transfers between devices, scatter_rows(): return lax.psum_scatter(values, 'mp', scatter_dimension=0, tiled=True)  144 us
    dot_general x64, matrix products, block_step(): jnp.einsum('rig,ril->rgl', key_matrix * jnp.exp(final_decay[:, None, :] -...  116 us
    dot_general x64, matrix products, block_step(): jnp.einsum('rqo,rol->rql', query_rows * jnp.exp(prefix_decay), running_st...  103 us
    exp x32, other arithmetic, block_step(): jnp.exp(spread)  102 us
    all_gather x5, waiting for transfers between devices, gather_rows(): return lax.all_gather(values, 'mp', axis=0, tiled=True)  94.6 us
  transfers between devices with their start and end apart: 23, of which 13 were waited for; matrix products, arithmetic and copies ran while one was open for 73% of the time, Pallas kernels for 0%

commit v1 on v0

v1 whole, which is shorter than its diff:
```python
import functools
import math

import jax
import jax.numpy as jnp
from jax import lax
from jax.experimental import pallas as pl
from jax.experimental.pallas import tpu as pltpu
from jax.sharding import Mesh
from jax.sharding import PartitionSpec as P

f32=jnp.float32; bf16=jnp.bfloat16
HDIM=72; SIDE=16; LANES=128; CHUNK=128; MARGIN=64
LEVELS=(64,32,16,8,4,2,1)
GATE_NORM=16.0; head_eps=1e-5
LOG2E=math.log2(math.e)

def parts(x, n):
    out=[]
    for _ in range(n-1):
        p=x.astype(bf16); out.append(p); x=x-p.astype(f32)
    out.append(x.astype(bf16)); return out

def mm(a,b,ca,cb):
    return lax.dot_general(a,b,(((ca,),(cb,)),((),())),preferred_element_type=f32)

def mmx(a,b,ca,cb,n):
    if n==1: return mm(a.astype(bf16),b.astype(bf16),ca,cb)
    ah,al=parts(a,2); bh,bl=parts(b,2)
    return mm(ah,bh,ca,cb)+(mm(ah,bl,ca,cb)+mm(al,bh,ca,cb))

def sel_mm(m,x,n):
    ps=parts(x,n)
    r=mm(m,ps[-1],1,0)
    for p in ps[-2::-1]: r=mm(m,p,1,0)+r
    return r

def iota2(shape,d): return lax.broadcasted_iota(jnp.int32,shape,d)

def level_matrix():
    i=iota2((CHUNK,CHUNK),0); j=iota2((CHUNK,CHUNK),1)
    x=i^j
    lvl=jnp.zeros((CHUNK,CHUNK),jnp.int32)
    for b in LEVELS[::-1]: lvl=jnp.where(x>=b,b,lvl)
    return lvl,i,j

def level_ops(q,k,L,lw):
    row=iota2((CHUNK,LANES),0)
    out=[]
    for b in LEVELS:
        n=CHUNK//(2*b)
        if b>=8:
            L3=L.reshape(n,2*b,LANES); D=L3-L3[:,b-1:b,:]
            E=jnp.exp2(-jnp.abs(D)).reshape(CHUNK,LANES)
            q3=q.reshape(n,2*b,LANES); k3=k.reshape(n,2*b,LANES)
            X=jnp.concatenate([k3[:,:b],q3[:,b:]],axis=1).reshape(CHUNK,LANES)
        else:
            right=(row&b)!=0
            X=jnp.where(right,q,k)
            L3=L.reshape(CHUNK//8,8,LANES)
            if b==4:
                D=(L3-L3[:,3:4,:]).reshape(CHUNK,LANES); E=jnp.exp2(-jnp.abs(D))
            elif b==2:
                s=lax.broadcasted_iota(jnp.int32,L3.shape,1)
                R=jnp.where(s<4,L3[:,1:2,:],L3[:,5:6,:])
                E=jnp.exp2(-jnp.abs(L3-R)).reshape(CHUNK,LANES)
            else:
                E=jnp.exp2(jnp.where(right,lw,0.0))
        out.append((b,E,X*E))
    return out

def log_decay2(pre):
    return (jnp.minimum(pre,0.0)-jnp.log1p(jnp.exp(-jnp.abs(pre))))*(LOG2E/GATE_NORM)

def image_masks(base,rows,width,height):
    p=iota2((rows,LANES),0)+base
    col=p&(width-1)
    r=(p//width)&(height-1)
    return col,r

def conv_forward(vp,up,um,taps,store,total,width,height):
    tiles=total//CHUNK
    for t in range(tiles):
        o=MARGIN+t*CHUNK
        col,_=image_masks(0,CHUNK,width,height)
        c=vp[o:o+CHUNK,:]
        left=jnp.where(col!=0,vp[o-1:o-1+CHUNK,:],0.0)
        right=jnp.where(col!=width-1,vp[o+1:o+1+CHUNK,:],0.0)
        def comb(a): return left*taps[3*a:3*a+1,:]+c*taps[3*a+1:3*a+2,:]+right*taps[3*a+2:3*a+3,:]
        um[o:o+CHUNK,:]=comb(0)
        store(t,comb(1))
        up[o:o+CHUNK,:]=comb(2)

def conv_finish(up,um,add,total,width,height):
    for t in range(total//CHUNK):
        o=MARGIN+t*CHUNK
        _,r=image_masks(t*CHUNK,CHUNK,width,height)
        down=jnp.where(r!=height-1,up[o+width:o+width+CHUNK,:],0.0)
        upv=jnp.where(r!=0,um[o-width:o-width+CHUNK,:],0.0)
        add(t,down+upv)

def fwd_kernel(PS,PA,total,big_ref,q_ref,k_ref,v_ref,g_ref,p_ref,taps_ref,gain_ref,mixed_ref,comb_ref,a_ref,s_ref,vp,up,um,lvl_ref,tri_ref,st):
    chunks=total//CHUNK
    @pl.when(pl.program_id(0)==0)
    def _():
        lvl,i,j=level_matrix()
        lvl_ref[...]=jnp.where(i>j,lvl,jnp.where(i==j,-1,-2))
        tri_ref[...]=jnp.where(i>=j,1.0,0.0).astype(bf16)
        z=jnp.zeros((MARGIN,LANES),f32)
        for r in (vp,up,um):
            r[0:MARGIN,:]=z; r[MARGIN+total:,:]=z
    big=big_ref[0]==4*SIDE*SIDE
    taps=taps_ref[0]; gain=gain_ref[...]
    vp[MARGIN:MARGIN+total,:]=v_ref[0]
    def conv(width):
        def store(t,x): comb_ref[0,t*CHUNK:(t+1)*CHUNK,:]=x
        def add(t,x): comb_ref[0,t*CHUNK:(t+1)*CHUNK,:]+=x
        conv_forward(vp,up,um,taps,store,total,width,width)
        conv_finish(up,um,add,total,width,width)
    @pl.when(big)
    def _(): conv(2*SIDE)
    @pl.when(jnp.logical_not(big))
    def _(): conv(SIDE)
    per=SIDE*SIDE//CHUNK
    def step(c,_):
        rows=pl.ds(pl.multiple_of(c*CHUNK,CHUNK),CHUNK)
        start=jnp.where(big,c==0,lax.rem(c,per)==0)
        S=jnp.where(start,0.0,st[...])
        s_ref[0,c]=S
        q=q_ref[0,rows,:]*(HDIM**-0.5); k=k_ref[0,rows,:]; v=v_ref[0,rows,:]
        lw=log_decay2(p_ref[0,rows,:])
        L=sel_mm(tri_ref[...],lw,3)
        lvl=lvl_ref[...]
        diag=jnp.sum(q*k,axis=1,keepdims=True)
        A=jnp.where(lvl==-1,diag,0.0)
        for b,E,W in level_ops(q,k,L,lw):
            A=jnp.where(lvl==b,mmx(W,W,1,1,PS),A)
        a_ref[0,c]=A.astype(a_ref.dtype)
        last=L[CHUNK-1:CHUNK,:]
        o=mmx(A,v,1,0,PA)+mmx(q*jnp.exp2(L),S,1,1,PA)
        st[...]=S*jnp.exp2(last)+mmx(v,k*jnp.exp2(last-L),0,0,PA)
        cb=comb_ref[0,rows,:]+o
        comb_ref[0,rows,:]=cb
        g=g_ref[0,rows,:]
        r=lax.rsqrt(jnp.sum(cb*cb,axis=1,keepdims=True)*(1.0/HDIM)+head_eps)
        mixed_ref[0,rows,:]=(cb*r*gain*(g/(1.0+jnp.exp(-g)))).astype(bf16)
        return 0
    lax.fori_loop(0,chunks,step,0)

def gla_forward(big,qkvg,pre,taps,gain,PS=2,PA=2,adt=f32):
    _,H,total,_=qkvg.shape; chunks=total//CHUNK
    row=pl.BlockSpec((1,total,LANES),lambda h:(h,0,0))
    def of(i): return pl.BlockSpec((None,1,total,LANES),lambda h:(i,h,0,0))
    return pl.pallas_call(
        functools.partial(fwd_kernel,PS,PA,total),
        grid=(H,),
        in_specs=[pl.BlockSpec(memory_space=pltpu.SMEM)]+[of(i) for i in range(4)]+[row]+[pl.BlockSpec((1,16,LANES),lambda h:(h,0,0)),pl.BlockSpec((1,LANES),lambda h:(0,0))],
        out_specs=[row,row,pl.BlockSpec((1,chunks,CHUNK,CHUNK),lambda h:(h,0,0,0)),pl.BlockSpec((1,chunks,LANES,LANES),lambda h:(h,0,0,0))],
        out_shape=[jax.ShapeDtypeStruct((H,total,LANES),bf16),jax.ShapeDtypeStruct((H,total,LANES),f32),
                   jax.ShapeDtypeStruct((H,chunks,CHUNK,CHUNK),adt),jax.ShapeDtypeStruct((H,chunks,LANES,LANES),f32)],
        scratch_shapes=[pltpu.VMEM((total+2*MARGIN,LANES),f32)]*3+[pltpu.VMEM((CHUNK,CHUNK),jnp.int32),pltpu.VMEM((CHUNK,CHUNK),bf16),pltpu.VMEM((LANES,LANES),f32)],
        compiler_params=pltpu.CompilerParams(vmem_limit_bytes=40*2**20,dimension_semantics=("arbitrary",)),
        name="gla_forward",
    )(big,qkvg,qkvg,qkvg,qkvg,pre,taps,gain)

def bwd_kernel(PS,PA,total,big_ref,q_ref,k_ref,v_ref,g_ref,p_ref,comb_ref,a_ref,s_ref,gm_ref,taps_ref,gain_ref,
               dqk_ref,dpre_ref,dtaps_ref,dvec_ref,vp,dcp,gl,gr,dvl,lvl_ref,tri_ref,ds,car):
    chunks=total//CHUNK
    @pl.when(pl.program_id(0)==0)
    def _():
        lvl,i,j=level_matrix()
        lvl_ref[...]=jnp.where(i==j,-1,lvl)
        tri_ref[0]=jnp.where(i>=j,1.0,0.0).astype(bf16)
        tri_ref[1]=jnp.where(i<=j,1.0,0.0).astype(bf16)
        z=jnp.zeros((MARGIN,LANES),f32)
        for r in (vp,dcp,gl,gr):
            r[0:MARGIN,:]=z; r[MARGIN+total:,:]=z
    big=big_ref[0]==4*SIDE*SIDE
    taps=taps_ref[0]; gain=gain_ref[...]
    vp[MARGIN:MARGIN+total,:]=v_ref[0]
    def rowwise(c,acc):
        rows=pl.ds(pl.multiple_of(c*CHUNK,CHUNK),CHUNK)
        cb=comb_ref[0,rows,:]; g=g_ref[0,rows,:]; gm=gm_ref[0,rows,:].astype(f32)
        r=lax.rsqrt(jnp.sum(cb*cb,axis=1,keepdims=True)*(1.0/HDIM)+head_eps)
        n=cb*r
        sg=1.0/(1.0+jnp.exp(-g)); silu=g*sg
        dqk_ref[3,0,rows,:]=(gm*n*gain*(sg+silu*(1.0-sg))).astype(bf16)
        dn=gm*silu
        acc=acc+jnp.sum((dn*n).reshape(CHUNK//8,8,LANES),axis=0)
        dn=dn*gain
        dc=r*(dn-n*(jnp.sum(dn*n,axis=1,keepdims=True)*(1.0/HDIM)))
        dcp[pl.ds(pl.multiple_of(MARGIN+c*CHUNK,MARGIN),CHUNK),:]=dc
        return acc
    dgain=lax.fori_loop(0,chunks,rowwise,jnp.zeros((8,LANES),f32))
    dvec_ref[0,0:1,:]=jnp.sum(dgain,axis=0,keepdims=True)
    def conv(width):
        height=width
        accs=[jnp.zeros((8,LANES),f32) for _ in range(9)]
        for t in range(chunks):
            o=MARGIN+t*CHUNK
            col,r=image_masks(t*CHUNK,CHUNK,width,height)
            zs=[jnp.where(r!=height-1,dcp[o+width:o+width+CHUNK,:],0.0),dcp[o:o+CHUNK,:],jnp.where(r!=0,dcp[o-width:o-width+CHUNK,:],0.0)]
            vs=[jnp.where(col!=0,vp[o-1:o-1+CHUNK,:],0.0),vp[o:o+CHUNK,:],jnp.where(col!=width-1,vp[o+1:o+1+CHUNK,:],0.0)]
            for a in range(3):
                for b in range(3):
                    accs[3*a+b]=accs[3*a+b]+jnp.sum((zs[a]*vs[b]).reshape(CHUNK//8,8,LANES),axis=0)
            def comb(b): return zs[0]*taps[b:b+1,:]+zs[1]*taps[3+b:4+b,:]+zs[2]*taps[6+b:7+b,:]
            gl[o:o+CHUNK,:]=comb(0)
            dvl[t*CHUNK:(t+1)*CHUNK,:]=comb(1)
            gr[o:o+CHUNK,:]=comb(2)
        for i in range(9):
            dtaps_ref[0,i:i+1,:]=jnp.sum(accs[i],axis=0,keepdims=True)
        for t in range(chunks):
            o=MARGIN+t*CHUNK
            col,_=image_masks(0,CHUNK,width,height)
            dvl[t*CHUNK:(t+1)*CHUNK,:]+=jnp.where(col!=width-1,gl[o+1:o+1+CHUNK,:],0.0)+jnp.where(col!=0,gr[o-1:o-1+CHUNK,:],0.0)
    @pl.when(big)
    def _(): conv(2*SIDE)
    @pl.when(jnp.logical_not(big))
    def _(): conv(SIDE)
    per=SIDE*SIDE//CHUNK
    row=iota2((CHUNK,LANES),0)
    def step(i,acc):
        c=chunks-1-i
        rows=pl.ds(pl.multiple_of(c*CHUNK,CHUNK),CHUNK)
        end=jnp.where(big,c==chunks-1,lax.rem(c,per)==per-1)
        dS=jnp.where(end,0.0,ds[...])
        carry=jnp.where(end,0.0,car[0:1,:])
        q=q_ref[0,rows,:]*(HDIM**-0.5); k=k_ref[0,rows,:]; v=v_ref[0,rows,:]
        pre=p_ref[0,rows,:]
        lw=log_decay2(pre)
        L=sel_mm(tri_ref[0],lw,3)
        do=dcp[pl.ds(pl.multiple_of(MARGIN+c*CHUNK,MARGIN),CHUNK),:]
        lvl=lvl_ref[...]
        low=tri_ref[0].astype(f32)>0.5
        G=jnp.where(low,mmx(do,v,1,1,PS),mmx(v,do,1,1,PS))
        last=L[CHUNK-1:CHUNK,:]
        eL=jnp.exp2(L); eR=jnp.exp2(last-L)
        S=s_ref[0,c]
        dq=eL*mmx(do,S,1,0,PA)
        kR=k*eR
        dk=eR*mmx(v,dS,1,0,PA)
        dv=dvl[rows,:]+mmx(a_ref[0,c].astype(f32),do,0,0,PA)+mmx(kR,dS,1,1,PA)
        ds[...]=dS*jnp.exp2(last)+mmx(do,q*eL,0,0,PA)
        for b,E,W in level_ops(q,k,L,lw):
            Y=E*mmx(jnp.where(lvl==b,G,0.0),W,1,0,PS)
            right=(row&b)!=0
            dq=dq+jnp.where(right,Y,0.0); dk=dk+jnp.where(right,0.0,Y)
        z=q*dq-k*dk
        suf=sel_mm(tri_ref[1],z,3)+carry
        car[0:1,:]=suf[0:1,:]
        dp=suf*((1.0/GATE_NORM)/(1.0+jnp.exp(pre)))
        dpre_ref[0,rows,:]=dp
        t=jnp.sum(do*v,axis=1,keepdims=True)
        dqk_ref[0,0,rows,:]=((dq+t*k)*(HDIM**-0.5)).astype(bf16)
        dqk_ref[1,0,rows,:]=(dk+t*q).astype(bf16)
        dqk_ref[2,0,rows,:]=dv.astype(bf16)
        return acc+jnp.sum(dp.reshape(CHUNK//8,8,LANES),axis=0)
    db=lax.fori_loop(0,chunks,step,jnp.zeros((8,LANES),f32))
    dvec_ref[0,1:2,:]=jnp.sum(db,axis=0,keepdims=True)

def gla_backward(big,qkvg,pre,comb,A,S,gm,taps,gain,PS=2,PA=2):
    _,H,total,_=qkvg.shape; chunks=total//CHUNK
    row=pl.BlockSpec((1,total,LANES),lambda h:(h,0,0))
    def of(i): return pl.BlockSpec((None,1,total,LANES),lambda h:(i,h,0,0))
    return pl.pallas_call(
        functools.partial(bwd_kernel,PS,PA,total),
        grid=(H,),
        in_specs=[pl.BlockSpec(memory_space=pltpu.SMEM)]+[of(i) for i in range(4)]+[row]*2+[pl.BlockSpec((1,chunks,CHUNK,CHUNK),lambda h:(h,0,0,0)),pl.BlockSpec((1,chunks,LANES,LANES),lambda h:(h,0,0,0)),row,
                  pl.BlockSpec((1,16,LANES),lambda h:(h,0,0)),pl.BlockSpec((1,LANES),lambda h:(0,0))],
        out_specs=[pl.BlockSpec((4,1,total,LANES),lambda h:(0,h,0,0)),row,pl.BlockSpec((1,16,LANES),lambda h:(h,0,0)),pl.BlockSpec((1,8,LANES),lambda h:(h,0,0))],
        out_shape=[jax.ShapeDtypeStruct((4,H,total,LANES),bf16),jax.ShapeDtypeStruct((H,total,LANES),f32),
                   jax.ShapeDtypeStruct((H,16,LANES),f32),jax.ShapeDtypeStruct((H,8,LANES),f32)],
        scratch_shapes=[pltpu.VMEM((total+2*MARGIN,LANES),f32)]*4+[pltpu.VMEM((total,LANES),f32),pltpu.VMEM((CHUNK,CHUNK),jnp.int32),pltpu.VMEM((2,CHUNK,CHUNK),bf16),pltpu.VMEM((LANES,LANES),f32),pltpu.VMEM((8,LANES),f32)],
        compiler_params=pltpu.CompilerParams(vmem_limit_bytes=48*2**20,dimension_semantics=("arbitrary",)),
        name="gla_backward",
    )(big,qkvg,qkvg,qkvg,qkvg,pre,comb,A,S,gm,taps,gain)


ROWS = 256


def head_window(res, column):
    base = column // LANES * LANES
    off = column - base
    width = LANES if off + HDIM <= LANES else 2 * LANES
    part = res[:, base : base + width]
    if off:
        part = pltpu.roll(part, width - off, 1)
    part = part[:, :LANES]
    return jnp.where(iota2(part.shape, 1) < HDIM, part, 0.0)


def heads_joined(pieces):
    blocks = [None] * (len(pieces) * HDIM // LANES + 1)

    def put(index, value):
        blocks[index] = value if blocks[index] is None else blocks[index] + value

    for h, x in enumerate(pieces):
        index, off = h * HDIM // LANES, h * HDIM % LANES
        if off == 0:
            put(index, x)
            continue
        r = pltpu.roll(x, off, 1)
        if off + HDIM <= LANES:
            put(index, r)
        else:
            lane = iota2(r.shape, 1)
            put(index, jnp.where(lane >= off, r, 0.0))
            put(index + 1, jnp.where(lane < off, r, 0.0))
    total = len(pieces) * HDIM
    blocks = [b for b in blocks if b is not None]
    return jnp.concatenate(blocks, axis=1)[:, :total]


def project_kernel(H, turn_ref, x_ref, w_ref, down_ref, up_ref, bias_ref, out_ref, pre_ref, lat_ref):
    x = x_ref[...]
    span = 2 * H * HDIM
    for s in range(2):
        res = mm(x, w_ref[:, s * span : (s + 1) * span], 1, 0)
        for i in range(2 * H):
            out_ref[2 * s + i // H, i % H] = head_window(res, i * HDIM)
    latent = mm(x, down_ref[...], 1, 0)
    lat_ref[...] = latent
    pre = bias_ref[...] + sum(mm(p, up_ref[...], 1, 0) for p in parts(latent, 3)[::-1])
    for h in range(H):
        pre_ref[h] = pre[:, h * LANES : (h + 1) * LANES]


def project(turn, x, w, down, up, bias, H):
    total, width = x.shape
    tiles = total // ROWS

    def turned(i, t):
        return lax.rem(i + t[0], tiles)

    full = lambda a: pl.BlockSpec(a.shape, lambda i, t: (0, 0))
    return pl.pallas_call(
        functools.partial(project_kernel, H),
        grid_spec=pltpu.PrefetchScalarGridSpec(
            num_scalar_prefetch=1,
            grid=(tiles,),
            in_specs=[pl.BlockSpec((ROWS, width), lambda i, t: (i, 0)), full(w), full(down), full(up), full(bias)],
            out_specs=[
                pl.BlockSpec((4, H, ROWS, LANES), lambda i, t: (0, 0, turned(i, t), 0)),
                pl.BlockSpec((H, ROWS, LANES), lambda i, t: (0, turned(i, t), 0)),
                pl.BlockSpec((ROWS, LANES), lambda i, t: (turned(i, t), 0)),
            ],
        ),
        out_shape=[
            jax.ShapeDtypeStruct((4, H, total, LANES), f32),
            jax.ShapeDtypeStruct((H, total, LANES), f32),
            jax.ShapeDtypeStruct((total, LANES), f32),
        ],
        compiler_params=pltpu.CompilerParams(vmem_limit_bytes=56 * 2**20, dimension_semantics=("arbitrary",)),
        name="project",
    )(turn, x, w, down, up, bias)


def attend_kernel(H, turn_ref, m_ref, w_ref, out_ref, cat_ref):
    cat = heads_joined([m_ref[h].astype(f32) for h in range(H)]).astype(bf16)
    cat_ref[...] = cat
    out_ref[...] = mm(cat, w_ref[...], 1, 1)


def attend(turn, mixed, w):
    H, total, _ = mixed.shape
    tiles = total // ROWS
    inner = H * HDIM
    return pl.pallas_call(
        functools.partial(attend_kernel, H),
        grid_spec=pltpu.PrefetchScalarGridSpec(
            num_scalar_prefetch=1,
            grid=(tiles,),
            in_specs=[
                pl.BlockSpec((H, ROWS, LANES), lambda i, t: (0, lax.rem(i + t[0], tiles), 0)),
                pl.BlockSpec(w.shape, lambda i, t: (0, 0)),
            ],
            out_specs=[pl.BlockSpec((ROWS, w.shape[0]), lambda i, t: (i, 0)), pl.BlockSpec((ROWS, inner), lambda i, t: (i, 0))],
        ),
        out_shape=[jax.ShapeDtypeStruct((total, w.shape[0]), f32), jax.ShapeDtypeStruct((total, inner), bf16)],
        compiler_params=pltpu.CompilerParams(vmem_limit_bytes=40 * 2**20, dimension_semantics=("arbitrary",)),
        name="attend",
    )(turn, mixed, w)


def attend_back_kernel(H, turn_ref, g_ref, w_ref, out_ref):
    res = mm(g_ref[...], w_ref[...], 1, 0)
    res = jnp.concatenate([res, jnp.zeros((ROWS, -res.shape[1] % LANES), f32)], axis=1)
    for h in range(H):
        out_ref[h] = head_window(res, h * HDIM)


def attend_back(turn, grad, w, H):
    total, width = grad.shape
    tiles = total // ROWS
    return pl.pallas_call(
        functools.partial(attend_back_kernel, H),
        grid_spec=pltpu.PrefetchScalarGridSpec(
            num_scalar_prefetch=1,
            grid=(tiles,),
            in_specs=[pl.BlockSpec((ROWS, width), lambda i, t: (i, 0)), pl.BlockSpec(w.shape, lambda i, t: (0, 0))],
            out_specs=pl.BlockSpec((H, ROWS, LANES), lambda i, t: (0, lax.rem(i + t[0], tiles), 0)),
        ),
        out_shape=jax.ShapeDtypeStruct((H, total, LANES), f32),
        compiler_params=pltpu.CompilerParams(vmem_limit_bytes=40 * 2**20, dimension_semantics=("arbitrary",)),
        name="attend_back",
    )(turn, grad, w)


def project_back_kernel(H, turn_ref, d_ref, p_ref, lat_ref, w_ref, down_ref, up_ref, out_ref, cat_ref, glat_ref, dup_ref):
    @pl.when(pl.program_id(0) == 0)
    def _():
        dup_ref[...] = jnp.zeros_like(dup_ref)

    lat = parts(lat_ref[...], 2)
    glat = jnp.zeros((ROWS, LANES), f32)
    for h in range(H):
        dp = parts(p_ref[h], 3)
        up = up_ref[:, h * LANES : (h + 1) * LANES]
        glat = glat + (mm(dp[2], up, 1, 1) + mm(dp[1], up, 1, 1) + mm(dp[0], up, 1, 1))
        dup_ref[h] += mm(lat[0], dp[1], 0, 0) + mm(lat[1], dp[0], 0, 0) + mm(lat[0], dp[0], 0, 0)
    glat_ref[...] = glat
    span = 2 * H * HDIM
    acc = sum(mm(p, down_ref[...], 1, 1) for p in parts(glat, 2)[::-1])
    for s in range(2):
        cat = heads_joined([d_ref[2 * s + i // H, i % H].astype(f32) for i in range(2 * H)]).astype(bf16)
        cat_ref[:, s * span : (s + 1) * span] = cat
        acc = acc + mm(cat, w_ref[:, s * span : (s + 1) * span], 1, 1)
    out_ref[...] = acc


def project_back(turn, d, dpre, latent, w, down, up):
    _, H, total, _ = d.shape
    tiles = total // ROWS
    width, cols = w.shape

    def turned(i, t):
        return lax.rem(i + t[0], tiles)

    full = lambda a: pl.BlockSpec(a.shape, lambda i, t: (0, 0))
    return pl.pallas_call(
        functools.partial(project_back_kernel, H),
        grid_spec=pltpu.PrefetchScalarGridSpec(
            num_scalar_prefetch=1,
            grid=(tiles,),
            in_specs=[
                pl.BlockSpec((4, H, ROWS, LANES), lambda i, t: (0, 0, turned(i, t), 0)),
                pl.BlockSpec((H, ROWS, LANES), lambda i, t: (0, turned(i, t), 0)),
                pl.BlockSpec((ROWS, LANES), lambda i, t: (turned(i, t), 0)),
                full(w), full(down), full(up),
            ],
            out_specs=[
                pl.BlockSpec((ROWS, width), lambda i, t: (i, 0)),
                pl.BlockSpec((ROWS, cols), lambda i, t: (i, 0)),
                pl.BlockSpec((ROWS, LANES), lambda i, t: (i, 0)),
                pl.BlockSpec((H, LANES, LANES), lambda i, t: (0, 0, 0)),
            ],
        ),
        out_shape=[
            jax.ShapeDtypeStruct((total, width), f32),
            jax.ShapeDtypeStruct((total, cols), bf16),
            jax.ShapeDtypeStruct((total, LANES), f32),
            jax.ShapeDtypeStruct((H, LANES, LANES), f32),
        ],
        compiler_params=pltpu.CompilerParams(vmem_limit_bytes=56 * 2**20, dimension_semantics=("arbitrary",)),
        name="project_back",
    )(turn, d, dpre, latent, w, down, up)


NORM_EPS = 1e-06
FLIP = [(0, 1), (1, 0)]
EVERY = ("dq", "mp")
COLUMNS = ("dq", "core")


def swap(x):
    return lax.ppermute(x, ("core", "mp"), [(0, 0), (1, 2), (2, 1), (3, 3)])


def other(x):
    return lax.ppermute(x, "core", FLIP)


def both(x):
    return jnp.concatenate([x, other(x)], axis=0)


def summed(x):
    half = x.shape[0] // 2
    return x[:half] + other(x[half:])


def gathered(x):
    return lax.all_gather(x, EVERY, axis=0, tiled=True)


def reduced(x):
    return lax.psum_scatter(x.astype(bf16), EVERY, scatter_dimension=0, tiled=True).astype(f32)


def modulate(rows, shift, scale):
    center = rows - jnp.mean(rows, axis=-1, keepdims=True)
    normed = center * lax.rsqrt(jnp.mean(center * center, axis=-1, keepdims=True) + NORM_EPS)
    return normed * (1.0 + scale[:, None, :]) + shift[:, None, :]


def per_head(x, heads, rows):
    x = x.reshape(x.shape[0], heads, HDIM)
    return jnp.pad(x, ((0, rows - x.shape[0]), (0, 0), (0, LANES - HDIM)))


def contract(a, b, i, j):
    return lax.dot_general(a, b, (((i,), (j,)), ((), ())), preferred_element_type=f32)


def silu(v):
    return v * jax.nn.sigmoid(v)


def on_device(
    block_input, out_grad, time_table, class_table, time_ids, class_ids, image_patches, ada_weight, ada_bias,
    proj_weight, decay_down, decay_up, decay_bias, head_gain, conv_taps, out_weight, fc1_weight, fc2_weight,
):
    rows, width = block_input.shape
    inner = proj_weight.shape[2]
    heads = inner // HDIM
    core = lax.axis_index("core")
    y = lax.axis_index("mp")
    dq = lax.axis_size("dq")
    slot_rows = SIDE * SIDE
    own_slots = rows // slot_rows
    unit_slots = 2 * own_slots

    w_proj = gathered(swap(proj_weight.transpose(1, 0, 2).reshape(-1, 4 * inner)))
    x = swap(block_input)
    w_out = gathered(swap(out_weight.T))
    w_fc1 = gathered(swap(fc1_weight))
    w_fc2 = gathered(swap(fc2_weight.T))
    g_rows = swap(out_grad)

    ids = jnp.concatenate([time_ids, class_ids, image_patches])[None]
    ids = lax.all_to_all(jnp.broadcast_to(ids, (2 * dq, ids.shape[1])), COLUMNS, split_axis=0, concat_axis=0, tiled=True)
    t_all, c_all = ids[:, :unit_slots].reshape(-1), ids[:, unit_slots : 2 * unit_slots].reshape(-1)
    big_all = ids[:, 2 * unit_slots] == 4 * slot_rows
    me = 2 * lax.axis_index("dq") + y
    patches = lax.dynamic_slice_in_dim(ids[:, 2 * unit_slots], me, 1)
    condition = time_table[t_all].astype(f32) + class_table[c_all].astype(f32)
    silu_all = silu(condition).astype(bf16)
    columns = jnp.dot(silu_all, ada_weight, preferred_element_type=f32) + ada_bias.astype(f32)
    part = columns.shape[1]
    columns = columns.reshape(2 * dq, unit_slots, part)
    columns = jnp.where(big_all[:, None, None], columns[:, :1], columns)
    columns = lax.dynamic_index_in_dim(columns.reshape(dq, 2, 2, own_slots, part), y, 1, keepdims=False)
    columns = lax.all_to_all(columns.reshape(2 * dq, own_slots, part), COLUMNS, split_axis=0, concat_axis=0, tiled=True)
    modulation = columns.transpose(1, 0, 2).reshape(own_slots, 6 * width)
    shift1, scale1, gate1, shift2, scale2, gate2 = jnp.split(modulation, 6, axis=1)

    start = core * inner
    up_local = lax.dynamic_slice_in_dim(decay_up, start, inner, 1)
    bias_local = lax.dynamic_slice_in_dim(decay_bias, start, inner, 0)
    taps_local = lax.dynamic_slice_in_dim(conv_taps, start, inner, 1)
    lowrank = decay_down.shape[1]
    down_pad = jnp.pad(decay_down, ((0, 0), (0, LANES - lowrank)))
    up_pad = per_head(up_local, heads, LANES).reshape(LANES, heads * LANES)
    bias_pad = per_head(bias_local[None].astype(f32), heads, 1).reshape(1, heads * LANES)
    taps_pad = per_head(taps_local.astype(f32), heads, 16).transpose(1, 0, 2)
    gain_pad = jnp.pad(head_gain.astype(f32), (0, LANES - HDIM))[None]
    turn = (core * (rows // ROWS)).astype(jnp.int32)[None]

    residual = x.astype(f32).reshape(own_slots, slot_rows, width)
    hidden, norm_back_one = jax.vjp(modulate, residual, shift1, scale1)
    hidden_all = both(hidden.reshape(rows, width).astype(bf16))
    qkvg, pre, latent = project(turn, hidden_all, w_proj, down_pad, up_pad, bias_pad, heads)
    mixed, comb, scores, states = gla_forward(patches, qkvg, pre, taps_pad, gain_pad)
    attn_part, mixed_cat = attend(turn, mixed, w_out)
    attention = summed(attn_part).reshape(own_slots, slot_rows, width)
    after_attn = residual + gate1[:, None, :] * attention
    hidden_two, norm_back_two = jax.vjp(modulate, after_attn, shift2, scale2)
    hidden_two_all = both(hidden_two.reshape(rows, width).astype(bf16))
    up_proj = jnp.dot(hidden_two_all, w_fc1, preferred_element_type=f32)
    active, gelu_back = jax.vjp(functools.partial(jax.nn.gelu, approximate=True), up_proj)
    active_low = active.astype(bf16)
    feed_out = summed(contract(active_low, w_fc2, 1, 1)).reshape(own_slots, slot_rows, width)
    result = after_attn + gate2[:, None, :] * feed_out
    block_out = swap(result.reshape(rows, width).astype(bf16))

    grad_rows = g_rows.astype(f32).reshape(own_slots, slot_rows, width)
    grad_gate_two = jnp.sum(grad_rows * feed_out, axis=1)
    grad_feed_all = both((grad_rows * gate2[:, None, :]).astype(bf16).reshape(rows, width))
    grad_active = jnp.dot(grad_feed_all, w_fc2, preferred_element_type=f32)
    grad_fc2 = reduced(contract(grad_feed_all, active_low, 0, 0))
    grad_up = gelu_back(grad_active)[0].astype(bf16)
    grad_fc1 = reduced(contract(hidden_two_all, grad_up, 0, 0))
    grad_hidden_two = summed(contract(grad_up, w_fc1, 1, 1))
    grad_after, grad_shift_two, grad_scale_two = norm_back_two(grad_hidden_two.reshape(own_slots, slot_rows, width))
    grad_after = grad_after + grad_rows
    grad_gate_one = jnp.sum(grad_after * attention, axis=1)
    grad_attn_all = both((grad_after * gate1[:, None, :]).astype(bf16).reshape(rows, width))
    grad_mixed = attend_back(turn, grad_attn_all, w_out, heads)
    grad_out = reduced(contract(grad_attn_all, mixed_cat, 0, 0))
    d_qkvg, d_pre, d_taps, d_vec = gla_backward(patches, qkvg, pre, comb, scores, states, grad_mixed, taps_pad, gain_pad)
    hidden_part, d_cat, grad_latent, d_up = project_back(turn, d_qkvg, d_pre, latent, w_proj, down_pad, up_pad)
    grad_proj = reduced(contract(hidden_all, d_cat, 0, 0))
    grad_residual, grad_shift_one, grad_scale_one = norm_back_one(summed(hidden_part).reshape(own_slots, slot_rows, width))
    input_grad = swap((grad_residual + grad_after).reshape(rows, width))

    lat_hi = grad_latent[:, :lowrank].astype(bf16)
    lat_lo = (grad_latent[:, :lowrank] - lat_hi.astype(f32)).astype(bf16)
    d_down = contract(hidden_all, jnp.concatenate([lat_hi, lat_lo], axis=1), 0, 0)
    d_down = d_down[:, :lowrank] + d_down[:, lowrank:]

    def placed(value):
        return lax.dynamic_update_slice_in_dim(jnp.zeros((value.shape[0], width), f32), value, start, 1)

    d_up = d_up[:, :lowrank, :HDIM].transpose(1, 0, 2).reshape(lowrank, inner)
    d_taps = d_taps[:, :9, :HDIM].transpose(1, 0, 2).reshape(9, inner)
    d_bias = d_vec[:, 1, :HDIM].reshape(1, inner)
    d_gain = jnp.sum(d_vec[:, 0, :HDIM], axis=0)
    stacked = placed(jnp.concatenate([d_up, d_taps, d_bias], axis=0))
    flat = jnp.concatenate([d_down.reshape(lowrank, width), stacked, jnp.pad(d_gain, (0, width - HDIM))[None]], axis=0)
    for bit in range(dq.bit_length() - 1):
        flat = flat + lax.ppermute(flat, "dq", [(i, i ^ (1 << bit)) for i in range(dq)])
    flat = flat + lax.ppermute(flat, "mp", FLIP)
    flat = flat + other(flat)
    down_sum = flat[:lowrank].reshape(width, lowrank)
    up_sum = flat[lowrank : 2 * lowrank]
    taps_sum = flat[2 * lowrank : 2 * lowrank + 9]
    bias_sum = flat[2 * lowrank + 9]
    gain_sum = flat[2 * lowrank + 10, :HDIM]

    grad_mod = jnp.concatenate(
        [grad_shift_one, grad_scale_one, grad_gate_one, grad_shift_two, grad_scale_two, grad_gate_two], axis=1
    ).astype(bf16)
    grad_mod = grad_mod.reshape(own_slots, 2 * dq, part).transpose(1, 0, 2)
    got = lax.all_to_all(grad_mod, COLUMNS, split_axis=0, concat_axis=0, tiled=True).reshape(dq, 1, unit_slots, part)
    away = lax.ppermute(got, "mp", FLIP)
    got = jnp.where(y == 0, jnp.concatenate([got, away], axis=1), jnp.concatenate([away, got], axis=1))
    got = got.reshape(2 * dq, unit_slots, part).astype(f32)
    folded = jnp.sum(got, axis=1, keepdims=True)
    first = jnp.arange(unit_slots)[None, :, None] == 0
    got = jnp.where(big_all[:, None, None], jnp.where(first, folded, 0.0), got).reshape(-1, part)
    ada_bias_grad = jnp.sum(got, axis=0)
    ada_weight_grad = jnp.dot(silu_all.astype(f32).T, got, precision=lax.Precision.HIGHEST, preferred_element_type=f32)
    grad_silu = jnp.dot(got, ada_weight.astype(f32).T, precision=lax.Precision.HIGHEST, preferred_element_type=f32)
    grad_silu = lax.all_to_all(grad_silu, COLUMNS, split_axis=0, concat_axis=0, tiled=True)
    grad_silu = jnp.sum(grad_silu.reshape(2 * dq, unit_slots, width), axis=0)
    own_cond = time_table[time_ids].astype(f32) + class_table[class_ids].astype(f32)
    gate = jax.nn.sigmoid(own_cond)
    cond_grad = grad_silu * (gate * (1.0 + own_cond * (1.0 - gate)))

    proj_grad = swap(grad_proj).reshape(-1, 4, inner).transpose(1, 0, 2)
    return (
        block_out, input_grad, cond_grad, ada_weight_grad, ada_bias_grad, proj_grad, down_sum, up_sum, bias_sum,
        gain_sum, taps_sum, swap(grad_out).T, swap(grad_fc1), swap(grad_fc2).T,
    )


def solution(mesh):
    dp, mp = mesh.shape["dp"], mesh.shape["mp"]
    split = Mesh(mesh.devices.reshape(dp // 2, 2, mp), ("dq", "core", "mp"))
    d = ("dq", "core")
    every = ("dq", "core", "mp")
    return jax.shard_map(
        on_device,
        mesh=split,
        in_specs=(
            P(every, None), P(every, None), P(), P(), P(d), P(d), P(d), P(None, d), P(d), P(None, d, "mp"),
            P(), P(), P(), P(), P(), P("mp", d), P(d, "mp"), P("mp", d),
        ),
        out_specs=(
            P(every, None), P(every, None), P(d, None), P(None, d), P(d), P(None, d, "mp"),
            P(), P(), P(), P(), P(), P("mp", d), P(d, "mp"), P("mp", d),
        ),
        check_vma=False,
    )
```

time: 3060 us -> 997 us (0.33)
  other arithmetic: 1420 us -> 56.7 us
  matrix products: 471 us -> 93.9 us
  local copies, waits for them, and re-layouts: 380 us -> 90 us
  Pallas kernels: 0 us -> 211 us
  waiting for transfers between devices: 553 us -> 407 us
  blocking collectives: 118 us -> 10.4 us
    dot_general x64 -> x0, other arithmetic: 653 us -> none  [block_step(): jnp.einsum('hik,hjk,hijk->hij', query_rows, key_matrix, jnp.exp(spread),...]
    dot_general x215 -> x12, matrix products: 471 us -> 93.9 us  [the longest x7 60.9 us: contract(): lax.dot_general(a, b, (((i,), (j,)), ((), ())), preferred_element_type=f32)]
    reduce_sum x68 -> x11, other arithmetic: 309 us -> 5.91 us  [the longest x4 2.21 us: modulate(): center = rows - jnp.mean(rows, axis=-1, keepdims=True)]
    pallas_call x0 -> x6, Pallas kernels: none -> 211 us  [the longest x1 86.7 us: gla_forward(): pl.pallas_call(functools.partial(fwd_kernel, PS, PA, total), grid=(H,), i...]
    another operation x97 -> x0, other arithmetic: 169 us -> none  [the longest x80 154 us: block_step(): prefix_decay = jnp.cumsum(log_decay, axis=1)]
    all_gather x9 -> x4, waiting for transfers between devices: 247 us -> 82.9 us  [gathered(): return lax.all_gather(x, EVERY, axis=0, tiled=True)]
    exp x32 -> x0, other arithmetic: 102 us -> none  [block_step(): jnp.exp(spread)]
    reduce_scatter x6 -> x3, waiting for transfers between devices: 144 us -> 244 us  [reduced(): lax.psum_scatter(x.astype(bf16), EVERY, scatter_dimension=0, tiled=True)]
  transfers between devices with their start and end apart: 23 -> 37, of which waited for: 13 -> 18; matrix products, arithmetic and copies ran while one was open for 73% -> 17% of each run, Pallas kernels for 0% -> 21%
where the time goes in v1:
time: 997 us; the launch traced here: 983 us
  waiting for transfers between devices  407 us (41%)
  Pallas kernels  211 us (21%)
  starting transfers between devices  98.2 us (10%)
  matrix products  93.9 us (9%)
  local copies, waits for them, and re-layouts  90 us (9%)
  other arithmetic  56.7 us (6%)
  between operations  16.1 us (2%)
  blocking collectives  10.4 us (1%)
    reduce_scatter x3, waiting for transfers between devices, reduced(): lax.psum_scatter(x.astype(bf16), EVERY, scatter_dimension=0, tiled=True)  244 us
    pallas_call x1, Pallas kernels, gla_forward(): pl.pallas_call(functools.partial(fwd_kernel, PS, PA, total), grid=(H,), i...  86.7 us
    pallas_call x1, Pallas kernels, gla_backward(): pl.pallas_call(functools.partial(bwd_kernel, PS, PA, total), grid=(H,), i...  84.8 us
    all_gather x4, waiting for transfers between devices, gathered(): return lax.all_gather(x, EVERY, axis=0, tiled=True)  82.9 us
    dot_general x7, matrix products, contract(): lax.dot_general(a, b, (((i,), (j,)), ((), ())), preferred_element_type=f32)  60.9 us
    ppermute x12, waiting for transfers between devices, swap(): return lax.ppermute(x, ('core', 'mp'), [(0, 0), (1, 2), (2, 1), (3, 3)])  47.4 us
    ppermute x12, starting transfers between devices, swap(): return lax.ppermute(x, ('core', 'mp'), [(0, 0), (1, 2), (2, 1), (3, 3)])  44.4 us
    unnamed x137, local copies, waits for them, and re-layouts  38 us
  transfers between devices with their start and end apart: 37, of which 18 were waited for; matrix products, arithmetic and copies ran while one was open for 17% of the time, Pallas kernels for 21%

profile of v1, /device:TPU:1, one launch (start us, length us, event | category | flops | bytes accessed | tf_op | source)
XLA Modules:
  0.0 983.2 jit_solution(12813383700989778734)
XLA Ops:
  8.9 4.5 collective-permute-start.2
  13.4 4.8 collective-permute-done.2
  19.0 3.6 collective-permute-start.3
  22.7 2.4 collective-permute-done.3
  25.8 3.6 collective-permute-start.6
  29.5 7.8 collective-permute-done.6
  38.0 2.8 collective-permute-start.7
  41.5 5.2 collective-permute-done.7
  48.1 5.9 all-to-all-start
  54.1 2.8 collective-permute-start
  56.9 2.9 all-to-all-done
  61.5 3.4 gather_fusion
  64.9 2.4 convolution_add_fusion
  74.3 10.4 %all_to_all.25 = f32[16,2,432]{2,1,0:T(2,128)S(1)} all-to-all(f32[16,2,432]{2,1,0:T(2,128)S(1)} %bitcast.125), channel_id=1, replica_groups=mesh['dq'=8,'core'=2,'mp'=2] {'dq','core'}, dimensions={0} | all-to-all | bytes 110592 | tf_op jit(solution)/shard_map/all_to_all | solution.py:556
  99.6 3.2 pad_maximum_fusion.x_ref
  102.8 3.8 all-gather.5.cloned.1.call-done.w_ref
  106.6 15.4 %project.1 = (f32[4,8,1024,128]{3,2,1,0:T(8,128)}, f32[8,1024,128]{2,1,0:T(8,128)}, f32[1024,128]{1,0:T(8,128)}) custom-call(s32[1]{0:T(128)} %bitcast.6.turn_ref, bf16[1024,1152]{1,0:T(8,128)(2,1)} %pad_maximum_fusion.x_ref, bf16[1152,2304]{1,0:T(8,128)(2,1)} %all-gather.5.cloned.1.call-done.w_ref, bf16[1152,128]{1,0:T(8,128)(2,1)} %pad.27.down_ref, ...), custom_call_target="tpu_custom_call" | custom-call | tf_op jit(solution)/shard_map/project/pallas_call | solution.py:339
  122.0 86.7 %gla_forward.1 = (bf16[8,1024,128]{2,1,0:T(8,128)(2,1)S(1)}, f32[8,1024,128]{2,1,0:T(8,128)S(1)}, f32[8,8,128,128]{3,2,1,0:T(8,128)S(1)}, f32[8,8,128,128]{3,2,1,0:T(8,128)}) custom-call(s32[1]{0:T(128)} %bitcast.7.big_ref, f32[4,8,1024,128]{3,2,1,0:T(8,128)} %get-tuple-element.31.q_ref.k_ref.v_ref.g_ref, ...), custom_call_target="tpu_custom_call" | custom-call | tf_op jit(solution)/shard_map/gla_forward/pallas_call | solution.py:154
  217.0 3.2 attend.1
  223.3 4.7 collective-permute-start.10
  232.0 21.7 %collective-permute-done.10 = bf16[512,1152]{1,0:T(8,128)(2,1)S(1)} collective-permute-done((bf16[512,1152]{1,0:T(8,128)(2,1)S(1)}, bf16[512,1152]{1,0:T(8,128)(2,1)S(1)}, u32[]{:S(2)}, u32[]{:S(2)}) %collective-permute-start.10) | collective-permute-done | bytes 1179680 | tf_op jit(solution)/shard_map/ppermute | solution.py:479
  258.0 11.9 %fusion.23 = f32[1024,2304]{1,0:T(8,128)} fusion(bf16[1152,2304]{1,0:T(8,128)(2,1)} %all-gather.9.cloned.1.call-done, bf16[512,1152]{1,0:T(8,128)(2,1)} %collective-permute-done.5, bf16[512,1152]{1,0:T(8,128)(2,1)} %fusion.19), kind=kOutput, calls=%fused_computation.67 | convolution fusion | flops 5440536576 | bytes 17104896 | tf_op jit(solution)/shard_map/dot_general | solution.py:582
  269.9 77.1 %all-gather.11.cloned.1.call-done = bf16[1152,2304]{1,0:T(8,128)(2,1)} async-done(((bf16[72,2304]{1,0:T(8,128)(2,1)}), bf16[1152,2304]{1,0:T(8,128)(2,1)}) %all-gather.11.cloned.1.call-update) | async-done | bytes 5308432 | tf_op jit(solution)/shard_map/all_gather | solution.py:496
  347.0 14.5 %fusion.6 = bf16[1024,2304]{1,0:T(8,128)(2,1)S(1)} fusion(f32[1024,2304]{1,0:T(8,128)} %fusion.23, bf16[1152,2304]{1,0:T(8,128)(2,1)} %all-gather.11.cloned.1.call-done, bf16[512,1152]{1,0:T(8,128)(2,1)} %collective-permute-done.11, bf16[512,1152]{1,0:T(8,128)(2,1)} %fusion.17), kind=kOutput, calls=%fused_computation.15 | convolution fusion | flops 5487722496 | bytes 21823488 | tf_op jit(solution)/shard_map/dot_general | solution.py:592
  361.5 10.5 %fusion.57 = f32[1024,1152]{1,0:T(8,128)S(1)} fusion(bf16[1024,2304]{1,0:T(8,128)(2,1)S(1)} %fusion.6, bf16[1152,2304]{1,0:T(8,128)(2,1)} %all-gather.9.cloned.1.call-done), kind=kOutput, calls=%fused_computation.158 | convolution fusion | flops 5435817984 | bytes 14745600 | tf_op jit(solution)/shard_map/dot_general | solution.py:515
  373.9 4.2 collective-permute-done.12
  381.9 2.5 collective-permute-done.13
  385.4 3.2 convolution_convert_fusion.3
  388.7 10.5 %convolution_convert_fusion.1 = bf16[1152,2304]{1,0:T(8,128)(2,1)} fusion(bf16[1024,2304]{1,0:T(8,128)(2,1)} %copy-done.61, bf16[512,1152]{1,0:T(8,128)(2,1)} %collective-permute-done.5, bf16[512,1152]{1,0:T(8,128)(2,1)} %fusion.19), kind=kOutput, calls=%fused_computation.7 | convolution fusion | flops 5443190784 | bytes 12386304 | tf_op jit(solution)/shard_map/dot_general | solution.py:515
  399.2 11.6 %convolution_convert_fusion = bf16[1152,2304]{1,0:T(8,128)(2,1)} fusion(bf16[512,1152]{1,0:T(8,128)(2,1)} %collective-permute-done.11, bf16[512,1152]{1,0:T(8,128)(2,1)} %fusion.17, f32[1024,2304]{1,0:T(8,128)} %fusion.23), kind=kOutput, calls=%fused_computation.6 | convolution fusion | flops 5464424448 | bytes 17104896 | tf_op jit(solution)/shard_map/dot_general | solution.py:515
  413.0 3.8 attend_back.1.gm_ref
  416.8 2.1 copy-done.1
  419.0 84.8 %gla_backward.1 = (bf16[4,8,1024,128]{3,2,1,0:T(8,128)(2,1)}, f32[8,1024,128]{2,1,0:T(8,128)S(1)}, f32[8,16,128]{2,1,0:T(8,128)S(1)}, f32[8,8,128]{2,1,0:T(8,128)S(1)}) custom-call(s32[1]{0:T(128)} %bitcast.7.big_ref, f32[4,8,1024,128]{3,2,1,0:T(8,128)} %get-tuple-element.31.q_ref.k_ref.v_ref.g_ref, ...), custom_call_target="tpu_custom_call" | custom-call | tf_op jit(solution)/shard_map/gla_backward/pallas_call | solution.py:266
  503.8 2.0 copy-done.7
  505.9 17.3 %project_back.1 = (f32[1024,1152]{1,0:T(8,128)}, bf16[1024,2304]{1,0:T(8,128)(2,1)}, f32[1024,128]{1,0:T(8,128)}, f32[8,128,128]{2,1,0:T(8,128)}) custom-call(s32[1]{0:T(128)} %bitcast.6.turn_ref, bf16[4,8,1024,128]{3,2,1,0:T(8,128)(2,1)} %get-tuple-element.38.d_ref, f32[8,1024,128]{2,1,0:T(8,128)} %copy-done.7, f32[1024,128]{1,0:T(8,128)} %get-tuple-element.40.lat_ref, ...), custom_call_target="tpu_custom_call" | custom-call | tf_op jit(solution)/shard_map/project_back/pallas_call | solution.py:443
  523.1 10.5 %convolution_convert_fusion.2 = bf16[1152,2304]{1,0:T(8,128)(2,1)} fusion(bf16[1024,2304]{1,0:T(8,128)(2,1)} %get-tuple-element.42, bf16[512,1152]{1,0:T(8,128)(2,1)} %collective-permute-done.1, bf16[512,1152]{1,0:T(8,128)(2,1)} %fusion.14), kind=kOutput, calls=%fused_computation.8 | convolution fusion | flops 5443190784 | bytes 12386304 | tf_op jit(solution)/shard_map/dot_general | solution.py:515
  533.7 12.5 %fusion.50 = f32[1024,1152]{1,0:T(8,128)S(1)} fusion(bf16[1152,2304]{1,0:T(8,128)(2,1)} %all-gather.11.cloned.1.call-done, f32[1024,2304]{1,0:T(8,128)} %fusion.23), kind=kOutput, calls=%fused_computation.152 | convolution fusion | flops 5457051648 | bytes 19464192 | tf_op jit(solution)/shard_map/dot_general | solution.py:515
  549.0 3.4 slice.85
  556.0 2.2 fusion.31
  558.8 2.0 copy.132
  569.1 6.6 collective-permute-done.18
  578.6 4.1 collective-permute-done.19
  589.2 6.3 collective-permute-done.20
  596.6 3.0 collective-permute-start.21
  599.6 5.1 collective-permute-done.21
  606.8 9.8 fusion.21
  620.9 3.4 all-to-all-start.2
  624.3 4.5 add_add_fusion.3
  628.8 3.3 collective-permute-start.15
  632.9 3.2 gather_fusion.2
  639.2 17.4 %collective-permute-start.16 = (bf16[8,1,4,432]{3,2,0,1:T(4,128)(2,1)S(1)}, bf16[8,1,4,432]{3,2,0,1:T(4,128)(2,1)S(1)}, u32[]{:S(2)}, u32[]{:S(2)}) collective-permute-start(bf16[8,1,4,432]{3,2,0,1:T(4,128)(2,1)S(1)} %reshape.442), channel_id=1, source_target_pairs={{0,1},{1,0},{2,3},{3,2},{4,5},{5,4},{6,7},{7,6},{8,9},{9,8},{10,11... | collective-permute-start | bytes 82952 | tf_op jit(solution)/shard_map/ppermute | solution.py:638
  657.3 3.6 fusion.16
  660.9 2.3 collective-permute-start.9
  666.3 12.9 %all-to-all-start.3 = ((f32[16,4,1152]{2,1,0:T(4,128)}), f32[16,4,1152]{2,1,0:T(4,128)S(1)}, u32[]{:S(2)}, u32[]{:S(2)}) async-start(f32[16,4,1152]{2,1,0:T(4,128)} %copy.126), calls=%async_computation.3 | async-start | bytes 589824 | tf_op jit(solution)/shard_map/all_to_all | solution.py:647
  681.3 3.0 collective-permute-start.23
  691.8 2.7 collective-permute-start.24
  694.5 105.5 %reduce-scatter.11.cloned.1.call-done = bf16[72,2304]{1,0:T(8,128)(2,1)} async-done(((bf16[1152,2304]{1,0:T(8,128)(2,1)}), bf16[72,2304]{1,0:T(8,128)(2,1)}) %reduce-scatter.11.cloned.1.call-update) | async-done | bytes 331792 | tf_op jit(solution)/shard_map/reduce_scatter | solution.py:500
  801.9 5.5 collective-permute-start.25
  807.4 138.9 %reduce-scatter.7.cloned.1.call-done = bf16[72,2304]{1,0:T(8,128)(2,1)} async-done(((bf16[1152,2304]{1,0:T(8,128)(2,1)}), bf16[72,2304]{1,0:T(8,128)(2,1)}) %reduce-scatter.7.cloned.1.call-update) | async-done | bytes 331792 | tf_op jit(solution)/shard_map/reduce_scatter | solution.py:500
  948.1 5.4 collective-permute-start.17
  953.6 2.3 fusion.27
  956.6 5.5 collective-permute-done.17
  964.7 2.4 copy.158
  967.1 3.2 copy.159
  (314 shorter events, 118.9 us)
Async XLA Ops:
  7.2 52.9 %copy-start = (bf16[1001,1152]{1,0:T(8,128)(2,1)S(1)}, bf16[1001,1152]{1,0:T(8,128)(2,1)}, u32[]{:S(2)}) copy-start(bf16[1001,1152]{1,0:T(8,128)(2,1)} %param.21) | copy-start | bytes 6918916
  7.2 40.2 %copy-start.55 = (s32[4]{0:T(128)S(1)}, s32[4]{0:T(128)}, u32[]{:S(2)}) copy-start(s32[4]{0:T(128)} %param.23) | copy-start | bytes 52
  7.2 40.2 %copy-start.56 = (s32[4]{0:T(128)S(1)}, s32[4]{0:T(128)}, u32[]{:S(2)}) copy-start(s32[4]{0:T(128)} %param.22) | copy-start | bytes 52
  7.2 49.7 %copy-start.57 = (bf16[432]{0:T(512)(128)(2,1)S(1)}, bf16[432]{0:T(512)(128)(2,1)}, u32[]{:S(2)}) copy-start(bf16[432]{0:T(512)(128)(2,1)} %param.26) | copy-start | bytes 2596
  7.2 99.4 %all-gather.5.cloned.1.call-start = ((), (), s32[]{:S(2)}) async-start(), calls=%async_computation.8 | async-start | bytes 5640192 | tf_op jit(solution)/shard_map/all_gather | solution.py:496
  8.9 9.3 collective-permute-start.2
  19.0 195.1 %all-gather.7.cloned.1.call-start = ((), (), s32[]{:S(2)}) async-start(), calls=%async_computation.9 | async-start | bytes 1566720 | tf_op jit(solution)/shard_map/all_gather | solution.py:496
  19.0 6.1 collective-permute-start.3
  25.7 232.2 %all-gather.9.cloned.1.call-start = ((), (), s32[]{:S(2)}) async-start(), calls=%async_computation.10 | async-start | bytes 5640192 | tf_op jit(solution)/shard_map/all_gather | solution.py:496
  25.8 11.4 %collective-permute-start.6 = (bf16[72,2304]{1,0:T(8,128)(2,1)}, bf16[72,2304]{1,0:T(8,128)(2,1)S(1)}, u32[]{:S(2)}, u32[]{:S(2)}) collective-permute-start(bf16[72,2304]{1,0:T(8,128)(2,1)} %param.34), channel_id=1, source_target_pairs={{0,0},{1,2},{2,1},{3,3},{4,4},{5,6},{6,5},{7,7},{8,8},{9,10},{10,9... | collective-permute-start | bytes 995336 | tf_op jit(solution)/shard_map/ppermute | solution.py:479
  38.0 309.0 %all-gather.11.cloned.1.call-start = ((), (), s32[]{:S(2)}) async-start(), calls=%async_computation.11 | async-start | bytes 5640192 | tf_op jit(solution)/shard_map/all_gather | solution.py:496
  38.0 8.7 collective-permute-start.7
  48.1 11.7 %all-to-all-start = ((s32[16,1,9]{2,1,0:T(1,128)}), s32[16,1,9]{2,1,0:T(1,128)S(1)}, u32[]{:S(2)}, u32[]{:S(2)}) async-start(s32[16,1,9]{2,1,0:T(1,128)} %broadcast_in_dim.134), calls=%async_computation | async-start | bytes 16384 | tf_op jit(solution)/shard_map/all_to_all | solution.py:544
  54.1 625.6 %reduce-scatter.13.cloned.1.call-start = ((), (), s32[]{:S(2)}) async-start(), calls=%async_computation.15 | async-start | bytes 1566720
  54.1 34.3 %collective-permute-start = (bf16[512,1152]{1,0:T(8,128)(2,1)}, bf16[512,1152]{1,0:T(8,128)(2,1)S(1)}, u32[]{:S(2)}, u32[]{:S(2)}) collective-permute-start(bf16[512,1152]{1,0:T(8,128)(2,1)} %param.18), channel_id=1, source_target_pairs={{0,0},{1,2},{2,1},{3,3},{4,4},{5,6},{6,5},{7,7},{8,8},{9,10},{10,9... | collective-permute-start | bytes 3538952 | tf_op jit(solution)/shard_map/ppermute | solution.py:479
  71.0 14.4 %copy-start.59 = (pred[8,2]{0,1:T(4,128)(4,1)}, pred[8,2]{0,1:T(4,128)(4,1)S(1)}, u32[]{:S(2)}) copy-start(pred[8,2]{0,1:T(4,128)(4,1)S(1)} %copy.115) | copy-start | bytes 52
  88.4 165.3 %copy-start.39 = (f32[2,1152]{1,0:T(2,128)}, f32[2,1152]{1,0:T(2,128)S(1)}, u32[]{:S(2)}) copy-start(f32[2,1152]{1,0:T(2,128)S(1)} %get-tuple-element.140) | copy-start | bytes 27652
  88.4 4.8 copy-start.58
  88.6 8.3 copy-start.36
  91.9 7.7 collective-permute-start.1
  221.2 6.9 copy-start.2
  221.2 6.9 copy-start.15
  221.4 6.7 collective-permute-start.4
  223.3 30.4 %collective-permute-start.10 = (bf16[512,1152]{1,0:T(8,128)(2,1)S(1)}, bf16[512,1152]{1,0:T(8,128)(2,1)S(1)}, u32[]{:S(2)}, u32[]{:S(2)}) collective-permute-start(bf16[512,1152]{1,0:T(8,128)(2,1)S(1)} %copy-done.60), channel_id=1, source_target_pairs={{0,0},{1,2},{2,1},{3,3},{4,4},{5,6},{6,5},{7,7},{8,8},{9,10},{10,9... | collective-permute-start | bytes 3538952 | tf_op jit(solution)/shard_map/ppermute | solution.py:479
  231.9 26.0 %collective-permute-start.5 = (bf16[512,1152]{1,0:T(8,128)(2,1)}, bf16[512,1152]{1,0:T(8,128)(2,1)}, u32[]{:S(2)}, u32[]{:S(2)}) collective-permute-start(bf16[512,1152]{1,0:T(8,128)(2,1)} %fusion.19), channel_id=1, source_target_pairs={{0,2},{2,0},{1,3},{3,1},{4,6},{6,4},{5,7},{7,5},{8,10},{10,8},{9,1... | collective-permute-start | bytes 3538952 | tf_op jit(solution)/shard_map/ppermute | solution.py:483
  256.0 13.9 %collective-permute-start.11 = (bf16[512,1152]{1,0:T(8,128)(2,1)}, bf16[512,1152]{1,0:T(8,128)(2,1)}, u32[]{:S(2)}, u32[]{:S(2)}) collective-permute-start(bf16[512,1152]{1,0:T(8,128)(2,1)} %fusion.17), channel_id=1, source_target_pairs={{0,2},{2,0},{1,3},{3,1},{4,6},{6,4},{5,7},{7,5},{8,10},{10,8},{9,1... | collective-permute-start | bytes 3538952 | tf_op jit(solution)/shard_map/ppermute | solution.py:483
  361.5 10.5 %copy-start.61 = (bf16[1024,2304]{1,0:T(8,128)(2,1)}, bf16[1024,2304]{1,0:T(8,128)(2,1)S(1)}, u32[]{:S(2)}) copy-start(bf16[1024,2304]{1,0:T(8,128)(2,1)S(1)} %fusion.6) | copy-start | bytes 14155780
  372.0 6.0 copy-start.13
  372.2 5.9 collective-permute-start.12
  380.2 207.8 %copy-start.46 = (f32[512]{0:T(512)}, f32[512]{0:T(512)S(1)}, u32[]{:S(2)}) copy-start(f32[512]{0:T(512)S(1)} %negate_multiply_fusion.1) | copy-start | bytes 6148
  381.6 2.8 collective-permute-start.13
  388.6 301.3 %reduce-scatter.9.cloned.1.call-start = ((), (), s32[]{:S(2)}) async-start(), calls=%async_computation.13 | async-start | bytes 5640192 | tf_op jit(solution)/shard_map/reduce_scatter | solution.py:500
  399.2 400.9 %reduce-scatter.11.cloned.1.call-start = ((), (), s32[]{:S(2)}) async-start(), calls=%async_computation.14 | async-start | bytes 5640192 | tf_op jit(solution)/shard_map/reduce_scatter | solution.py:500
  410.8 535.4 %reduce-scatter.7.cloned.1.call-start = ((), (), s32[]{:S(2)}) async-start(), calls=%async_computation.12 | async-start | bytes 5640192 | tf_op jit(solution)/shard_map/reduce_scatter | solution.py:500
  547.9 58.8 %collective-permute-start.8 = (f32[512,1152]{1,0:T(8,128)}, f32[512,1152]{1,0:T(8,128)}, u32[]{:S(2)}, u32[]{:S(2)}) collective-permute-start(f32[512,1152]{1,0:T(8,128)} %slice.111), channel_id=1, source_target_pairs={{0,2},{2,0},{1,3},{3,1},{4,6},{6,4},{5,7},{7,5},{8,10},{10,8},{9,1... | collective-permute-start | bytes 7077896 | tf_op jit(solution)/shard_map/ppermute | solution.py:483
  552.5 54.3 %collective-permute-start.14 = (f32[512,1152]{1,0:T(8,128)}, f32[512,1152]{1,0:T(8,128)}, u32[]{:S(2)}, u32[]{:S(2)}) collective-permute-start(f32[512,1152]{1,0:T(8,128)} %slice.85), channel_id=1, source_target_pairs={{0,2},{2,0},{1,3},{3,1},{4,6},{6,4},{5,7},{7,5},{8,10},{10,8},{9,1... | collective-permute-start | bytes 7077896 | tf_op jit(solution)/shard_map/ppermute | solution.py:483
  558.2 28.1 %copy-start.41 = (f32[512]{0:T(512)S(1)}, f32[512]{0:T(512)}, u32[]{:S(2)}) copy-start(f32[512]{0:T(512)} %copy-done.40) | copy-start | bytes 6148
  558.2 28.6 %copy-start.37 = (f32[512]{0:T(512)S(1)}, f32[512]{0:T(512)}, u32[]{:S(2)}) copy-start(f32[512]{0:T(512)} %copy-done.36) | copy-start | bytes 6148
  558.8 47.9 %copy-start.16 = (bf16[512,1152]{1,0:T(8,128)(2,1)S(1)}, bf16[512,1152]{1,0:T(8,128)(2,1)}, u32[]{:S(2)}) copy-start(bf16[512,1152]{1,0:T(8,128)(2,1)} %copy-done.14) | copy-start | bytes 3538948
  567.5 8.1 collective-permute-start.18
  576.7 6.0 collective-permute-start.19
  583.4 12.1 %collective-permute-start.20 = (f32[43,1152]{1,0:T(8,128)}, f32[43,1152]{1,0:T(8,128)}, u32[]{:S(2)}, u32[]{:S(2)}) collective-permute-start(f32[43,1152]{1,0:T(8,128)} %add.256), channel_id=1, source_target_pairs={{0,16},{4,20},{8,24},{12,28},{16,0},{20,4},{24,8},{28,12},{1,17},{... | collective-permute-start | bytes 594440 | tf_op jit(solution)/shard_map/ppermute | solution.py:624
  596.6 8.2 collective-permute-start.21
  605.5 32.6 %collective-permute-start.22 = (f32[43,1152]{1,0:T(8,128)}, f32[43,1152]{1,0:T(8,128)}, u32[]{:S(2)}, u32[]{:S(2)}) collective-permute-start(f32[43,1152]{1,0:T(8,128)} %add.258), channel_id=1, source_target_pairs={{0,2},{2,0},{1,3},{3,1},{4,6},{6,4},{5,7},{7,5},{8,10},{10,8},{9,1... | collective-permute-start | bytes 594440 | tf_op jit(solution)/shard_map/ppermute | solution.py:483
  606.7 9.8 copy-start.35
  620.9 18.3 %all-to-all-start.2 = ((bf16[16,2,432]{2,1,0:T(2,128)(2,1)}), bf16[16,2,432]{2,1,0:T(2,128)(2,1)S(1)}, u32[]{:S(2)}, u32[]{:S(2)}) async-start(bf16[16,2,432]{2,1,0:T(2,128)(2,1)} %copy.122), calls=%async_computation.2 | async-start | bytes 65536 | tf_op jit(solution)/shard_map/all_to_all | solution.py:637
  624.3 13.1 %copy-start.51 = (pred[16]{0:T(512)(128)(4,1)S(1)}, pred[16]{0:T(512)(128)(4,1)}, u32[]{:S(2)}) copy-start(pred[16]{0:T(512)(128)(4,1)} %copy-done.50) | copy-start | bytes 52
  628.8 327.8 %collective-permute-start.15 = (f32[512,1152]{1,0:T(8,128)}, f32[512,1152]{1,0:T(8,128)}, u32[]{:S(2)}, u32[]{:S(2)}) collective-permute-start(f32[512,1152]{1,0:T(8,128)} %add_add_fusion.3), channel_id=1, source_target_pairs={{0,0},{1,2},{2,1},{3,3},{4,4},{5,6},{6,5},{7,7},{8,8},{9,10},{10,9... | collective-permute-start | bytes 7077896 | tf_op jit(solution)/shard_map/ppermute | solution.py:479
  639.2 24.0 %collective-permute-start.16 = (bf16[8,1,4,432]{3,2,0,1:T(4,128)(2,1)S(1)}, bf16[8,1,4,432]{3,2,0,1:T(4,128)(2,1)S(1)}, u32[]{:S(2)}, u32[]{:S(2)}) collective-permute-start(bf16[8,1,4,432]{3,2,0,1:T(4,128)(2,1)S(1)} %reshape.442), channel_id=1, source_target_pairs={{0,1},{1,0},{2,3},{3,2},{4,5},{5,4},{6,7},{7,6},{8,9},{9,8},{10,11... | collective-permute-start | bytes 82952 | tf_op jit(solution)/shard_map/ppermute | solution.py:638
  657.3 6.2 copy-start.52
  660.9 295.7 %collective-permute-start.9 = (bf16[512,1152]{1,0:T(8,128)(2,1)}, bf16[512,1152]{1,0:T(8,128)(2,1)}, u32[]{:S(2)}, u32[]{:S(2)}) collective-permute-start(bf16[512,1152]{1,0:T(8,128)(2,1)} %fusion.16), channel_id=1, source_target_pairs={{0,0},{1,2},{2,1},{3,3},{4,4},{5,6},{6,5},{7,7},{8,8},{9,10},{10,9... | collective-permute-start | bytes 3538952 | tf_op jit(solution)/shard_map/ppermute | solution.py:479
  663.2 22.3 %copy-start.33 = (bf16[8,1,4,432]{3,2,0,1:T(4,128)(2,1)}, bf16[8,1,4,432]{3,2,0,1:T(4,128)(2,1)S(1)}, u32[]{:S(2)}) copy-start(bf16[8,1,4,432]{3,2,0,1:T(4,128)(2,1)S(1)} %collective-permute-done.16) | copy-start | bytes 82948
  663.4 22.1 %copy-start.32 = (f32[16,432]{1,0:T(8,128)}, f32[16,432]{1,0:T(8,128)S(1)}, u32[]{:S(2)}) copy-start(f32[16,432]{1,0:T(8,128)S(1)} %broadcast_in_dim.149) | copy-start | bytes 82948
  666.3 289.7 %all-to-all-start.3 = ((f32[16,4,1152]{2,1,0:T(4,128)}), f32[16,4,1152]{2,1,0:T(4,128)S(1)}, u32[]{:S(2)}, u32[]{:S(2)}) async-start(f32[16,4,1152]{2,1,0:T(4,128)} %copy.126), calls=%async_computation.3 | async-start | bytes 589824 | tf_op jit(solution)/shard_map/all_to_all | solution.py:647
  681.3 266.8 %collective-permute-start.23 = (f32[72,576]{1,0:T(8,128)}, f32[72,576]{1,0:T(8,128)}, u32[]{:S(2)}, u32[]{:S(2)}) collective-permute-start(f32[72,576]{1,0:T(8,128)} %convert_element_type.148), channel_id=1, source_target_pairs={{0,0},{1,2},{2,1},{3,3},{4,4},{5,6},{6,5},{7,7},{8,8},{9,10},{10,9... | collective-permute-start | bytes 497672 | tf_op jit(solution)/shard_map/ppermute | solution.py:479
  686.6 266.9 %copy-start.27 = (bf16[64,1152]{1,0:T(8,128)(2,1)S(1)}, bf16[64,1152]{1,0:T(8,128)(2,1)}, u32[]{:S(2)}) copy-start(bf16[64,1152]{1,0:T(8,128)(2,1)} %gather_fusion.1) | copy-start | bytes 442372
  687.5 266.1 %copy-start.28 = (bf16[64,1152]{1,0:T(8,128)(2,1)S(1)}, bf16[64,1152]{1,0:T(8,128)(2,1)}, u32[]{:S(2)}) copy-start(bf16[64,1152]{1,0:T(8,128)(2,1)} %gather_fusion) | copy-start | bytes 442372
  687.5 266.1 %copy-start.53 = (pred[64]{0:T(512)(128)(4,1)S(1)}, pred[64]{0:T(512)(128)(4,1)}, u32[]{:S(2)}) copy-start(pred[64]{0:T(512)(128)(4,1)} %broadcast_in_dim.158) | copy-start | bytes 196
  687.5 266.1 %copy-start.54 = (pred[64]{0:T(512)(128)(4,1)S(1)}, pred[64]{0:T(512)(128)(4,1)}, u32[]{:S(2)}) copy-start(pred[64]{0:T(512)(128)(4,1)} %broadcast_in_dim.155) | copy-start | bytes 196
  691.8 264.2 %copy-start.43 = (bf16[4,1152]{1,0:T(4,128)(2,1)S(1)}, bf16[4,1152]{1,0:T(4,128)(2,1)}, u32[]{:S(2)}) copy-start(bf16[4,1152]{1,0:T(4,128)(2,1)} %gather_fusion.2) | copy-start | bytes 27652
  691.8 264.2 %copy-start.44 = (bf16[4,1152]{1,0:T(4,128)(2,1)S(1)}, bf16[4,1152]{1,0:T(4,128)(2,1)}, u32[]{:S(2)}) copy-start(bf16[4,1152]{1,0:T(4,128)(2,1)} %gather_fusion.3) | copy-start | bytes 27652
  691.8 264.8 %collective-permute-start.24 = (f32[72,2304]{1,0:T(8,128)}, f32[72,2304]{1,0:T(8,128)}, u32[]{:S(2)}, u32[]{:S(2)}) collective-permute-start(f32[72,2304]{1,0:T(8,128)} %convert_element_type.150), channel_id=1, source_target_pairs={{0,0},{1,2},{2,1},{3,3},{4,4},{5,6},{6,5},{7,7},{8,8},{9,10},{10,9... | collective-permute-start | bytes 1990664 | tf_op jit(solution)/shard_map/ppermute | solution.py:479
  801.9 154.7 %collective-permute-start.25 = (f32[72,2304]{1,0:T(8,128)}, f32[72,2304]{1,0:T(8,128)}, u32[]{:S(2)}, u32[]{:S(2)}) collective-permute-start(f32[72,2304]{1,0:T(8,128)} %convert_element_type.152), channel_id=1, source_target_pairs={{0,0},{1,2},{2,1},{3,3},{4,4},{5,6},{6,5},{7,7},{8,8},{9,10},{10,9... | collective-permute-start | bytes 1990664 | tf_op jit(solution)/shard_map/ppermute | solution.py:479
  948.1 14.1 %collective-permute-start.17 = (f32[72,2304]{1,0:T(8,128)}, f32[72,2304]{1,0:T(8,128)}, u32[]{:S(2)}, u32[]{:S(2)}) collective-permute-start(f32[72,2304]{1,0:T(8,128)} %convert_element_type.143), channel_id=1, source_target_pairs={{0,0},{1,2},{2,1},{3,3},{4,4},{5,6},{6,5},{7,7},{8,8},{9,10},{10,9... | collective-permute-start | bytes 1990664 | tf_op jit(solution)/shard_map/ppermute | solution.py:479
  (35 other events, 61.6 us)
Sparse Core Ops, SparseCore 0:
  19.1 87.4 all-gather.4
  109.3 55.4 all-gather.6
  168.1 89.8 all-gather.8
  261.2 85.6 all-gather.10
  388.7 114.1 reduce-scatter.12
  509.0 142.6 reduce-scatter.8
  657.8 142.1 reduce-scatter.10
  806.2 140.0 reduce-scatter.6

commit v2 on v1

--- a/solution.py
+++ b/solution.py
@@ -14,6 +14,9 @@
 LEVELS=(64,32,16,8,4,2,1)
 GATE_NORM=16.0; head_eps=1e-5
 LOG2E=math.log2(math.e)
+
+def cost(us):
+    return pl.CostEstimate(flops=us*900*10**6, bytes_accessed=10**6, transcendentals=0)
 
 def parts(x, n):
     out=[]
@@ -145,7 +148,7 @@
         r=lax.rsqrt(jnp.sum(cb*cb,axis=1,keepdims=True)*(1.0/HDIM)+head_eps)
         mixed_ref[0,rows,:]=(cb*r*gain*(g/(1.0+jnp.exp(-g)))).astype(bf16)
         return 0
-    lax.fori_loop(0,chunks,step,0)
+    lax.fori_loop(0,chunks,step,0,unroll=4)
 
 def gla_forward(big,qkvg,pre,taps,gain,PS=2,PA=2,adt=f32):
     _,H,total,_=qkvg.shape; chunks=total//CHUNK
@@ -160,7 +163,7 @@
                    jax.ShapeDtypeStruct((H,chunks,CHUNK,CHUNK),adt),jax.ShapeDtypeStruct((H,chunks,LANES,LANES),f32)],
         scratch_shapes=[pltpu.VMEM((total+2*MARGIN,LANES),f32)]*3+[pltpu.VMEM((CHUNK,CHUNK),jnp.int32),pltpu.VMEM((CHUNK,CHUNK),bf16),pltpu.VMEM((LANES,LANES),f32)],
         compiler_params=pltpu.CompilerParams(vmem_limit_bytes=40*2**20,dimension_semantics=("arbitrary",)),
-        name="gla_forward",
+        name="gla_forward", cost_estimate=cost(65),
     )(big,qkvg,qkvg,qkvg,qkvg,pre,taps,gain)
 
 def bwd_kernel(PS,PA,total,big_ref,q_ref,k_ref,v_ref,g_ref,p_ref,comb_ref,a_ref,s_ref,gm_ref,taps_ref,gain_ref,
@@ -256,7 +259,7 @@
         dqk_ref[1,0,rows,:]=(dk+t*q).astype(bf16)
         dqk_ref[2,0,rows,:]=dv.astype(bf16)
         return acc+jnp.sum(dp.reshape(CHUNK//8,8,LANES),axis=0)
-    db=lax.fori_loop(0,chunks,step,jnp.zeros((8,LANES),f32))
+    db=lax.fori_loop(0,chunks,step,jnp.zeros((8,LANES),f32),unroll=4)
     dvec_ref[0,1:2,:]=jnp.sum(db,axis=0,keepdims=True)
 
 def gla_backward(big,qkvg,pre,comb,A,S,gm,taps,gain,PS=2,PA=2):
@@ -273,7 +276,7 @@
                    jax.ShapeDtypeStruct((H,16,LANES),f32),jax.ShapeDtypeStruct((H,8,LANES),f32)],
         scratch_shapes=[pltpu.VMEM((total+2*MARGIN,LANES),f32)]*4+[pltpu.VMEM((total,LANES),f32),pltpu.VMEM((CHUNK,CHUNK),jnp.int32),pltpu.VMEM((2,CHUNK,CHUNK),bf16),pltpu.VMEM((LANES,LANES),f32),pltpu.VMEM((8,LANES),f32)],
         compiler_params=pltpu.CompilerParams(vmem_limit_bytes=48*2**20,dimension_semantics=("arbitrary",)),
-        name="gla_backward",
+        name="gla_backward", cost_estimate=cost(80),
     )(big,qkvg,qkvg,qkvg,qkvg,pre,comb,A,S,gm,taps,gain)
 
 
@@ -314,11 +317,29 @@
     return jnp.concatenate(blocks, axis=1)[:, :total]
 
 
-def project_kernel(H, turn_ref, x_ref, w_ref, down_ref, up_ref, bias_ref, out_ref, pre_ref, lat_ref):
-    x = x_ref[...]
+def first_rows(tiles, width):
+    return pl.BlockSpec((ROWS, width), lambda i, t: (jnp.minimum(i, tiles // 2 - 1), 0))
+
+
+def last_rows(tiles, width):
+    return pl.BlockSpec((ROWS, width), lambda i, t: (jnp.maximum(i - tiles // 2, 0), 0))
+
+
+def put_half(half, value, own_ref, away_ref):
+    @pl.when(pl.program_id(0) < half)
+    def _():
+        own_ref[...] = value.astype(own_ref.dtype)
+
+    @pl.when(pl.program_id(0) >= half)
+    def _():
+        away_ref[...] = value.astype(away_ref.dtype)
+
+
+def project_kernel(H, half, turn_ref, x_ref, y_ref, wa_ref, wb_ref, down_ref, up_ref, bias_ref, out_ref, pre_ref, lat_ref):
+    x = jnp.where(pl.program_id(0) < half, x_ref[...], y_ref[...])
     span = 2 * H * HDIM
     for s in range(2):
-        res = mm(x, w_ref[:, s * span : (s + 1) * span], 1, 0)
+        res = mm(x, (wa_ref, wb_ref)[s][:, :span], 1, 0)
         for i in range(2 * H):
             out_ref[2 * s + i // H, i % H] = head_window(res, i * HDIM)
     latent = mm(x, down_ref[...], 1, 0)
@@ -328,8 +349,8 @@
         pre_ref[h] = pre[:, h * LANES : (h + 1) * LANES]
 
 
-def project(turn, x, w, down, up, bias, H):
-    total, width = x.shape
+def project(turn, x, away, wa, wb, down, up, bias, H):
+    total, width = 2 * x.shape[0], x.shape[1]
     tiles = total // ROWS
 
     def turned(i, t):
@@ -337,11 +358,11 @@
 
     full = lambda a: pl.BlockSpec(a.shape, lambda i, t: (0, 0))
     return pl.pallas_call(
-        functools.partial(project_kernel, H),
+        functools.partial(project_kernel, H, tiles // 2),
         grid_spec=pltpu.PrefetchScalarGridSpec(
             num_scalar_prefetch=1,
             grid=(tiles,),
-            in_specs=[pl.BlockSpec((ROWS, width), lambda i, t: (i, 0)), full(w), full(down), full(up), full(bias)],
+            in_specs=[first_rows(tiles, width), last_rows(tiles, width), full(wa), full(wb), full(down), full(up), full(bias)],
             out_specs=[
                 pl.BlockSpec((4, H, ROWS, LANES), lambda i, t: (0, 0, turned(i, t), 0)),
                 pl.BlockSpec((H, ROWS, LANES), lambda i, t: (0, turned(i, t), 0)),
@@ -354,14 +375,14 @@
             jax.ShapeDtypeStruct((total, LANES), f32),
         ],
         compiler_params=pltpu.CompilerParams(vmem_limit_bytes=56 * 2**20, dimension_semantics=("arbitrary",)),
-        name="project",
-    )(turn, x, w, down, up, bias)
-
-
-def attend_kernel(H, turn_ref, m_ref, w_ref, out_ref, cat_ref):
+        name="project", cost_estimate=cost(15),
+    )(turn, x, away, wa, wb, down, up, bias)
+
+
+def attend_kernel(H, half, turn_ref, m_ref, w_ref, own_ref, away_ref, cat_ref):
     cat = heads_joined([m_ref[h].astype(f32) for h in range(H)]).astype(bf16)
     cat_ref[...] = cat
-    out_ref[...] = mm(cat, w_ref[...], 1, 1)
+    put_half(half, mm(cat, w_ref[...], 1, 1), own_ref, away_ref)
 
 
 def attend(turn, mixed, w):
@@ -369,7 +390,7 @@
     tiles = total // ROWS
     inner = H * HDIM
     return pl.pallas_call(
-        functools.partial(attend_kernel, H),
+        functools.partial(attend_kernel, H, tiles // 2),
         grid_spec=pltpu.PrefetchScalarGridSpec(
             num_scalar_prefetch=1,
             grid=(tiles,),
@@ -377,11 +398,11 @@
                 pl.BlockSpec((H, ROWS, LANES), lambda i, t: (0, lax.rem(i + t[0], tiles), 0)),
                 pl.BlockSpec(w.shape, lambda i, t: (0, 0)),
             ],
-            out_specs=[pl.BlockSpec((ROWS, w.shape[0]), lambda i, t: (i, 0)), pl.BlockSpec((ROWS, inner), lambda i, t: (i, 0))],
+            out_specs=[first_rows(tiles, w.shape[0]), last_rows(tiles, w.shape[0]), pl.BlockSpec((ROWS, inner), lambda i, t: (i, 0))],
         ),
-        out_shape=[jax.ShapeDtypeStruct((total, w.shape[0]), f32), jax.ShapeDtypeStruct((total, inner), bf16)],
+        out_shape=[jax.ShapeDtypeStruct((total // 2, w.shape[0]), f32)] * 2 + [jax.ShapeDtypeStruct((total, inner), bf16)],
         compiler_params=pltpu.CompilerParams(vmem_limit_bytes=40 * 2**20, dimension_semantics=("arbitrary",)),
-        name="attend",
+        name="attend", cost_estimate=cost(4),
     )(turn, mixed, w)
 
 
@@ -405,14 +426,39 @@
         ),
         out_shape=jax.ShapeDtypeStruct((H, total, LANES), f32),
         compiler_params=pltpu.CompilerParams(vmem_limit_bytes=40 * 2**20, dimension_semantics=("arbitrary",)),
-        name="attend_back",
+        name="attend_back", cost_estimate=cost(4),
     )(turn, grad, w)
 
 
-def project_back_kernel(H, turn_ref, d_ref, p_ref, lat_ref, w_ref, down_ref, up_ref, out_ref, cat_ref, glat_ref, dup_ref):
+def join_kernel(H, turn_ref, d_ref, cata_ref, catb_ref):
+    for s in range(2):
+        cat = heads_joined([d_ref[2 * s + i // H, i % H].astype(f32) for i in range(2 * H)])
+        (cata_ref, catb_ref)[s][...] = cat.astype(bf16)
+
+
+def join(turn, d):
+    _, H, total, _ = d.shape
+    tiles = total // ROWS
+    cols = 2 * H * HDIM
+    return pl.pallas_call(
+        functools.partial(join_kernel, H),
+        grid_spec=pltpu.PrefetchScalarGridSpec(
+            num_scalar_prefetch=1,
+            grid=(tiles,),
+            in_specs=[pl.BlockSpec((4, H, ROWS, LANES), lambda i, t: (0, 0, lax.rem(i + t[0], tiles), 0))],
+            out_specs=[pl.BlockSpec((ROWS, cols), lambda i, t: (i, 0))] * 2,
+        ),
+        out_shape=[jax.ShapeDtypeStruct((total, cols), bf16)] * 2,
+        compiler_params=pltpu.CompilerParams(vmem_limit_bytes=40 * 2**20, dimension_semantics=("arbitrary",)),
+        name="join", cost_estimate=cost(8),
+    )(turn, d)
+
+
+def project_back_kernel(H, half, turn_ref, x_ref, cata_ref, catb_ref, p_ref, lat_ref, wa_ref, wb_ref, down_ref, up_ref, own_ref, away_ref, ddown_ref, dup_ref):
     @pl.when(pl.program_id(0) == 0)
     def _():
         dup_ref[...] = jnp.zeros_like(dup_ref)
+        ddown_ref[...] = jnp.zeros_like(ddown_ref)
 
     lat = parts(lat_ref[...], 2)
     glat = jnp.zeros((ROWS, LANES), f32)
@@ -421,62 +467,61 @@
         up = up_ref[:, h * LANES : (h + 1) * LANES]
         glat = glat + (mm(dp[2], up, 1, 1) + mm(dp[1], up, 1, 1) + mm(dp[0], up, 1, 1))
         dup_ref[h] += mm(lat[0], dp[1], 0, 0) + mm(lat[1], dp[0], 0, 0) + mm(lat[0], dp[0], 0, 0)
-    glat_ref[...] = glat
-    span = 2 * H * HDIM
-    acc = sum(mm(p, down_ref[...], 1, 1) for p in parts(glat, 2)[::-1])
-    for s in range(2):
-        cat = heads_joined([d_ref[2 * s + i // H, i % H].astype(f32) for i in range(2 * H)]).astype(bf16)
-        cat_ref[:, s * span : (s + 1) * span] = cat
-        acc = acc + mm(cat, w_ref[:, s * span : (s + 1) * span], 1, 1)
-    out_ref[...] = acc
-
-
-def project_back(turn, d, dpre, latent, w, down, up):
-    _, H, total, _ = d.shape
+    split = parts(glat, 2)[::-1]
+    ddown_ref[...] += sum(mm(x_ref[...], p, 0, 0) for p in split)
+    acc = sum(mm(p, down_ref[...], 1, 1) for p in split)
+    acc = acc + mm(cata_ref[...], wa_ref[:, : cata_ref.shape[1]], 1, 1) + mm(catb_ref[...], wb_ref[:, : catb_ref.shape[1]], 1, 1)
+    put_half(half, acc, own_ref, away_ref)
+
+
+def project_back(turn, x, cat_a, cat_b, dpre, latent, wa, wb, down, up):
+    H, total, _ = dpre.shape
     tiles = total // ROWS
-    width, cols = w.shape
+    width, cols = x.shape[1], cat_a.shape[1]
 
     def turned(i, t):
         return lax.rem(i + t[0], tiles)
 
     full = lambda a: pl.BlockSpec(a.shape, lambda i, t: (0, 0))
     return pl.pallas_call(
-        functools.partial(project_back_kernel, H),
+        functools.partial(project_back_kernel, H, tiles // 2),
         grid_spec=pltpu.PrefetchScalarGridSpec(
             num_scalar_prefetch=1,
             grid=(tiles,),
             in_specs=[
-                pl.BlockSpec((4, H, ROWS, LANES), lambda i, t: (0, 0, turned(i, t), 0)),
+                pl.BlockSpec((ROWS, width), lambda i, t: (i, 0)),
+                pl.BlockSpec((ROWS, cols), lambda i, t: (i, 0)),
+                pl.BlockSpec((ROWS, cols), lambda i, t: (i, 0)),
                 pl.BlockSpec((H, ROWS, LANES), lambda i, t: (0, turned(i, t), 0)),
                 pl.BlockSpec((ROWS, LANES), lambda i, t: (turned(i, t), 0)),
-                full(w), full(down), full(up),
+                full(wa), full(wb), full(down), full(up),
             ],
             out_specs=[
-                pl.BlockSpec((ROWS, width), lambda i, t: (i, 0)),
-                pl.BlockSpec((ROWS, cols), lambda i, t: (i, 0)),
-                pl.BlockSpec((ROWS, LANES), lambda i, t: (i, 0)),
+                first_rows(tiles, width),
+                last_rows(tiles, width),
+                pl.BlockSpec((width, LANES), lambda i, t: (0, 0)),
                 pl.BlockSpec((H, LANES, LANES), lambda i, t: (0, 0, 0)),
             ],
         ),
         out_shape=[
-            jax.ShapeDtypeStruct((total, width), f32),
-            jax.ShapeDtypeStruct((total, cols), bf16),
-            jax.ShapeDtypeStruct((total, LANES), f32),
+            jax.ShapeDtypeStruct((total // 2, width), f32),
+            jax.ShapeDtypeStruct((total // 2, width), f32),
+            jax.ShapeDtypeStruct((width, LANES), f32),
             jax.ShapeDtypeStruct((H, LANES, LANES), f32),
         ],
         compiler_params=pltpu.CompilerParams(vmem_limit_bytes=56 * 2**20, dimension_semantics=("arbitrary",)),
-        name="project_back",
-    )(turn, d, dpre, latent, w, down, up)
+        name="project_back", cost_estimate=cost(2),
+    )(turn, x, cat_a, cat_b, dpre, latent, wa, wb, down, up)
 
 
 NORM_EPS = 1e-06
 FLIP = [(0, 1), (1, 0)]
-EVERY = ("dq", "mp")
 COLUMNS = ("dq", "core")
 
 
 def swap(x):
-    return lax.ppermute(x, ("core", "mp"), [(0, 0), (1, 2), (2, 1), (3, 3)])
+    away = lax.ppermute(x, ("core", "mp"), [(1, 2), (2, 1)])
+    return jnp.where(lax.axis_index("core") == lax.axis_index("mp"), x, away)
 
 
 def other(x):
@@ -492,12 +537,66 @@
     return x[:half] + other(x[half:])
 
 
-def gathered(x):
-    return lax.all_gather(x, EVERY, axis=0, tiled=True)
-
-
-def reduced(x):
-    return lax.psum_scatter(x.astype(bf16), EVERY, scatter_dimension=0, tiled=True).astype(f32)
+def across(x):
+    return lax.ppermute(x, "mp", FLIP)
+
+
+def bits():
+    count = lax.axis_size("dq").bit_length() - 1
+    return [("dq", count - 1 - i) for i in range(count)] + [("mp", 0)]
+
+
+def flipped(x, bit):
+    axis, place = bit
+    return lax.ppermute(x, axis, [(i, i ^ (1 << place)) for i in range(lax.axis_size(axis))])
+
+
+def own_bit(bit):
+    return (lax.axis_index(bit[0]) >> bit[1]) & 1
+
+
+def orders():
+    count = len(bits())
+    far = list(range(count - 2))
+    return far + [count - 1, count - 2], far + [count - 2, count - 1]
+
+
+def spread(x, order, steps):
+    names = bits()
+    for step in steps:
+        place = order[step]
+        away, mine = flipped(x, names[place]), own_bit(names[place])
+        at = sum(h < place for h in order[:step])
+        x = jnp.stack([jnp.where(mine == 0, x, away), jnp.where(mine == 0, away, x)], axis=at)
+    return x.reshape(-1, x.shape[-1]) if len(order) - 1 in steps else x
+
+
+def fold_step(x, order, step):
+    names = bits()
+    if step == 0:
+        x = x.reshape((2,) * len(names) + (-1, x.shape[-1]))
+    left = sorted(order[: len(order) - step])
+    place = order[len(order) - 1 - step]
+    at, mine = left.index(place), own_bit(names[place])
+    send = lax.dynamic_index_in_dim(x, 1 - mine, at, keepdims=False)
+    keep = lax.dynamic_index_in_dim(x, mine, at, keepdims=False)
+    x = keep.astype(f32) + flipped(send, names[place]).astype(f32)
+    return x if len(left) == 1 else x.astype(bf16)
+
+
+def folded_in(x, order, gates):
+    sums = [x]
+    for step in range(1, len(order)):
+        for gate in gates.get(len(order) - step, ()):
+            x = after(x, gate)
+        x = fold_step(x, order, step)
+        sums.append(x)
+    return sums
+
+
+def after(x, *first):
+    marks = sum(f[(0,) * f.ndim].astype(f32) for f in first)
+    return jnp.where(jnp.isnan(marks), jnp.zeros_like(x), x)
 
 
 def modulate(rows, shift, scale):
@@ -533,15 +632,22 @@
     own_slots = rows // slot_rows
     unit_slots = 2 * own_slots
 
-    w_proj = gathered(swap(proj_weight.transpose(1, 0, 2).reshape(-1, 4 * inner)))
+    cut = 2 * inner
+    order_a, order_b = orders()
+    last = len(order_a)
+    w_part = swap(proj_weight.transpose(1, 0, 2).reshape(-1, 4 * inner))
+    w_out = lax.all_gather(swap(out_weight.T), ("dq", "mp"), axis=0, tiled=True)
+    w_a = spread(w_part[:, :cut], order_a, range(1))
+    w_b = spread(w_part[:, cut:], order_b, range(1))
+
+    ids = jnp.concatenate([time_ids, class_ids, image_patches])[None]
+    ids = after(ids, w_part)
+    ids = lax.all_to_all(jnp.broadcast_to(ids, (2 * dq, ids.shape[1])), COLUMNS, split_axis=0, concat_axis=0, tiled=True)
+    ids = after(ids, w_a, w_b)
+    w_a = spread(w_a, order_a, range(1, last - 2))
+    w_b = spread(w_b, order_b, range(1, last - 2))
+
     x = swap(block_input)
-    w_out = gathered(swap(out_weight.T))
-    w_fc1 = gathered(swap(fc1_weight))
-    w_fc2 = gathered(swap(fc2_weight.T))
-    g_rows = swap(out_grad)
-
-    ids = jnp.concatenate([time_ids, class_ids, image_patches])[None]
-    ids = lax.all_to_all(jnp.broadcast_to(ids, (2 * dq, ids.shape[1])), COLUMNS, split_axis=0, concat_axis=0, tiled=True)
     t_all, c_all = ids[:, :unit_slots].reshape(-1), ids[:, unit_slots : 2 * unit_slots].reshape(-1)
     big_all = ids[:, 2 * unit_slots] == 4 * slot_rows
     me = 2 * lax.axis_index("dq") + y
@@ -553,9 +659,28 @@
     columns = columns.reshape(2 * dq, unit_slots, part)
     columns = jnp.where(big_all[:, None, None], columns[:, :1], columns)
     columns = lax.dynamic_index_in_dim(columns.reshape(dq, 2, 2, own_slots, part), y, 1, keepdims=False)
-    columns = lax.all_to_all(columns.reshape(2 * dq, own_slots, part), COLUMNS, split_axis=0, concat_axis=0, tiled=True)
-    modulation = columns.transpose(1, 0, 2).reshape(own_slots, 6 * width)
+    columns = after(columns.reshape(2 * dq, own_slots, part), w_a, w_b)
+    received = lax.all_to_all(columns, COLUMNS, split_axis=0, concat_axis=0, tiled=True)
+    modulation = received.transpose(1, 0, 2).reshape(own_slots, 6 * width)
     shift1, scale1, gate1, shift2, scale2, gate2 = jnp.split(modulation, 6, axis=1)
+    residual = x.astype(f32).reshape(own_slots, slot_rows, width)
+    hidden, norm_back_one = jax.vjp(modulate, residual, shift1, scale1)
+    hidden = hidden.reshape(rows, width).astype(bf16)
+    hidden_away = other(hidden)
+    hidden_all = jnp.concatenate([hidden, hidden_away], axis=0)
+
+    away = lax.ppermute(out_grad, "mp", FLIP)
+    straight = core == y
+    g_rows = jnp.where(straight, out_grad, other(away))
+    g_away = jnp.where(straight, other(out_grad), away)
+    w_a = spread(after(w_a, x, away), order_a, range(last - 2, last - 1))
+    w_b = spread(after(w_b, x, away), order_b, range(last - 2, last - 1))
+    w_a = spread(after(w_a, received), order_a, range(last - 1, last))
+    w_b = spread(after(w_b, received), order_b, range(last - 1, last))
+    hidden_units = fc1_weight.shape[1]
+    w_rest = jnp.concatenate([fc1_weight, fc2_weight.T], axis=1)
+    w_rest = lax.all_gather(after(w_rest, w_a, w_b), COLUMNS, axis=0, tiled=True)
+    w_fc1, w_fc2 = w_rest[:, :hidden_units], w_rest[:, hidden_units:]
 
     start = core * inner
     up_local = lax.dynamic_slice_in_dim(decay_up, start, inner, 1)
@@ -569,47 +694,80 @@
     gain_pad = jnp.pad(head_gain.astype(f32), (0, LANES - HDIM))[None]
     turn = (core * (rows // ROWS)).astype(jnp.int32)[None]
 
-    residual = x.astype(f32).reshape(own_slots, slot_rows, width)
-    hidden, norm_back_one = jax.vjp(modulate, residual, shift1, scale1)
-    hidden_all = both(hidden.reshape(rows, width).astype(bf16))
-    qkvg, pre, latent = project(turn, hidden_all, w_proj, down_pad, up_pad, bias_pad, heads)
+    grad_rows = g_rows.astype(f32).reshape(own_slots, slot_rows, width)
+    grad_feed = (grad_rows * gate2[:, None, :]).astype(bf16).reshape(rows, width)
+    gate2_away = across(gate2)
+    grad_feed_away = g_away.astype(f32).reshape(own_slots, slot_rows, width) * gate2_away[:, None, :]
+    grad_feed_away = grad_feed_away.astype(bf16).reshape(rows, width)
+    qkvg, pre, latent = project(turn, hidden, hidden_away, w_a, w_b, down_pad, up_pad, bias_pad, heads)
     mixed, comb, scores, states = gla_forward(patches, qkvg, pre, taps_pad, gain_pad)
-    attn_part, mixed_cat = attend(turn, mixed, w_out)
-    attention = summed(attn_part).reshape(own_slots, slot_rows, width)
+    attn_own, attn_away, mixed_cat = attend(turn, mixed, w_out)
+    attention = (attn_own + other(attn_away)).reshape(own_slots, slot_rows, width)
     after_attn = residual + gate1[:, None, :] * attention
     hidden_two, norm_back_two = jax.vjp(modulate, after_attn, shift2, scale2)
-    hidden_two_all = both(hidden_two.reshape(rows, width).astype(bf16))
-    up_proj = jnp.dot(hidden_two_all, w_fc1, preferred_element_type=f32)
-    active, gelu_back = jax.vjp(functools.partial(jax.nn.gelu, approximate=True), up_proj)
-    active_low = active.astype(bf16)
-    feed_out = summed(contract(active_low, w_fc2, 1, 1)).reshape(own_slots, slot_rows, width)
-    result = after_attn + gate2[:, None, :] * feed_out
-    block_out = swap(result.reshape(rows, width).astype(bf16))
-
-    grad_rows = g_rows.astype(f32).reshape(own_slots, slot_rows, width)
-    grad_gate_two = jnp.sum(grad_rows * feed_out, axis=1)
-    grad_feed_all = both((grad_rows * gate2[:, None, :]).astype(bf16).reshape(rows, width))
-    grad_active = jnp.dot(grad_feed_all, w_fc2, preferred_element_type=f32)
-    grad_fc2 = reduced(contract(grad_feed_all, active_low, 0, 0))
-    grad_up = gelu_back(grad_active)[0].astype(bf16)
-    grad_fc1 = reduced(contract(hidden_two_all, grad_up, 0, 0))
-    grad_hidden_two = summed(contract(grad_up, w_fc1, 1, 1))
+    hidden_two = hidden_two.reshape(rows, width).astype(bf16)
+    hidden_two_away = across(hidden_two)
+
+    def feed(h, g):
+        active, back = jax.vjp(functools.partial(jax.nn.gelu, approximate=True), jnp.dot(h, w_fc1, preferred_element_type=f32))
+        return active.astype(bf16), back(jnp.dot(g, w_fc2, preferred_element_type=f32))[0].astype(bf16)
+
+    active, grad_up = feed(hidden_two, grad_feed)
+    feed_own = contract(active, w_fc2, 1, 1)
+    grad_hidden_two_own = contract(grad_up, w_fc1, 1, 1)
+    hidden_two_away = after(hidden_two_away, feed_own, grad_hidden_two_own)
+    active_away, grad_up_away = feed(hidden_two_away, grad_feed_away)
+    grad_hidden_two_part = contract(grad_up_away, w_fc1, 1, 1).astype(bf16)
+    grad_hidden_two = across(grad_hidden_two_part)
+    grad_feed_all = jnp.concatenate([grad_feed, grad_feed_away], axis=0)
+    hidden_two_all = jnp.concatenate([hidden_two, hidden_two_away], axis=0)
+    active_all = jnp.concatenate([active, active_away], axis=0)
+    grad_up_all = jnp.concatenate([grad_up, grad_up_away], axis=0)
+    feed_away = across(after(contract(active_away, w_fc2, 1, 1).astype(bf16), grad_hidden_two_part))
+    grad_fc2 = contract(grad_feed_all, active_all, 0, 0).astype(bf16)
+    fc2_grad = lax.psum_scatter(grad_fc2, COLUMNS, scatter_dimension=0, tiled=True).astype(f32).T
+    grad_fc1 = contract(hidden_two_all, grad_up_all, 0, 0).astype(bf16)
+    fc1_grad = lax.psum_scatter(grad_fc1, COLUMNS, scatter_dimension=0, tiled=True).astype(f32)
+    grad_hidden_two = grad_hidden_two_own + after(grad_hidden_two, grad_fc1).astype(f32)
+
     grad_after, grad_shift_two, grad_scale_two = norm_back_two(grad_hidden_two.reshape(own_slots, slot_rows, width))
     grad_after = grad_after + grad_rows
     grad_gate_one = jnp.sum(grad_after * attention, axis=1)
     grad_attn_all = both((grad_after * gate1[:, None, :]).astype(bf16).reshape(rows, width))
     grad_mixed = attend_back(turn, grad_attn_all, w_out, heads)
-    grad_out = reduced(contract(grad_attn_all, mixed_cat, 0, 0))
-    d_qkvg, d_pre, d_taps, d_vec = gla_backward(patches, qkvg, pre, comb, scores, states, grad_mixed, taps_pad, gain_pad)
-    hidden_part, d_cat, grad_latent, d_up = project_back(turn, d_qkvg, d_pre, latent, w_proj, down_pad, up_pad)
-    grad_proj = reduced(contract(hidden_all, d_cat, 0, 0))
-    grad_residual, grad_shift_one, grad_scale_one = norm_back_one(summed(hidden_part).reshape(own_slots, slot_rows, width))
-    input_grad = swap((grad_residual + grad_after).reshape(rows, width))
-
-    lat_hi = grad_latent[:, :lowrank].astype(bf16)
-    lat_lo = (grad_latent[:, :lowrank] - lat_hi.astype(f32)).astype(bf16)
-    d_down = contract(hidden_all, jnp.concatenate([lat_hi, lat_lo], axis=1), 0, 0)
-    d_down = d_down[:, :lowrank] + d_down[:, lowrank:]
+    grad_out = contract(grad_attn_all, mixed_cat, 0, 0).astype(bf16)
+    out_step = fold_step(grad_out, order_a, 0)
+    d_qkvg, d_pre, d_taps, d_vec = gla_backward(
+        after(patches, grad_out), qkvg, pre, comb, scores, states, grad_mixed, taps_pad, gain_pad
+    )
+    feed_out = feed_own + after(feed_away, d_qkvg).astype(f32)
+    feed_out = feed_out.reshape(own_slots, slot_rows, width)
+    block_out = (after_attn + gate2[:, None, :] * feed_out).reshape(rows, width).astype(bf16)
+    grad_gate_two = jnp.sum(grad_rows * feed_out, axis=1)
+    cat_a, cat_b = join(after(turn, out_step), d_qkvg)
+    part_b = contract(hidden_all, cat_b, 0, 0).astype(bf16)
+    part_a = contract(hidden_all, cat_a, 0, 0).astype(bf16)
+    b_step = fold_step(part_b, order_b, 0)
+    a_step = fold_step(part_a, order_a, 0)
+    hidden_own, hidden_far, d_down, d_up = project_back(
+        after(turn, part_a, part_b), hidden_all, cat_a, cat_b, d_pre, latent, w_a, w_b, down_pad, up_pad
+    )
+    hidden_sum = (hidden_own + other(hidden_far)).reshape(own_slots, slot_rows, width)
+    grad_residual, grad_shift_one, grad_scale_one = norm_back_one(hidden_sum)
+    grad_mod = jnp.concatenate(
+        [grad_shift_one, grad_scale_one, grad_gate_one, grad_shift_two, grad_scale_two, grad_gate_two], axis=1
+    ).astype(bf16)
+    grad_mod = grad_mod.reshape(own_slots, 2 * dq, part).transpose(1, 0, 2)
+    got = lax.all_to_all(grad_mod, COLUMNS, split_axis=0, concat_axis=0, tiled=True).reshape(dq, 1, unit_slots, part)
+    gates = {2: (grad_mod,), 1: (got,)}
+    sums_b = folded_in(b_step, order_b, gates)
+    sums_a = folded_in(a_step, order_a, gates)
+    sums_out = folded_in(out_step, order_a, {len(order_a) - 1: (sums_b[0],), len(order_a) - 2: (sums_b[1],)})
+    block_out = swap(after(block_out, sums_b[0]))
+    grad_back = swap(jnp.concatenate([sums_a[-1], sums_b[-1], sums_out[-1]], axis=1))
+    input_grad = swap(after(after((grad_residual + grad_after).reshape(rows, width), sums_a[1]), sums_b[1]))
+
+    d_down = d_down[:, :lowrank]
 
     def placed(value):
         return lax.dynamic_update_slice_in_dim(jnp.zeros((value.shape[0], width), f32), value, start, 1)
@@ -620,21 +778,16 @@
     d_gain = jnp.sum(d_vec[:, 0, :HDIM], axis=0)
     stacked = placed(jnp.concatenate([d_up, d_taps, d_bias], axis=0))
     flat = jnp.concatenate([d_down.reshape(lowrank, width), stacked, jnp.pad(d_gain, (0, width - HDIM))[None]], axis=0)
-    for bit in range(dq.bit_length() - 1):
-        flat = flat + lax.ppermute(flat, "dq", [(i, i ^ (1 << bit)) for i in range(dq)])
-    flat = flat + lax.ppermute(flat, "mp", FLIP)
     flat = flat + other(flat)
+    for step, bit in enumerate(bits()):
+        flat = after(flat, (sums_a, sums_b)[step % 2][step // 2])
+        flat = flat + flipped(flat, bit)
     down_sum = flat[:lowrank].reshape(width, lowrank)
     up_sum = flat[lowrank : 2 * lowrank]
     taps_sum = flat[2 * lowrank : 2 * lowrank + 9]
     bias_sum = flat[2 * lowrank + 9]
     gain_sum = flat[2 * lowrank + 10, :HDIM]
 
-    grad_mod = jnp.concatenate(
-        [grad_shift_one, grad_scale_one, grad_gate_one, grad_shift_two, grad_scale_two, grad_gate_two], axis=1
-    ).astype(bf16)
-    grad_mod = grad_mod.reshape(own_slots, 2 * dq, part).transpose(1, 0, 2)
-    got = lax.all_to_all(grad_mod, COLUMNS, split_axis=0, concat_axis=0, tiled=True).reshape(dq, 1, unit_slots, part)
     away = lax.ppermute(got, "mp", FLIP)
     got = jnp.where(y == 0, jnp.concatenate([got, away], axis=1), jnp.concatenate([away, got], axis=1))
     got = got.reshape(2 * dq, unit_slots, part).astype(f32)
@@ -646,14 +799,14 @@
     grad_silu = jnp.dot(got, ada_weight.astype(f32).T, precision=lax.Precision.HIGHEST, preferred_element_type=f32)
     grad_silu = lax.all_to_all(grad_silu, COLUMNS, split_axis=0, concat_axis=0, tiled=True)
     grad_silu = jnp.sum(grad_silu.reshape(2 * dq, unit_slots, width), axis=0)
-    own_cond = time_table[time_ids].astype(f32) + class_table[class_ids].astype(f32)
+    own_cond = lax.dynamic_slice_in_dim(condition, (2 * lax.axis_index("dq") + core) * unit_slots, unit_slots, 0)
     gate = jax.nn.sigmoid(own_cond)
     cond_grad = grad_silu * (gate * (1.0 + own_cond * (1.0 - gate)))
 
-    proj_grad = swap(grad_proj).reshape(-1, 4, inner).transpose(1, 0, 2)
+    proj_grad = grad_back[:, : 4 * inner].reshape(-1, 4, inner).transpose(1, 0, 2)
     return (
         block_out, input_grad, cond_grad, ada_weight_grad, ada_bias_grad, proj_grad, down_sum, up_sum, bias_sum,
-        gain_sum, taps_sum, swap(grad_out).T, swap(grad_fc1), swap(grad_fc2).T,
+        gain_sum, taps_sum, grad_back[:, 4 * inner :].T, fc1_grad, fc2_grad,
     )
 
 

time: 997 us -> 727 us (0.73)
  waiting for transfers between devices: 407 us -> 139 us
  other arithmetic: 56.7 us -> 90.1 us
  between operations: 16.1 us -> 42.6 us
  Pallas kernels: 211 us -> 189 us
  matrix products: 93.9 us -> 78.1 us
  starting transfers between devices: 98.2 us -> 82.8 us
  blocking collectives: 10.4 us -> 0 us
    reduce_scatter x3 -> x2, waiting for transfers between devices: 244 us -> 0.01 us  [the longest x1 0.01 us: on_device(): lax.psum_scatter(grad_fc1, COLUMNS, scatter_dimension=0, tiled=True)]
    all_gather x4 -> x2, waiting for transfers between devices: 82.9 us -> 18.5 us  [the longest x1 18.5 us: on_device(): lax.all_gather(after(w_rest, w_a, w_b), COLUMNS, axis=0, tiled=True)]
    ppermute x16 -> x35, waiting for transfers between devices: 69.6 us -> 110 us  [the longest x24 68 us: flipped(): lax.ppermute(x, axis, [(i, i ^ 1 << place) for i in range(lax.axis_size(a...]
    select_n x2 -> x26, other arithmetic: 1.62 us -> 32.7 us  [the longest x21 24.7 us: after(): return jnp.where(jnp.isnan(marks), jnp.zeros_like(x), x)]
    pallas_call x1, Pallas kernels: 86.7 us -> 65.1 us  [gla_forward(): pl.pallas_call(functools.partial(fwd_kernel, PS, PA, total), grid=(H,), i...]
    ppermute x1, starting transfers between devices: 17.4 us -> 1.8 us  [on_device(): away = lax.ppermute(got, 'mp', FLIP)]
    dot_general x7 -> x9, matrix products: 60.9 us -> 48.3 us  [contract(): lax.dot_general(a, b, (((i,), (j,)), ((), ())), preferred_element_type=f32)]
    slice x4 -> x27, local copies, waits for them, and re-layouts: 5.44 us -> 17.4 us  [the longest x25 16.5 us: after(): marks = sum((f[(0,) * f.ndim].astype(f32) for f in first))]
  transfers between devices with their start and end apart: 37 -> 51, of which waited for: 18 -> 16; matrix products, arithmetic and copies ran while one was open for 17% -> 30% of each run, Pallas kernels for 21% -> 26%
where the time goes in v2:
time: 727 us; the launch traced here: 718 us
  Pallas kernels  189 us (26%)
  waiting for transfers between devices  139 us (19%)
  local copies, waits for them, and re-layouts  96.1 us (13%)
  other arithmetic  90.1 us (12%)
  starting transfers between devices  82.8 us (11%)
  matrix products  78.1 us (11%)
  between operations  42.6 us (6%)
    pallas_call x1, Pallas kernels, gla_backward(): pl.pallas_call(functools.partial(bwd_kernel, PS, PA, total), grid=(H,), i...  77.3 us
    ppermute x24, waiting for transfers between devices, flipped(): lax.ppermute(x, axis, [(i, i ^ 1 << place) for i in range(lax.axis_size(a...  68 us
    pallas_call x1, Pallas kernels, gla_forward(): pl.pallas_call(functools.partial(fwd_kernel, PS, PA, total), grid=(H,), i...  65.1 us
    dot_general x9, matrix products, contract(): lax.dot_general(a, b, (((i,), (j,)), ((), ())), preferred_element_type=f32)  48.3 us
    ppermute x6, waiting for transfers between devices, swap(): away = lax.ppermute(x, ('core', 'mp'), [(1, 2), (2, 1)])  31.7 us
    unnamed x236, local copies, waits for them, and re-layouts  30.4 us
    ppermute x6, starting transfers between devices, swap(): away = lax.ppermute(x, ('core', 'mp'), [(1, 2), (2, 1)])  28.7 us
    select_n x21, other arithmetic, after(): return jnp.where(jnp.isnan(marks), jnp.zeros_like(x), x)  24.7 us
  transfers between devices with their start and end apart: 51, of which 16 were waited for; matrix products, arithmetic and copies ran while one was open for 30% of the time, Pallas kernels for 26%

profile of v2, /device:TPU:1, one launch (start us, length us, event | category | flops | bytes accessed | tf_op | source)
XLA Modules:
  0.0 718.2 jit_solution(8424321359836104391)
XLA Ops:
  8.8 4.5 collective-permute-start.1
  13.4 5.1 collective-permute-done.1
  18.5 2.1 collective-permute-start.4
  20.6 3.9 collective-permute-start
  27.8 4.2 all-to-all-start
  32.7 2.3 collective-permute-start.2
  36.9 6.2 collective-permute-done.2
  46.0 2.8 gather_fusion
  52.2 7.7 %collective-permute-done.3 = bf16[2,72,1152]{2,1,0:T(8,128)(2,1)S(1)} collective-permute-done((bf16[2,72,1152]{2,1,0:T(8,128)(2,1)S(1)}, bf16[2,72,1152]{2,1,0:T(8,128)(2,1)S(1)}, u32[]{:S(2)}, u32[]{:S(2)}) %collective-permute-start.3) | collective-permute-done | bytes 331808 | tf_op jit(solution)/shard_map/ppermute | solution.py:551
  72.8 6.2 all-to-all-start.1
  79.0 6.0 all-to-all-done.1
  91.8 11.8 %collective-permute-done.11 = bf16[2,2,72,1152]{3,2,0,1:T(8,128)(2,1)} collective-permute-done((bf16[2,2,72,1152]{3,2,0,1:T(8,128)(2,1)}, bf16[2,2,72,1152]{3,2,0,1:T(8,128)(2,1)}, u32[]{:S(2)}, u32[]{:S(2)}) %collective-permute-start.11) | collective-permute-done | bytes 663584 | tf_op jit(solution)/shard_map/ppermute | solution.py:551
  107.3 6.6 collective-permute-start.13
  113.8 25.2 %collective-permute-done.13 = bf16[72,576]{1,0:T(8,128)(2,1)S(1)} collective-permute-done((bf16[72,576]{1,0:T(8,128)(2,1)S(1)}, bf16[72,576]{1,0:T(8,128)(2,1)S(1)}, u32[]{:S(2)}, u32[]{:S(2)}) %collective-permute-start.13) | collective-permute-done | bytes 82976 | tf_op jit(solution)/shard_map/ppermute | solution.py:523
  160.5 15.7 %project.1 = (f32[4,8,1024,128]{3,2,1,0:T(8,128)}, f32[8,1024,128]{2,1,0:T(8,128)}, f32[1024,128]{1,0:T(8,128)}) custom-call(s32[1]{0:T(128)} %bitcast.35.turn_ref, bf16[512,1152]{1,0:T(8,128)(2,1)} %copy-done.35, bf16[512,1152]{1,0:T(8,128)(2,1)} %copy-done.60, bf16[1152,1152]{1,0:T(8,128)(2,1)} %bitcast.257, bf16[1152,1152]{1,0:T(8,128)(2,1)} %bitcast.260, ...), custom_call_target="tpu_custom_call" | custom-call | flops 13500000256 | bytes 1000000 | tf_op jit(solution)/shard_map/project/pallas_call | solution.py:360
  176.3 65.1 %gla_forward.1 = (bf16[8,1024,128]{2,1,0:T(8,128)(2,1)S(1)}, f32[8,1024,128]{2,1,0:T(8,128)S(1)}, f32[8,8,128,128]{3,2,1,0:T(8,128)S(1)}, f32[8,8,128,128]{3,2,1,0:T(8,128)}) custom-call(s32[1]{0:T(128)} %bitcast.36.big_ref, f32[4,8,1024,128]{3,2,1,0:T(8,128)} %get-tuple-element.34.q_ref.k_ref.v_ref.g_ref, ...), custom_call_target="tpu_custom_call" | custom-call | flops 58500001792 | bytes 1000000 | tf_op jit(solution)/shard_map/gla_forward/pallas_call | solution.py:157
  241.4 2.0 copy-done.9
  246.8 3.7 attend.1
  251.5 2.9 collective-permute-done.17
  254.4 4.3 collective-permute-done.16
  258.8 2.7 fusion.72
  267.2 18.5 %all-gather.3.cloned.1.call-done = bf16[1152,4608]{1,0:T(8,128)(2,1)} async-done(((bf16[72,4608]{1,0:T(8,128)(2,1)}), bf16[1152,4608]{1,0:T(8,128)(2,1)}) %all-gather.3.cloned.1.call-update) | async-done | bytes 10616848 | tf_op jit(solution)/shard_map/all_gather | solution.py:682
  285.8 6.8 multiply_convert_fusion.1
  292.6 6.0 fusion.6
  298.6 3.2 fusion.32
  302.4 3.2 fusion.24
  309.0 5.2 multiply_convert_fusion
  314.2 5.7 fusion.13
  321.4 8.8 %convolution_convert_fusion.1 = bf16[1152,2304]{1,0:T(8,128)(2,1)} fusion(bf16[512,2304]{1,0:T(8,128)(2,1)S(1)} %fusion.13, bf16[512,2304]{1,0:T(8,128)(2,1)S(1)} %fusion.6, bf16[512,1152]{1,0:T(8,128)(2,1)S(1)} %broadcast_select_fusion, bf16[512,1152]{1,0:T(8,128)(2,1)} %fusion.63), kind=kOutput, calls=%fused_computation.3 | convolution fusion | flops 5452627968 | bytes 12386304 | tf_op jit(solution)/shard_map/dot_general | solution.py:614
  331.5 7.8 %fusion.43 = bf16[512,1152]{1,0:T(8,128)(2,1)} fusion(bf16[512,2304]{1,0:T(8,128)(2,1)} %copy-done.113, bf16[1152,4608]{1,0:T(8,128)(2,1)} %all-gather.3.cloned.1.call-done), kind=kOutput, calls=%fused_computation.61 | convolution fusion | flops 2718498816 | bytes 8847360 | tf_op jit(solution)/shard_map/dot_general | solution.py:614
  343.1 3.4 pad_maximum_fusion.2.x_ref
  352.0 7.6 %fusion.46 = bf16[512,1152]{1,0:T(8,128)(2,1)} fusion(bf16[512,2304]{1,0:T(8,128)(2,1)} %get-tuple-element.173, bf16[1152,4608]{1,0:T(8,128)(2,1)} %all-gather.3.cloned.1.call-done, pred[]{:T(512)} %bitcast.57), kind=kOutput, calls=%fused_computation.62 | convolution fusion | flops 2719088640 | bytes 8847872 | tf_op jit(solution)/shard_map/dot_general | solution.py:614
  360.0 6.9 collective-permute-done.18
  374.2 7.7 %convolution_convert_fusion = bf16[1152,2304]{1,0:T(8,128)(2,1)} fusion(bf16[512,2304]{1,0:T(8,128)(2,1)S(1)} %copy-done.112, bf16[512,2304]{1,0:T(8,128)(2,1)S(1)} %copy-done.111, bf16[512,1152]{1,0:T(8,128)(2,1)S(1)} %copy-done.63, bf16[512,1152]{1,0:T(8,128)(2,1)S(1)} %copy-done.65), kind=kOutput, calls=%fused_computation.2 | convolution fusion | flops 5452627968 | bytes 12386304 | tf_op jit(solution)/shard_map/dot_general | solution.py:614
  384.2 3.4 convolution_convert_fusion.4
  391.4 2.1 pad_maximum_fusion.3.g_ref
  393.7 3.8 attend_back.1.gm_ref
  399.5 77.3 %gla_backward.1 = (bf16[4,8,1024,128]{3,2,1,0:T(8,128)(2,1)}, f32[8,1024,128]{2,1,0:T(8,128)S(1)}, f32[8,16,128]{2,1,0:T(8,128)S(1)}, f32[8,8,128]{2,1,0:T(8,128)S(1)}) custom-call(s32[1]{0:T(128)S(6)} %select_n.512.big_ref, f32[4,8,1024,128]{3,2,1,0:T(8,128)} %get-tuple-element.34.q_ref.k_ref.v_ref.g_ref, ...), custom_call_target="tpu_custom_call" | custom-call | flops 71999995904 | bytes 1000000 | tf_op jit(solution)/shard_map/gla_backward/pallas_call | solution.py:269
  484.1 3.5 copy-done.7
  487.6 3.8 join.1
  491.4 3.3 convolution_convert_fusion.3
  497.6 3.3 convolution_convert_fusion.2
  504.2 19.7 %project_back.1 = (f32[512,1152]{1,0:T(8,128)}, f32[512,1152]{1,0:T(8,128)}, f32[1152,128]{1,0:T(8,128)}, f32[8,128,128]{2,1,0:T(8,128)}) custom-call(s32[1]{0:T(128)S(6)} %select_n.525.turn_ref, bf16[1024,1152]{1,0:T(8,128)(2,1)} %pad_maximum_fusion.2.x_ref, bf16[1024,1152]{1,0:T(8,128)(2,1)} %copy-done.3, bf16[1024,1152]{1,0:T(8,128)(2,1)} %copy-done.4, ...), custom_call_target="tpu_custom_call" | custom-call | flops 1800000000 | bytes 1000000 | tf_op jit(solution)/shard_map/project_back/pallas_call | solution.py:486
  534.5 2.3 collective-permute-start.38
  543.5 3.1 fusion.76
  546.6 12.2 %collective-permute-done.25 = bf16[2,2,2,72,1152]{4,3,0,1,2:T(8,128)(2,1)} collective-permute-done((bf16[2,2,2,72,1152]{4,3,0,1,2:T(8,128)(2,1)}, bf16[2,2,2,72,1152]{4,3,0,1,2:T(8,128)(2,1)}, u32[]{:S(2)}, u32[]{:S(2)}) %collective-permute-start.25) | collective-permute-done | bytes 1327136 | tf_op jit(solution)/shard_map/ppermute | solution.py:551
  558.7 7.4 %collective-permute-start.23 = (bf16[512,1152]{1,0:T(8,128)(2,1)}, bf16[512,1152]{1,0:T(8,128)(2,1)}, u32[]{:S(2)}, u32[]{:S(2)}) collective-permute-start(bf16[512,1152]{1,0:T(8,128)(2,1)} %fusion.76), channel_id=1, source_target_pairs={{1,2},{2,1},{5,6},{6,5},{9,10},{10,9},{13,14},{14,13},{17,18},{18,... | collective-permute-start | bytes 3538952 | tf_op jit(solution)/shard_map/ppermute | solution.py:523
  572.4 10.6 %collective-permute-done.39 = f32[43,1152]{1,0:T(8,128)S(1)} collective-permute-done((f32[43,1152]{1,0:T(8,128)S(1)}, f32[43,1152]{1,0:T(8,128)S(1)}, u32[]{:S(2)}, u32[]{:S(2)}) %collective-permute-start.39) | collective-permute-done | bytes 198176 | tf_op jit(solution)/shard_map/ppermute | solution.py:551
  583.9 4.7 fusion.71
  598.3 2.1 fusion.103
  601.8 2.2 broadcast_select_fusion.7
  605.8 2.2 broadcast_select_fusion.6
  609.8 4.8 all-to-all-start.2
  623.0 3.5 select_select_fusion
  639.4 5.7 all-to-all-start.3
  645.8 2.3 fusion.87
  648.2 2.1 collective-permute-start.28
  650.2 2.4 broadcast_select_fusion.2
  653.7 2.4 collective-permute-start.36
  659.8 2.3 collective-permute-start.31
  662.4 18.3 %collective-permute-done.42 = f32[43,1152]{1,0:T(8,128)S(1)} collective-permute-done((f32[43,1152]{1,0:T(8,128)S(1)}, f32[43,1152]{1,0:T(8,128)S(1)}, u32[]{:S(2)}, u32[]{:S(2)}) %collective-permute-start.42) | collective-permute-done | bytes 198176 | tf_op jit(solution)/shard_map/ppermute | solution.py:551
  681.9 4.2 collective-permute-start.37
  699.0 2.6 reshape.570
  704.3 3.5 broadcast_select_fusion.1
  (509 shorter events, 172.6 us)
Async XLA Ops:
  7.2 38.1 %copy-start = (bf16[1001,1152]{1,0:T(8,128)(2,1)S(1)}, bf16[1001,1152]{1,0:T(8,128)(2,1)}, u32[]{:S(2)}) copy-start(bf16[1001,1152]{1,0:T(8,128)(2,1)} %param.21) | copy-start | bytes 6918916
  7.2 18.1 %copy-start.102 = (bf16[432]{0:T(512)(128)(2,1)S(1)}, bf16[432]{0:T(512)(128)(2,1)}, u32[]{:S(2)}) copy-start(bf16[432]{0:T(512)(128)(2,1)} %param.26) | copy-start | bytes 2596
  7.2 19.9 %copy-start.107 = (s32[4]{0:T(128)S(1)}, s32[4]{0:T(128)}, u32[]{:S(2)}) copy-start(s32[4]{0:T(128)} %param.23) | copy-start | bytes 52
  7.2 19.9 %copy-start.108 = (s32[4]{0:T(128)S(1)}, s32[4]{0:T(128)}, u32[]{:S(2)}) copy-start(s32[4]{0:T(128)} %param.22) | copy-start | bytes 52
  8.8 9.6 %collective-permute-start.1 = (bf16[72,2304]{1,0:T(8,128)(2,1)S(1)}, bf16[72,2304]{1,0:T(8,128)(2,1)S(1)}, u32[]{:S(2)}, u32[]{:S(2)}) collective-permute-start(bf16[72,2304]{1,0:T(8,128)(2,1)S(1)} %reshape.546), channel_id=1, source_target_pairs={{1,2},{2,1},{5,6},{6,5},{9,10},{10,9},{13,14},{14,13},{17,18},{18,... | collective-permute-start | bytes 995336 | tf_op jit(solution)/shard_map/ppermute | solution.py:523
  18.5 13.5 %collective-permute-start.4 = (bf16[72,1152]{1,0:T(8,128)(2,1)S(1)}, bf16[72,1152]{1,0:T(8,128)(2,1)S(1)}, u32[]{:S(2)}, u32[]{:S(2)}) collective-permute-start(bf16[72,1152]{1,0:T(8,128)(2,1)S(1)} %slice.197), channel_id=1, source_target_pairs={{0,16},{4,20},{8,24},{12,28},{16,0},{20,4},{24,8},{28,12},{1,17},{... | collective-permute-start | bytes 497672 | tf_op jit(solution)/shard_map/ppermute | solution.py:551
  20.6 39.4 %collective-permute-start = (bf16[512,1152]{1,0:T(8,128)(2,1)}, bf16[512,1152]{1,0:T(8,128)(2,1)}, u32[]{:S(2)}, u32[]{:S(2)}) collective-permute-start(bf16[512,1152]{1,0:T(8,128)(2,1)} %param.18), channel_id=1, source_target_pairs={{1,2},{2,1},{5,6},{6,5},{9,10},{10,9},{13,14},{14,13},{17,18},{18,... | collective-permute-start | bytes 3538952 | tf_op jit(solution)/shard_map/ppermute | solution.py:523
  24.5 38.7 %collective-permute-start.7 = (bf16[512,1152]{1,0:T(8,128)(2,1)}, bf16[512,1152]{1,0:T(8,128)(2,1)}, u32[]{:S(2)}, u32[]{:S(2)}) collective-permute-start(bf16[512,1152]{1,0:T(8,128)(2,1)} %param.19), channel_id=1, source_target_pairs={{0,1},{1,0},{2,3},{3,2},{4,5},{5,4},{6,7},{7,6},{8,9},{9,8},{10,11... | collective-permute-start | bytes 3538952 | tf_op jit(solution)/shard_map/ppermute | solution.py:672
  27.8 17.2 %all-to-all-start = ((s32[16,1,9]{2,1,0:T(1,128)}), s32[16,1,9]{2,1,0:T(1,128)S(1)}, u32[]{:S(2)}, u32[]{:S(2)}) async-start(s32[16,1,9]{2,1,0:T(1,128)} %broadcast_in_dim.146), calls=%async_computation | async-start | bytes 16384 | tf_op jit(solution)/shard_map/all_to_all | solution.py:645
  32.7 10.4 %collective-permute-start.2 = (bf16[72,1152]{1,0:T(8,128)(2,1)S(1)}, bf16[72,1152]{1,0:T(8,128)(2,1)S(1)}, u32[]{:S(2)}, u32[]{:S(2)}) collective-permute-start(bf16[72,1152]{1,0:T(8,128)(2,1)S(1)} %get-tuple-element.156), channel_id=1, source_target_pairs={{0,16},{4,20},{8,24},{12,28},{16,0},{20,4},{24,8},{28,12},{1,17},{... | collective-permute-start | bytes 497672 | tf_op jit(solution)/shard_map/ppermute | solution.py:551
  35.7 32.9 %collective-permute-start.5 = (bf16[2,72,1152]{2,1,0:T(8,128)(2,1)}, bf16[2,72,1152]{2,1,0:T(8,128)(2,1)}, u32[]{:S(2)}, u32[]{:S(2)}) collective-permute-start(bf16[2,72,1152]{2,1,0:T(8,128)(2,1)} %pad_maximum_fusion.6), channel_id=1, source_target_pairs={{0,8},{4,12},{8,0},{12,4},{16,24},{20,28},{24,16},{28,20},{1,9},{5... | collective-permute-start | bytes 995336 | tf_op jit(solution)/shard_map/ppermute | solution.py:551
  51.4 8.5 %collective-permute-start.3 = (bf16[2,72,1152]{2,1,0:T(8,128)(2,1)S(1)}, bf16[2,72,1152]{2,1,0:T(8,128)(2,1)S(1)}, u32[]{:S(2)}, u32[]{:S(2)}) collective-permute-start(bf16[2,72,1152]{2,1,0:T(8,128)(2,1)S(1)} %pad_maximum_fusion.5), channel_id=1, source_target_pairs={{0,8},{4,12},{8,0},{12,4},{16,24},{20,28},{24,16},{28,20},{1,9},{5... | collective-permute-start | bytes 995336 | tf_op jit(solution)/shard_map/ppermute | solution.py:551
  61.8 89.0 %copy-start.14 = (bf16[512,1152]{1,0:T(8,128)(2,1)}, bf16[512,1152]{1,0:T(8,128)(2,1)S(1)}, u32[]{:S(2)}) copy-start(bf16[512,1152]{1,0:T(8,128)(2,1)S(1)} %get-tuple-element.135) | copy-start | bytes 3538948
  66.7 21.5 %collective-permute-start.9 = (bf16[2,2,72,1152]{3,2,0,1:T(8,128)(2,1)}, bf16[2,2,72,1152]{3,2,0,1:T(8,128)(2,1)}, u32[]{:S(2)}, u32[]{:S(2)}) collective-permute-start(bf16[2,2,72,1152]{3,2,0,1:T(8,128)(2,1)} %maximum_select_fusion.2), channel_id=1, source_target_pairs={{0,1},{1,0},{2,3},{3,2},{4,5},{5,4},{6,7},{7,6},{8,9},{9,8},{10,11... | collective-permute-start | bytes 1990664 | tf_op jit(solution)/shard_map/ppermute | solution.py:551
  69.6 18.5 %copy-start.37 = (bf16[2,1,72,1152]{3,2,0,1:T(8,128)(2,1)}, bf16[2,1,72,1152]{3,2,0,1:T(8,128)(2,1)S(1)}, u32[]{:S(2)}) copy-start(bf16[2,1,72,1152]{3,2,0,1:T(8,128)(2,1)S(1)} %get-tuple-element.149) | copy-start | bytes 995332
  72.8 12.3 %all-to-all-start.1 = ((f32[16,2,432]{2,1,0:T(2,128)}), f32[16,2,432]{2,1,0:T(2,128)S(1)}, u32[]{:S(2)}, u32[]{:S(2)}) async-start(f32[16,2,432]{2,1,0:T(2,128)} %bitcast.13), calls=%async_computation.1 | async-start | bytes 131072 | tf_op jit(solution)/shard_map/all_to_all | solution.py:663
  79.0 166.4 %all-gather.5.cloned.1.call-start = ((), (), s32[]{:S(2)}) async-start(), calls=%async_computation.7 | async-start | bytes 1566720 | tf_op jit(solution)/shard_map/all_gather | solution.py:639
  87.8 15.8 %collective-permute-start.11 = (bf16[2,2,72,1152]{3,2,0,1:T(8,128)(2,1)}, bf16[2,2,72,1152]{3,2,0,1:T(8,128)(2,1)}, u32[]{:S(2)}, u32[]{:S(2)}) collective-permute-start(bf16[2,2,72,1152]{3,2,0,1:T(8,128)(2,1)} %maximum_select_fusion.3), channel_id=1, source_target_pairs={{0,4},{4,0},{8,12},{12,8},{16,20},{20,16},{24,28},{28,24},{1,5},{5... | collective-permute-start | bytes 1990664 | tf_op jit(solution)/shard_map/ppermute | solution.py:551
  90.7 49.1 %collective-permute-start.10 = (bf16[2,2,2,72,1152]{4,3,0,1,2:T(8,128)(2,1)}, bf16[2,2,2,72,1152]{4,3,0,1,2:T(8,128)(2,1)}, u32[]{:S(2)}, u32[]{:S(2)}) collective-permute-start(bf16[2,2,2,72,1152]{4,3,0,1,2:T(8,128)(2,1)} %maximum_select_fusion), channel_id=1, source_target_pairs={{0,4},{4,0},{8,12},{12,8},{16,20},{20,16},{24,28},{28,24},{1,5},{5... | collective-permute-start | bytes 3981320 | tf_op jit(solution)/shard_map/ppermute | solution.py:551
  107.0 35.5 %collective-permute-start.12 = (bf16[2,2,2,72,1152]{4,3,0,1,2:T(8,128)(2,1)}, bf16[2,2,2,72,1152]{4,3,0,1,2:T(8,128)(2,1)}, u32[]{:S(2)}, u32[]{:S(2)}) collective-permute-start(bf16[2,2,2,72,1152]{4,3,0,1,2:T(8,128)(2,1)} %maximum_select_fusion.1), channel_id=1, source_target_pairs={{0,1},{1,0},{2,3},{3,2},{4,5},{5,4},{6,7},{7,6},{8,9},{9,8},{10,11... | collective-permute-start | bytes 3981320 | tf_op jit(solution)/shard_map/ppermute | solution.py:551
  107.3 31.8 %collective-permute-start.13 = (bf16[72,576]{1,0:T(8,128)(2,1)S(1)}, bf16[72,576]{1,0:T(8,128)(2,1)S(1)}, u32[]{:S(2)}, u32[]{:S(2)}) collective-permute-start(bf16[72,576]{1,0:T(8,128)(2,1)S(1)} %bitcast.279), channel_id=1, source_target_pairs={{1,2},{2,1},{5,6},{6,5},{9,10},{10,9},{13,14},{14,13},{17,18},{18,... | collective-permute-start | bytes 248840 | tf_op jit(solution)/shard_map/ppermute | solution.py:523
  139.7 146.0 %all-gather.3.cloned.1.call-start = ((), (), s32[]{:S(2)}) async-start(), calls=%async_computation.6 | async-start | bytes 11280384 | tf_op jit(solution)/shard_map/all_gather | solution.py:682
  149.3 558.5 %reduce-scatter.3.cloned.1.call-start = ((), (), s32[]{:S(2)}) async-start(), calls=%async_computation.8 | async-start | bytes 5640192 | tf_op jit(solution)/shard_map/reduce_scatter | solution.py:730
  152.1 7.3 %collective-permute-start.6 = (bf16[512,1152]{1,0:T(8,128)(2,1)S(1)}, bf16[512,1152]{1,0:T(8,128)(2,1)S(1)}, u32[]{:S(2)}, u32[]{:S(2)}) collective-permute-start(bf16[512,1152]{1,0:T(8,128)(2,1)S(1)} %fusion.56.x_ref), channel_id=1, source_target_pairs={{0,2},{2,0},{1,3},{3,1},{4,6},{6,4},{5,7},{7,5},{8,10},{10,8},{9,1... | collective-permute-start | bytes 3538952 | tf_op jit(solution)/shard_map/ppermute | solution.py:528
  250.5 12.5 %collective-permute-start.14 = (f32[512,1152]{1,0:T(8,128)S(1)}, f32[512,1152]{1,0:T(8,128)S(1)}, u32[]{:S(2)}, u32[]{:S(2)}) collective-permute-start(f32[512,1152]{1,0:T(8,128)S(1)} %get-tuple-element.38), channel_id=1, source_target_pairs={{0,2},{2,0},{1,3},{3,1},{4,6},{6,4},{5,7},{7,5},{8,10},{10,8},{9,1... | collective-permute-start | bytes 7077896 | tf_op jit(solution)/shard_map/ppermute | solution.py:528
  251.0 7.8 %collective-permute-start.16 = (bf16[512,1152]{1,0:T(8,128)(2,1)S(1)}, bf16[512,1152]{1,0:T(8,128)(2,1)S(1)}, u32[]{:S(2)}, u32[]{:S(2)}) collective-permute-start(bf16[512,1152]{1,0:T(8,128)(2,1)S(1)} %copy-done.59), channel_id=1, source_target_pairs={{0,2},{2,0},{1,3},{3,1},{4,6},{6,4},{5,7},{7,5},{8,10},{10,8},{9,1... | collective-permute-start | bytes 3538952 | tf_op jit(solution)/shard_map/ppermute | solution.py:528
  251.1 10.4 %collective-permute-start.8 = (bf16[512,1152]{1,0:T(8,128)(2,1)}, bf16[512,1152]{1,0:T(8,128)(2,1)S(1)}, u32[]{:S(2)}, u32[]{:S(2)}) collective-permute-start(bf16[512,1152]{1,0:T(8,128)(2,1)} %collective-permute-done.7), channel_id=1, source_target_pairs={{0,2},{2,0},{1,3},{3,1},{4,6},{6,4},{5,7},{7,5},{8,10},{10,8},{9,1... | collective-permute-start | bytes 3538952 | tf_op jit(solution)/shard_map/ppermute | solution.py:528
  251.5 2.9 collective-permute-start.17
  263.0 107.3 %copy-start.21 = (bf16[512,1152]{1,0:T(8,128)(2,1)}, bf16[512,1152]{1,0:T(8,128)(2,1)S(1)}, u32[]{:S(2)}) copy-start(bf16[512,1152]{1,0:T(8,128)(2,1)S(1)} %get-tuple-element.130) | copy-start | bytes 3538948
  267.2 40.4 %collective-permute-start.15 = (bf16[512,1152]{1,0:T(8,128)(2,1)}, bf16[512,1152]{1,0:T(8,128)(2,1)}, u32[]{:S(2)}, u32[]{:S(2)}) collective-permute-start(bf16[512,1152]{1,0:T(8,128)(2,1)} %fusion.63), channel_id=1, source_target_pairs={{0,1},{1,0},{2,3},{3,2},{4,5},{5,4},{6,7},{7,6},{8,9},{9,8},{10,11... | collective-permute-start | bytes 3538952 | tf_op jit(solution)/shard_map/ppermute | solution.py:541
  330.2 379.4 %reduce-scatter.5.cloned.1.call-start = ((), (), s32[]{:S(2)}) async-start(), calls=%async_computation.9 | async-start | bytes 5640192 | tf_op jit(solution)/shard_map/reduce_scatter | solution.py:728
  339.3 27.6 %collective-permute-start.18 = (bf16[512,1152]{1,0:T(8,128)(2,1)}, bf16[512,1152]{1,0:T(8,128)(2,1)}, u32[]{:S(2)}, u32[]{:S(2)}) collective-permute-start(bf16[512,1152]{1,0:T(8,128)(2,1)} %fusion.43), channel_id=1, source_target_pairs={{0,1},{1,0},{2,3},{3,2},{4,5},{5,4},{6,7},{7,6},{8,9},{9,8},{10,11... | collective-permute-start | bytes 3538952 | tf_op jit(solution)/shard_map/ppermute | solution.py:541
  359.7 183.7 %collective-permute-start.22 = (bf16[512,1152]{1,0:T(8,128)(2,1)}, bf16[512,1152]{1,0:T(8,128)(2,1)}, u32[]{:S(2)}, u32[]{:S(2)}) collective-permute-start(bf16[512,1152]{1,0:T(8,128)(2,1)} %fusion.46), channel_id=1, source_target_pairs={{0,1},{1,0},{2,3},{3,2},{4,5},{5,4},{6,7},{7,6},{8,9},{9,8},{10,11... | collective-permute-start | bytes 3538952 | tf_op jit(solution)/shard_map/ppermute | solution.py:541
  372.1 11.1 %collective-permute-start.19 = (bf16[512,1152]{1,0:T(8,128)(2,1)}, bf16[512,1152]{1,0:T(8,128)(2,1)S(1)}, u32[]{:S(2)}, u32[]{:S(2)}) collective-permute-start(bf16[512,1152]{1,0:T(8,128)(2,1)} %fusion.61), channel_id=1, source_target_pairs={{0,2},{2,0},{1,3},{3,1},{4,6},{6,4},{5,7},{7,5},{8,10},{10,8},{9,1... | collective-permute-start | bytes 3538952 | tf_op jit(solution)/shard_map/ppermute | solution.py:528
  390.6 91.5 %collective-permute-start.20 = (bf16[2,2,2,72,576]{4,3,2,1,0:T(8,128)(2,1)S(1)}, bf16[2,2,2,72,576]{4,3,2,1,0:T(8,128)(2,1)S(1)}, u32[]{:S(2)}, u32[]{:S(2)}) collective-permute-start(bf16[2,2,2,72,576]{4,3,2,1,0:T(8,128)(2,1)S(1)} %dynamic-slice_bitcast_fusion), channel_id=1, source_target_pairs={{0,4},{4,0},{8,12},{12,8},{16,20},{20,16},{24,28},{28,24},{1,5},{5... | collective-permute-start | bytes 1990664 | tf_op jit(solution)/shard_map/ppermute | solution.py:551
  496.1 40.8 %collective-permute-start.21 = (bf16[2,2,2,72,1152]{4,3,0,1,2:T(8,128)(2,1)}, bf16[2,2,2,72,1152]{4,3,0,1,2:T(8,128)(2,1)}, u32[]{:S(2)}, u32[]{:S(2)}) collective-permute-start(bf16[2,2,2,72,1152]{4,3,0,1,2:T(8,128)(2,1)} %bitcast.252), channel_id=1, source_target_pairs={{0,1},{1,0},{2,3},{3,2},{4,5},{5,4},{6,7},{7,6},{8,9},{9,8},{10,11... | collective-permute-start | bytes 3981320 | tf_op jit(solution)/shard_map/ppermute | solution.py:551
  529.9 28.8 %collective-permute-start.25 = (bf16[2,2,2,72,1152]{4,3,0,1,2:T(8,128)(2,1)}, bf16[2,2,2,72,1152]{4,3,0,1,2:T(8,128)(2,1)}, u32[]{:S(2)}, u32[]{:S(2)}) collective-permute-start(bf16[2,2,2,72,1152]{4,3,0,1,2:T(8,128)(2,1)} %bitcast.251), channel_id=1, source_target_pairs={{0,4},{4,0},{8,12},{12,8},{16,20},{20,16},{24,28},{28,24},{1,5},{5... | collective-permute-start | bytes 3981320 | tf_op jit(solution)/shard_map/ppermute | solution.py:551
  534.5 35.4 %collective-permute-start.38 = (f32[43,1152]{1,0:T(8,128)S(1)}, f32[43,1152]{1,0:T(8,128)S(1)}, u32[]{:S(2)}, u32[]{:S(2)}) collective-permute-start(f32[43,1152]{1,0:T(8,128)S(1)} %pad_maximum_fusion.7), channel_id=1, source_target_pairs={{0,2},{2,0},{1,3},{3,1},{4,6},{6,4},{5,7},{7,5},{8,10},{10,8},{9,1... | collective-permute-start | bytes 594440 | tf_op jit(solution)/shard_map/ppermute | solution.py:528
  536.9 46.9 %collective-permute-start.27 = (f32[512,1152]{1,0:T(8,128)}, f32[512,1152]{1,0:T(8,128)S(1)}, u32[]{:S(2)}, u32[]{:S(2)}) collective-permute-start(f32[512,1152]{1,0:T(8,128)} %get-tuple-element.49), channel_id=1, source_target_pairs={{0,2},{2,0},{1,3},{3,1},{4,6},{6,4},{5,7},{7,5},{8,10},{10,8},{9,1... | collective-permute-start | bytes 7077896 | tf_op jit(solution)/shard_map/ppermute | solution.py:528
  542.2 72.4 %collective-permute-start.34 = (bf16[2,2,72,576]{3,2,1,0:T(8,128)(2,1)}, bf16[2,2,72,576]{3,2,1,0:T(8,128)(2,1)}, u32[]{:S(2)}, u32[]{:S(2)}) collective-permute-start(bf16[2,2,72,576]{3,2,1,0:T(8,128)(2,1)} %dynamic-slice_bitcast_fusion.3), channel_id=1, source_target_pairs={{0,1},{1,0},{2,3},{3,2},{4,5},{5,4},{6,7},{7,6},{8,9},{9,8},{10,11... | collective-permute-start | bytes 995336 | tf_op jit(solution)/shard_map/ppermute | solution.py:551
  543.4 62.3 %collective-permute-start.24 = (bf16[2,2,72,1152]{3,2,0,1:T(8,128)(2,1)}, bf16[2,2,72,1152]{3,2,0,1:T(8,128)(2,1)}, u32[]{:S(2)}, u32[]{:S(2)}) collective-permute-start(bf16[2,2,72,1152]{3,2,0,1:T(8,128)(2,1)} %dynamic-slice_bitcast_fusion.2), channel_id=1, source_target_pairs={{0,4},{4,0},{8,12},{12,8},{16,20},{20,16},{24,28},{28,24},{1,5},{5... | collective-permute-start | bytes 1990664 | tf_op jit(solution)/shard_map/ppermute | solution.py:551
  543.5 40.3 %copy-start.28 = (f32[512,1152]{1,0:T(8,128)S(1)}, f32[512,1152]{1,0:T(8,128)}, u32[]{:S(2)}) copy-start(f32[512,1152]{1,0:T(8,128)} %get-tuple-element.133) | copy-start | bytes 7077892
  543.5 40.3 %copy-start.45 = (f32[512,1152]{1,0:T(8,128)S(1)}, f32[512,1152]{1,0:T(8,128)}, u32[]{:S(2)}) copy-start(f32[512,1152]{1,0:T(8,128)} %get-tuple-element.48) | copy-start | bytes 7077892
  546.6 23.4 %copy-start.68 = (f32[16,1152]{1,0:T(8,128)S(1)}, f32[16,1152]{1,0:T(8,128)}, u32[]{:S(2)}) copy-start(f32[16,1152]{1,0:T(8,128)} %reshape.571) | copy-start | bytes 221188
  546.6 23.4 %copy-start.86 = (f32[1,1152]{1,0:T(1,128)S(1)}, f32[1,1152]{1,0:T(1,128)}, u32[]{:S(2)}) copy-start(f32[1,1152]{1,0:T(1,128)} %broadcast_in_dim.180) | copy-start | bytes 13828
  558.7 89.4 %collective-permute-start.23 = (bf16[512,1152]{1,0:T(8,128)(2,1)}, bf16[512,1152]{1,0:T(8,128)(2,1)}, u32[]{:S(2)}, u32[]{:S(2)}) collective-permute-start(bf16[512,1152]{1,0:T(8,128)(2,1)} %fusion.76), channel_id=1, source_target_pairs={{1,2},{2,1},{5,6},{6,5},{9,10},{10,9},{13,14},{14,13},{17,18},{18,... | collective-permute-start | bytes 3538952 | tf_op jit(solution)/shard_map/ppermute | solution.py:523
  566.2 17.6 %copy-start.16 = (bf16[512,1152]{1,0:T(8,128)(2,1)S(1)}, bf16[512,1152]{1,0:T(8,128)(2,1)}, u32[]{:S(2)}) copy-start(bf16[512,1152]{1,0:T(8,128)(2,1)} %copy-done.14) | copy-start | bytes 3538948
  570.0 13.0 %collective-permute-start.39 = (f32[43,1152]{1,0:T(8,128)S(1)}, f32[43,1152]{1,0:T(8,128)S(1)}, u32[]{:S(2)}, u32[]{:S(2)}) collective-permute-start(f32[43,1152]{1,0:T(8,128)S(1)} %add_select_fusion.3), channel_id=1, source_target_pairs={{0,16},{4,20},{8,24},{12,28},{16,0},{20,4},{24,8},{28,12},{1,17},{... | collective-permute-start | bytes 594440 | tf_op jit(solution)/shard_map/ppermute | solution.py:551
  583.0 18.7 %collective-permute-start.26 = (bf16[2,2,72,1152]{3,2,0,1:T(8,128)(2,1)}, bf16[2,2,72,1152]{3,2,0,1:T(8,128)(2,1)}, u32[]{:S(2)}, u32[]{:S(2)}) collective-permute-start(bf16[2,2,72,1152]{3,2,0,1:T(8,128)(2,1)} %dynamic-slice_bitcast_fusion.1), channel_id=1, source_target_pairs={{0,1},{1,0},{2,3},{3,2},{4,5},{5,4},{6,7},{7,6},{8,9},{9,8},{10,11... | collective-permute-start | bytes 1990664 | tf_op jit(solution)/shard_map/ppermute | solution.py:551
  583.8 36.7 %collective-permute-start.40 = (f32[43,1152]{1,0:T(8,128)}, f32[43,1152]{1,0:T(8,128)}, u32[]{:S(2)}, u32[]{:S(2)}) collective-permute-start(f32[43,1152]{1,0:T(8,128)} %add_select_fusion.2), channel_id=1, source_target_pairs={{0,8},{4,12},{8,0},{12,4},{16,24},{20,28},{24,16},{28,20},{1,9},{5... | collective-permute-start | bytes 594440 | tf_op jit(solution)/shard_map/ppermute | solution.py:551
  609.8 17.9 %all-to-all-start.2 = ((bf16[16,2,432]{2,1,0:T(2,128)(2,1)}), bf16[16,2,432]{2,1,0:T(2,128)(2,1)}, u32[]{:S(2)}, u32[]{:S(2)}) async-start(bf16[16,2,432]{2,1,0:T(2,128)(2,1)} %copy.122), calls=%async_computation.2 | async-start | bytes 65536 | tf_op jit(solution)/shard_map/all_to_all | solution.py:761
  617.4 35.3 %collective-permute-start.35 = (bf16[2,72,576]{2,1,0:T(8,128)(2,1)}, bf16[2,72,576]{2,1,0:T(8,128)(2,1)}, u32[]{:S(2)}, u32[]{:S(2)}) collective-permute-start(bf16[2,72,576]{2,1,0:T(8,128)(2,1)} %dynamic-slice_bitcast_fusion.6), channel_id=1, source_target_pairs={{0,8},{4,12},{8,0},{12,4},{16,24},{20,28},{24,16},{28,20},{1,9},{5... | collective-permute-start | bytes 497672 | tf_op jit(solution)/shard_map/ppermute | solution.py:551
  626.4 29.7 %collective-permute-start.41 = (f32[43,1152]{1,0:T(8,128)}, f32[43,1152]{1,0:T(8,128)}, u32[]{:S(2)}, u32[]{:S(2)}) collective-permute-start(f32[43,1152]{1,0:T(8,128)} %add_select_fusion.1), channel_id=1, source_target_pairs={{0,4},{4,0},{8,12},{12,8},{16,20},{20,16},{24,28},{28,24},{1,5},{5... | collective-permute-start | bytes 594440 | tf_op jit(solution)/shard_map/ppermute | solution.py:551
  628.4 5.7 collective-permute-start.29
  632.1 26.5 %collective-permute-start.30 = (bf16[2,72,1152]{2,1,0:T(8,128)(2,1)}, bf16[2,72,1152]{2,1,0:T(8,128)(2,1)}, u32[]{:S(2)}, u32[]{:S(2)}) collective-permute-start(bf16[2,72,1152]{2,1,0:T(8,128)(2,1)} %dynamic-slice_bitcast_fusion.5), channel_id=1, source_target_pairs={{0,8},{4,12},{8,0},{12,4},{16,24},{20,28},{24,16},{28,20},{1,9},{5... | collective-permute-start | bytes 995336 | tf_op jit(solution)/shard_map/ppermute | solution.py:551
  634.2 27.9 %collective-permute-start.32 = (bf16[2,72,1152]{2,1,0:T(8,128)(2,1)}, bf16[2,72,1152]{2,1,0:T(8,128)(2,1)S(1)}, u32[]{:S(2)}, u32[]{:S(2)}) collective-permute-start(bf16[2,72,1152]{2,1,0:T(8,128)(2,1)} %dynamic-slice_bitcast_fusion.4), channel_id=1, source_target_pairs={{0,8},{4,12},{8,0},{12,4},{16,24},{20,28},{24,16},{28,20},{1,9},{5... | collective-permute-start | bytes 995336 | tf_op jit(solution)/shard_map/ppermute | solution.py:551
  639.4 53.5 %all-to-all-start.3 = ((f32[16,4,1152]{2,1,0:T(4,128)}), f32[16,4,1152]{2,1,0:T(4,128)}, u32[]{:S(2)}, u32[]{:S(2)}) async-start(f32[16,4,1152]{2,1,0:T(4,128)} %copy.126), calls=%async_computation.3 | async-start | bytes 589824 | tf_op jit(solution)/shard_map/all_to_all | solution.py:800
  648.2 56.1 %collective-permute-start.28 = (f32[512,1152]{1,0:T(8,128)S(1)}, f32[512,1152]{1,0:T(8,128)}, u32[]{:S(2)}, u32[]{:S(2)}) collective-permute-start(f32[512,1152]{1,0:T(8,128)S(1)} %copy-done.27), channel_id=1, source_target_pairs={{1,2},{2,1},{5,6},{6,5},{9,10},{10,9},{13,14},{14,13},{17,18},{18,... | collective-permute-start | bytes 7077896 | tf_op jit(solution)/shard_map/ppermute | solution.py:523
  653.7 4.8 collective-permute-start.36
  657.2 23.5 %collective-permute-start.42 = (f32[43,1152]{1,0:T(8,128)S(1)}, f32[43,1152]{1,0:T(8,128)S(1)}, u32[]{:S(2)}, u32[]{:S(2)}) collective-permute-start(f32[43,1152]{1,0:T(8,128)S(1)} %add_select_fusion), channel_id=1, source_target_pairs={{0,1},{1,0},{2,3},{3,2},{4,5},{5,4},{6,7},{7,6},{8,9},{9,8},{10,11... | collective-permute-start | bytes 594440 | tf_op jit(solution)/shard_map/ppermute | solution.py:551
  658.6 23.4 %copy-start.46 = (f32[72,576]{1,0:T(8,128)}, f32[72,576]{1,0:T(8,128)S(1)}, u32[]{:S(2)}) copy-start(f32[72,576]{1,0:T(8,128)S(1)} %convert_add_fusion.14) | copy-start | bytes 497668
  659.8 21.0 %collective-permute-start.31 = (bf16[72,1152]{1,0:T(8,128)(2,1)S(1)}, bf16[72,1152]{1,0:T(8,128)(2,1)S(1)}, u32[]{:S(2)}, u32[]{:S(2)}) collective-permute-start(bf16[72,1152]{1,0:T(8,128)(2,1)S(1)} %dynamic-slice_bitcast_fusion.8), channel_id=1, source_target_pairs={{0,16},{4,20},{8,24},{12,28},{16,0},{20,4},{24,8},{28,12},{1,17},{... | collective-permute-start | bytes 497672 | tf_op jit(solution)/shard_map/ppermute | solution.py:551
  662.2 18.6 %collective-permute-start.33 = (bf16[72,1152]{1,0:T(8,128)(2,1)S(1)}, bf16[72,1152]{1,0:T(8,128)(2,1)S(1)}, u32[]{:S(2)}, u32[]{:S(2)}) collective-permute-start(bf16[72,1152]{1,0:T(8,128)(2,1)S(1)} %dynamic-slice_bitcast_fusion.7), channel_id=1, source_target_pairs={{0,16},{4,20},{8,24},{12,28},{16,0},{20,4},{24,8},{28,12},{1,17},{... | collective-permute-start | bytes 497672 | tf_op jit(solution)/shard_map/ppermute | solution.py:551
  681.9 14.8 %collective-permute-start.37 = (f32[72,2880]{1,0:T(8,128)}, f32[72,2880]{1,0:T(8,128)}, u32[]{:S(2)}, u32[]{:S(2)}) collective-permute-start(f32[72,2880]{1,0:T(8,128)} %pad_maximum_fusion.4), channel_id=1, source_target_pairs={{1,2},{2,1},{5,6},{6,5},{9,10},{10,9},{13,14},{14,13},{17,18},{18,... | collective-permute-start | bytes 2488328 | tf_op jit(solution)/shard_map/ppermute | solution.py:523
  (101 other events, 701.6 us)
Sparse Core Ops, SparseCore 0:
  139.8 53.3 all-gather.4
  196.1 89.5 all-gather.2
  330.3 79.1 reduce-scatter.2
  413.4 78.4 reduce-scatter.4

commit v3 on v2

--- a/solution.py
+++ b/solution.py
@@ -137,7 +137,15 @@
         diag=jnp.sum(q*k,axis=1,keepdims=True)
         A=jnp.where(lvl==-1,diag,0.0)
         for b,E,W in level_ops(q,k,L,lw):
-            A=jnp.where(lvl==b,mmx(W,W,1,1,PS),A)
+            if b>=8:
+                n=CHUNK//(2*b)
+                late=W.reshape(n,2*b,LANES)[:,b:].reshape(CHUNK//2,LANES)
+                part=mmx(late,W,1,1,PS).reshape(n,b,CHUNK)
+                A3=A.reshape(n,2*b,CHUNK)
+                part=jnp.where(lvl.reshape(n,2*b,CHUNK)[:,b:]==b,part,A3[:,b:])
+                A=jnp.concatenate([A3[:,:b],part],axis=1).reshape(CHUNK,CHUNK)
+            else:
+                A=jnp.where(lvl==b,mmx(W,W,1,1,PS),A)
         a_ref[0,c]=A.astype(a_ref.dtype)
         last=L[CHUNK-1:CHUNK,:]
         o=mmx(A,v,1,0,PA)+mmx(q*jnp.exp2(L),S,1,1,PA)
@@ -150,7 +158,7 @@
         return 0
     lax.fori_loop(0,chunks,step,0,unroll=4)
 
-def gla_forward(big,qkvg,pre,taps,gain,PS=2,PA=2,adt=f32):
+def gla_forward(big,qkvg,pre,taps,gain,PS=1,PA=2,adt=f32):
     _,H,total,_=qkvg.shape; chunks=total//CHUNK
     row=pl.BlockSpec((1,total,LANES),lambda h:(h,0,0))
     def of(i): return pl.BlockSpec((None,1,total,LANES),lambda h:(i,h,0,0))
@@ -167,12 +175,12 @@
     )(big,qkvg,qkvg,qkvg,qkvg,pre,taps,gain)
 
 def bwd_kernel(PS,PA,total,big_ref,q_ref,k_ref,v_ref,g_ref,p_ref,comb_ref,a_ref,s_ref,gm_ref,taps_ref,gain_ref,
-               dqk_ref,dpre_ref,dtaps_ref,dvec_ref,vp,dcp,gl,gr,dvl,lvl_ref,tri_ref,ds,car):
+               dqk_ref,dpre_ref,dtaps_ref,dvec_ref,vp,dcp,gl,gr,dvl,mask_ref,tri_ref,ds,car):
     chunks=total//CHUNK
     @pl.when(pl.program_id(0)==0)
     def _():
         lvl,i,j=level_matrix()
-        lvl_ref[...]=jnp.where(i==j,-1,lvl)
+        for at,b in enumerate(LEVELS): mask_ref[at]=jnp.where(lvl==b,1.0,0.0).astype(bf16)
         tri_ref[0]=jnp.where(i>=j,1.0,0.0).astype(bf16)
         tri_ref[1]=jnp.where(i<=j,1.0,0.0).astype(bf16)
         z=jnp.zeros((MARGIN,LANES),f32)
@@ -234,7 +242,6 @@
         lw=log_decay2(pre)
         L=sel_mm(tri_ref[0],lw,3)
         do=dcp[pl.ds(pl.multiple_of(MARGIN+c*CHUNK,MARGIN),CHUNK),:]
-        lvl=lvl_ref[...]
         low=tri_ref[0].astype(f32)>0.5
         G=jnp.where(low,mmx(do,v,1,1,PS),mmx(v,do,1,1,PS))
         last=L[CHUNK-1:CHUNK,:]
@@ -245,10 +252,22 @@
         dk=eR*mmx(v,dS,1,0,PA)
         dv=dvl[rows,:]+mmx(a_ref[0,c].astype(f32),do,0,0,PA)+mmx(kR,dS,1,1,PA)
         ds[...]=dS*jnp.exp2(last)+mmx(do,q*eL,0,0,PA)
-        for b,E,W in level_ops(q,k,L,lw):
-            Y=E*mmx(jnp.where(lvl==b,G,0.0),W,1,0,PS)
-            right=(row&b)!=0
-            dq=dq+jnp.where(right,Y,0.0); dk=dk+jnp.where(right,0.0,Y)
+        Gs=parts(G,PS)
+        for at,(b,E,W) in enumerate(level_ops(q,k,L,lw)):
+            Gb=[g*mask_ref[at] for g in Gs]
+            if PS==1:
+                Y=E*mm(Gb[0],W.astype(bf16),1,0)
+            else:
+                Wh,Wl=parts(W,2)
+                Y=E*(mm(jnp.concatenate(Gb,axis=1),jnp.concatenate([Wh,Wh],axis=0),1,0)+mm(Gb[0],Wl,1,0))
+            if b>=8:
+                n=CHUNK//(2*b)
+                Y=Y.reshape(n,2*b,LANES); q3=dq.reshape(n,2*b,LANES); k3=dk.reshape(n,2*b,LANES)
+                dq=jnp.concatenate([q3[:,:b],q3[:,b:]+Y[:,b:]],axis=1).reshape(CHUNK,LANES)
+                dk=jnp.concatenate([k3[:,:b]+Y[:,:b],k3[:,b:]],axis=1).reshape(CHUNK,LANES)
+            else:
+                late=jnp.where((row&b)!=0,Y,0.0)
+                dq=dq+late; dk=dk+(Y-late)
         z=q*dq-k*dk
         suf=sel_mm(tri_ref[1],z,3)+carry
         car[0:1,:]=suf[0:1,:]
@@ -262,21 +281,22 @@
     db=lax.fori_loop(0,chunks,step,jnp.zeros((8,LANES),f32),unroll=4)
     dvec_ref[0,1:2,:]=jnp.sum(db,axis=0,keepdims=True)
 
-def gla_backward(big,qkvg,pre,comb,A,S,gm,taps,gain,PS=2,PA=2):
+def gla_backward(base,count,big,qkvg,pre,comb,A,S,gm,taps,gain,PS=2,PA=2):
     _,H,total,_=qkvg.shape; chunks=total//CHUNK
-    row=pl.BlockSpec((1,total,LANES),lambda h:(h,0,0))
-    def of(i): return pl.BlockSpec((None,1,total,LANES),lambda h:(i,h,0,0))
+    row=pl.BlockSpec((1,total,LANES),lambda h:(h+base,0,0))
+    out=pl.BlockSpec((1,total,LANES),lambda h:(h,0,0))
+    def of(i): return pl.BlockSpec((None,1,total,LANES),lambda h:(i,h+base,0,0))
     return pl.pallas_call(
         functools.partial(bwd_kernel,PS,PA,total),
-        grid=(H,),
-        in_specs=[pl.BlockSpec(memory_space=pltpu.SMEM)]+[of(i) for i in range(4)]+[row]*2+[pl.BlockSpec((1,chunks,CHUNK,CHUNK),lambda h:(h,0,0,0)),pl.BlockSpec((1,chunks,LANES,LANES),lambda h:(h,0,0,0)),row,
-                  pl.BlockSpec((1,16,LANES),lambda h:(h,0,0)),pl.BlockSpec((1,LANES),lambda h:(0,0))],
-        out_specs=[pl.BlockSpec((4,1,total,LANES),lambda h:(0,h,0,0)),row,pl.BlockSpec((1,16,LANES),lambda h:(h,0,0)),pl.BlockSpec((1,8,LANES),lambda h:(h,0,0))],
-        out_shape=[jax.ShapeDtypeStruct((4,H,total,LANES),bf16),jax.ShapeDtypeStruct((H,total,LANES),f32),
-                   jax.ShapeDtypeStruct((H,16,LANES),f32),jax.ShapeDtypeStruct((H,8,LANES),f32)],
-        scratch_shapes=[pltpu.VMEM((total+2*MARGIN,LANES),f32)]*4+[pltpu.VMEM((total,LANES),f32),pltpu.VMEM((CHUNK,CHUNK),jnp.int32),pltpu.VMEM((2,CHUNK,CHUNK),bf16),pltpu.VMEM((LANES,LANES),f32),pltpu.VMEM((8,LANES),f32)],
+        grid=(count,),
+        in_specs=[pl.BlockSpec(memory_space=pltpu.SMEM)]+[of(i) for i in range(4)]+[row]*2+[pl.BlockSpec((1,chunks,CHUNK,CHUNK),lambda h:(h+base,0,0,0)),pl.BlockSpec((1,chunks,LANES,LANES),lambda h:(h+base,0,0,0)),row,
+                  pl.BlockSpec((1,16,LANES),lambda h:(h+base,0,0)),pl.BlockSpec((1,LANES),lambda h:(0,0))],
+        out_specs=[pl.BlockSpec((4,1,total,LANES),lambda h:(0,h,0,0)),out,pl.BlockSpec((1,16,LANES),lambda h:(h,0,0)),pl.BlockSpec((1,8,LANES),lambda h:(h,0,0))],
+        out_shape=[jax.ShapeDtypeStruct((4,count,total,LANES),bf16),jax.ShapeDtypeStruct((count,total,LANES),f32),
+                   jax.ShapeDtypeStruct((count,16,LANES),f32),jax.ShapeDtypeStruct((count,8,LANES),f32)],
+        scratch_shapes=[pltpu.VMEM((total+2*MARGIN,LANES),f32)]*4+[pltpu.VMEM((total,LANES),f32),pltpu.VMEM((len(LEVELS),CHUNK,CHUNK),bf16),pltpu.VMEM((2,CHUNK,CHUNK),bf16),pltpu.VMEM((LANES,LANES),f32),pltpu.VMEM((8,LANES),f32)],
         compiler_params=pltpu.CompilerParams(vmem_limit_bytes=48*2**20,dimension_semantics=("arbitrary",)),
-        name="gla_backward", cost_estimate=cost(80),
+        name="gla_backward", cost_estimate=cost(10*count),
     )(big,qkvg,qkvg,qkvg,qkvg,pre,comb,A,S,gm,taps,gain)
 
 
@@ -341,7 +361,7 @@
     for s in range(2):
         res = mm(x, (wa_ref, wb_ref)[s][:, :span], 1, 0)
         for i in range(2 * H):
-            out_ref[2 * s + i // H, i % H] = head_window(res, i * HDIM)
+            out_ref[2 * i // H, s * (H // 2) + i % (H // 2)] = head_window(res, i * HDIM)
     latent = mm(x, down_ref[...], 1, 0)
     lat_ref[...] = latent
     pre = bias_ref[...] + sum(mm(p, up_ref[...], 1, 0) for p in parts(latent, 3)[::-1])
@@ -430,52 +450,47 @@
     )(turn, grad, w)
 
 
-def join_kernel(H, turn_ref, d_ref, cata_ref, catb_ref):
-    for s in range(2):
-        cat = heads_joined([d_ref[2 * s + i // H, i % H].astype(f32) for i in range(2 * H)])
-        (cata_ref, catb_ref)[s][...] = cat.astype(bf16)
+def join_kernel(H, turn_ref, d_ref, cat_ref):
+    cat_ref[...] = heads_joined([d_ref[i // H, i % H].astype(f32) for i in range(4 * H)]).astype(bf16)
 
 
 def join(turn, d):
     _, H, total, _ = d.shape
     tiles = total // ROWS
-    cols = 2 * H * HDIM
+    cols = 4 * H * HDIM
     return pl.pallas_call(
         functools.partial(join_kernel, H),
         grid_spec=pltpu.PrefetchScalarGridSpec(
             num_scalar_prefetch=1,
             grid=(tiles,),
             in_specs=[pl.BlockSpec((4, H, ROWS, LANES), lambda i, t: (0, 0, lax.rem(i + t[0], tiles), 0))],
-            out_specs=[pl.BlockSpec((ROWS, cols), lambda i, t: (i, 0))] * 2,
+            out_specs=pl.BlockSpec((ROWS, cols), lambda i, t: (i, 0)),
         ),
-        out_shape=[jax.ShapeDtypeStruct((total, cols), bf16)] * 2,
+        out_shape=jax.ShapeDtypeStruct((total, cols), bf16),
         compiler_params=pltpu.CompilerParams(vmem_limit_bytes=40 * 2**20, dimension_semantics=("arbitrary",)),
-        name="join", cost_estimate=cost(8),
+        name="join", cost_estimate=cost(4),
     )(turn, d)
 
 
-def project_back_kernel(H, half, turn_ref, x_ref, cata_ref, catb_ref, p_ref, lat_ref, wa_ref, wb_ref, down_ref, up_ref, own_ref, away_ref, ddown_ref, dup_ref):
+def project_back_kernel(H, half, turn_ref, x_ref, cata_ref, catb_ref, pa_ref, pb_ref, lat_ref, wa_ref, wb_ref, down_ref, up_ref, own_ref, away_ref, ddown_ref, dup_ref):
     @pl.when(pl.program_id(0) == 0)
     def _():
         dup_ref[...] = jnp.zeros_like(dup_ref)
         ddown_ref[...] = jnp.zeros_like(ddown_ref)
 
     lat = parts(lat_ref[...], 2)
-    glat = jnp.zeros((ROWS, LANES), f32)
-    for h in range(H):
-        dp = parts(p_ref[h], 3)
-        up = up_ref[:, h * LANES : (h + 1) * LANES]
-        glat = glat + (mm(dp[2], up, 1, 1) + mm(dp[1], up, 1, 1) + mm(dp[0], up, 1, 1))
-        dup_ref[h] += mm(lat[0], dp[1], 0, 0) + mm(lat[1], dp[0], 0, 0) + mm(lat[0], dp[0], 0, 0)
+    dp = parts(jnp.concatenate([p[h] for p in (pa_ref, pb_ref) for h in range(H // 2)], axis=1), 2)
+    glat = mm(dp[1], up_ref[...], 1, 1) + mm(dp[0], up_ref[...], 1, 1)
+    dup_ref[...] += mm(lat[0], dp[1], 0, 0) + mm(lat[1], dp[0], 0, 0) + mm(lat[0], dp[0], 0, 0)
     split = parts(glat, 2)[::-1]
-    ddown_ref[...] += sum(mm(x_ref[...], p, 0, 0) for p in split)
+    ddown_ref[...] += sum(mm(p, x_ref[...], 0, 0) for p in split)
     acc = sum(mm(p, down_ref[...], 1, 1) for p in split)
     acc = acc + mm(cata_ref[...], wa_ref[:, : cata_ref.shape[1]], 1, 1) + mm(catb_ref[...], wb_ref[:, : catb_ref.shape[1]], 1, 1)
     put_half(half, acc, own_ref, away_ref)
 
 
-def project_back(turn, x, cat_a, cat_b, dpre, latent, wa, wb, down, up):
-    H, total, _ = dpre.shape
+def project_back(turn, x, cat_a, cat_b, dpre_a, dpre_b, latent, wa, wb, down, up):
+    H, total = 2 * dpre_a.shape[0], dpre_a.shape[1]
     tiles = total // ROWS
     width, cols = x.shape[1], cat_a.shape[1]
 
@@ -492,26 +507,27 @@
                 pl.BlockSpec((ROWS, width), lambda i, t: (i, 0)),
                 pl.BlockSpec((ROWS, cols), lambda i, t: (i, 0)),
                 pl.BlockSpec((ROWS, cols), lambda i, t: (i, 0)),
-                pl.BlockSpec((H, ROWS, LANES), lambda i, t: (0, turned(i, t), 0)),
+                pl.BlockSpec((H // 2, ROWS, LANES), lambda i, t: (0, turned(i, t), 0)),
+                pl.BlockSpec((H // 2, ROWS, LANES), lambda i, t: (0, turned(i, t), 0)),
                 pl.BlockSpec((ROWS, LANES), lambda i, t: (turned(i, t), 0)),
                 full(wa), full(wb), full(down), full(up),
             ],
             out_specs=[
                 first_rows(tiles, width),
                 last_rows(tiles, width),
-                pl.BlockSpec((width, LANES), lambda i, t: (0, 0)),
-                pl.BlockSpec((H, LANES, LANES), lambda i, t: (0, 0, 0)),
+                pl.BlockSpec((LANES, width), lambda i, t: (0, 0)),
+                pl.BlockSpec((LANES, H * LANES), lambda i, t: (0, 0)),
             ],
         ),
         out_shape=[
             jax.ShapeDtypeStruct((total // 2, width), f32),
             jax.ShapeDtypeStruct((total // 2, width), f32),
-            jax.ShapeDtypeStruct((width, LANES), f32),
-            jax.ShapeDtypeStruct((H, LANES, LANES), f32),
+            jax.ShapeDtypeStruct((LANES, width), f32),
+            jax.ShapeDtypeStruct((LANES, H * LANES), f32),
         ],
         compiler_params=pltpu.CompilerParams(vmem_limit_bytes=56 * 2**20, dimension_semantics=("arbitrary",)),
         name="project_back", cost_estimate=cost(2),
-    )(turn, x, cat_a, cat_b, dpre, latent, wa, wb, down, up)
+    )(turn, x, cat_a, cat_b, dpre_a, dpre_b, latent, wa, wb, down, up)
 
 
 NORM_EPS = 1e-06
@@ -561,37 +577,36 @@
     return far + [count - 1, count - 2], far + [count - 2, count - 1]
 
 
-def spread(x, order, steps):
+def spread(x, order, steps, work=()):
     names = bits()
     for step in steps:
         place = order[step]
         away, mine = flipped(x, names[place]), own_bit(names[place])
         at = sum(h < place for h in order[:step])
+        x = after(x, *work) if work else x
         x = jnp.stack([jnp.where(mine == 0, x, away), jnp.where(mine == 0, away, x)], axis=at)
     return x.reshape(-1, x.shape[-1]) if len(order) - 1 in steps else x
 
 
-def fold_step(x, order, step):
+def fold_split(x, order, step):
     names = bits()
     if step == 0:
         x = x.reshape((2,) * len(names) + (-1, x.shape[-1]))
     left = sorted(order[: len(order) - step])
     place = order[len(order) - 1 - step]
     at, mine = left.index(place), own_bit(names[place])
-    send = lax.dynamic_index_in_dim(x, 1 - mine, at, keepdims=False)
-    keep = lax.dynamic_index_in_dim(x, mine, at, keepdims=False)
-    x = keep.astype(f32) + flipped(send, names[place]).astype(f32)
-    return x if len(left) == 1 else x.astype(bf16)
-
-
-def folded_in(x, order, gates):
-    sums = [x]
-    for step in range(1, len(order)):
-        for gate in gates.get(len(order) - step, ()):
-            x = after(x, gate)
-        x = fold_step(x, order, step)
-        sums.append(x)
-    return sums
+    return lax.dynamic_index_in_dim(x, 1 - mine, at, keepdims=False), lax.dynamic_index_in_dim(x, mine, at, keepdims=False)
+
+
+def fold_sum(split, order, step, work=()):
+    send, keep = split
+    keep = after(keep, *work) if work else keep
+    x = keep.astype(f32) + flipped(send, bits()[order[len(order) - 1 - step]]).astype(f32)
+    return x if step == len(order) - 1 else x.astype(bf16)
+
+
+def fold_step(x, order, step):
+    return fold_sum(fold_split(x, order, step), order, step)
 
 
 def after(x, *first):
@@ -635,15 +650,17 @@
     cut = 2 * inner
     order_a, order_b = orders()
     last = len(order_a)
-    w_part = swap(proj_weight.transpose(1, 0, 2).reshape(-1, 4 * inner))
-    w_out = lax.all_gather(swap(out_weight.T), ("dq", "mp"), axis=0, tiled=True)
+    w_part = swap(proj_weight.reshape(4, -1, 2, inner // 2).transpose(1, 2, 0, 3).reshape(-1, 4 * inner))
+    w_out = swap(out_weight.T)
     w_a = spread(w_part[:, :cut], order_a, range(1))
     w_b = spread(w_part[:, cut:], order_b, range(1))
 
     ids = jnp.concatenate([time_ids, class_ids, image_patches])[None]
-    ids = after(ids, w_part)
+    ids = after(ids, w_part, w_out)
+    w_out = lax.all_gather(w_out, ("dq", "mp"), axis=0, tiled=True)
     ids = lax.all_to_all(jnp.broadcast_to(ids, (2 * dq, ids.shape[1])), COLUMNS, split_axis=0, concat_axis=0, tiled=True)
     ids = after(ids, w_a, w_b)
+    away = across(after(out_grad, w_a, w_b))
     w_a = spread(w_a, order_a, range(1, last - 2))
     w_b = spread(w_b, order_b, range(1, last - 2))
 
@@ -669,19 +686,6 @@
     hidden_away = other(hidden)
     hidden_all = jnp.concatenate([hidden, hidden_away], axis=0)
 
-    away = lax.ppermute(out_grad, "mp", FLIP)
-    straight = core == y
-    g_rows = jnp.where(straight, out_grad, other(away))
-    g_away = jnp.where(straight, other(out_grad), away)
-    w_a = spread(after(w_a, x, away), order_a, range(last - 2, last - 1))
-    w_b = spread(after(w_b, x, away), order_b, range(last - 2, last - 1))
-    w_a = spread(after(w_a, received), order_a, range(last - 1, last))
-    w_b = spread(after(w_b, received), order_b, range(last - 1, last))
-    hidden_units = fc1_weight.shape[1]
-    w_rest = jnp.concatenate([fc1_weight, fc2_weight.T], axis=1)
-    w_rest = lax.all_gather(after(w_rest, w_a, w_b), COLUMNS, axis=0, tiled=True)
-    w_fc1, w_fc2 = w_rest[:, :hidden_units], w_rest[:, hidden_units:]
-
     start = core * inner
     up_local = lax.dynamic_slice_in_dim(decay_up, start, inner, 1)
     bias_local = lax.dynamic_slice_in_dim(decay_bias, start, inner, 0)
@@ -694,13 +698,25 @@
     gain_pad = jnp.pad(head_gain.astype(f32), (0, LANES - HDIM))[None]
     turn = (core * (rows // ROWS)).astype(jnp.int32)[None]
 
+    straight = core == y
+    g_rows = jnp.where(straight, out_grad, other(away))
+    g_away = jnp.where(straight, other(out_grad), away)
+    w_a = spread(after(w_a, x, away), order_a, range(last - 2, last - 1))
+    w_b = spread(after(w_b, x, away), order_b, range(last - 2, last - 1))
+    w_a = spread(after(w_a, received), order_a, range(last - 1, last))
+    w_b = spread(after(w_b, hidden), order_b, range(last - 1, last), (hidden_away, up_pad, bias_pad, taps_pad, down_pad, g_away))
+    hidden_units = fc1_weight.shape[1]
+    w_rest = jnp.concatenate([fc1_weight, fc2_weight.T], axis=1)
+    w_rest = lax.all_gather(after(w_rest, w_a, w_b), COLUMNS, axis=0, tiled=True)
+    w_fc1, w_fc2 = w_rest[:, :hidden_units], w_rest[:, hidden_units:]
+
     grad_rows = g_rows.astype(f32).reshape(own_slots, slot_rows, width)
     grad_feed = (grad_rows * gate2[:, None, :]).astype(bf16).reshape(rows, width)
     gate2_away = across(gate2)
     grad_feed_away = g_away.astype(f32).reshape(own_slots, slot_rows, width) * gate2_away[:, None, :]
     grad_feed_away = grad_feed_away.astype(bf16).reshape(rows, width)
     qkvg, pre, latent = project(turn, hidden, hidden_away, w_a, w_b, down_pad, up_pad, bias_pad, heads)
-    mixed, comb, scores, states = gla_forward(patches, qkvg, pre, taps_pad, gain_pad)
+    mixed, comb, scores, states = gla_forward(after(patches, grad_feed_away, grad_feed), qkvg, pre, taps_pad, gain_pad)
     attn_own, attn_away, mixed_cat = attend(turn, mixed, w_out)
     attention = (attn_own + other(attn_away)).reshape(own_slots, slot_rows, width)
     after_attn = residual + gate1[:, None, :] * attention
@@ -721,14 +737,14 @@
     grad_hidden_two = across(grad_hidden_two_part)
     grad_feed_all = jnp.concatenate([grad_feed, grad_feed_away], axis=0)
     hidden_two_all = jnp.concatenate([hidden_two, hidden_two_away], axis=0)
-    active_all = jnp.concatenate([active, active_away], axis=0)
-    grad_up_all = jnp.concatenate([grad_up, grad_up_away], axis=0)
+    active_all = after(jnp.concatenate([active, active_away], axis=0), grad_hidden_two_part)
+    grad_up_all = after(jnp.concatenate([grad_up, grad_up_away], axis=0), grad_hidden_two_part)
     feed_away = across(after(contract(active_away, w_fc2, 1, 1).astype(bf16), grad_hidden_two_part))
     grad_fc2 = contract(grad_feed_all, active_all, 0, 0).astype(bf16)
     fc2_grad = lax.psum_scatter(grad_fc2, COLUMNS, scatter_dimension=0, tiled=True).astype(f32).T
     grad_fc1 = contract(hidden_two_all, grad_up_all, 0, 0).astype(bf16)
     fc1_grad = lax.psum_scatter(grad_fc1, COLUMNS, scatter_dimension=0, tiled=True).astype(f32)
-    grad_hidden_two = grad_hidden_two_own + after(grad_hidden_two, grad_fc1).astype(f32)
+    grad_hidden_two = grad_hidden_two_own + after(grad_hidden_two, grad_fc1, grad_fc2).astype(f32)
 
     grad_after, grad_shift_two, grad_scale_two = norm_back_two(grad_hidden_two.reshape(own_slots, slot_rows, width))
     grad_after = grad_after + grad_rows
@@ -736,74 +752,95 @@
     grad_attn_all = both((grad_after * gate1[:, None, :]).astype(bf16).reshape(rows, width))
     grad_mixed = attend_back(turn, grad_attn_all, w_out, heads)
     grad_out = contract(grad_attn_all, mixed_cat, 0, 0).astype(bf16)
-    out_step = fold_step(grad_out, order_a, 0)
-    d_qkvg, d_pre, d_taps, d_vec = gla_backward(
-        after(patches, grad_out), qkvg, pre, comb, scores, states, grad_mixed, taps_pad, gain_pad
-    )
-    feed_out = feed_own + after(feed_away, d_qkvg).astype(f32)
+    grad_out = lax.psum_scatter(grad_out, ("dq", "mp"), scatter_dimension=0, tiled=True)
+    kept = (qkvg, pre, comb, scores, states, grad_mixed, taps_pad, gain_pad)
+    d_qkvg_a, d_pre_a, d_taps_a, d_vec_a = gla_backward(0, heads // 2, patches, *kept)
+    cat_a = join(turn, d_qkvg_a)
+    split_a = fold_split(contract(hidden_all, cat_a, 0, 0).astype(bf16), order_a, 0)
+    d_qkvg_b, d_pre_b, d_taps_b, d_vec_b = gla_backward(heads // 2, heads // 2, after(patches, *split_a), *kept)
+    sum_a = fold_sum(split_a, order_a, 0, (d_qkvg_b,))
+    feed_out = feed_own + after(feed_away, d_qkvg_b).astype(f32)
     feed_out = feed_out.reshape(own_slots, slot_rows, width)
     block_out = (after_attn + gate2[:, None, :] * feed_out).reshape(rows, width).astype(bf16)
     grad_gate_two = jnp.sum(grad_rows * feed_out, axis=1)
-    cat_a, cat_b = join(after(turn, out_step), d_qkvg)
-    part_b = contract(hidden_all, cat_b, 0, 0).astype(bf16)
-    part_a = contract(hidden_all, cat_a, 0, 0).astype(bf16)
-    b_step = fold_step(part_b, order_b, 0)
-    a_step = fold_step(part_a, order_a, 0)
+    cat_b = join(after(turn, sum_a), d_qkvg_b)
+    split_b = fold_split(contract(hidden_all, cat_b, 0, 0).astype(bf16), order_a, 0)
+    split_a = fold_split(sum_a, order_a, 1)
     hidden_own, hidden_far, d_down, d_up = project_back(
-        after(turn, part_a, part_b), hidden_all, cat_a, cat_b, d_pre, latent, w_a, w_b, down_pad, up_pad
+        after(turn, *split_a, *split_b), hidden_all, cat_a, cat_b, d_pre_a, d_pre_b, latent, w_a, w_b, down_pad, up_pad
     )
     hidden_sum = (hidden_own + other(hidden_far)).reshape(own_slots, slot_rows, width)
     grad_residual, grad_shift_one, grad_scale_one = norm_back_one(hidden_sum)
+    input_grad = (grad_residual + grad_after).reshape(rows, width)
+
     grad_mod = jnp.concatenate(
         [grad_shift_one, grad_scale_one, grad_gate_one, grad_shift_two, grad_scale_two, grad_gate_two], axis=1
-    ).astype(bf16)
-    grad_mod = grad_mod.reshape(own_slots, 2 * dq, part).transpose(1, 0, 2)
-    got = lax.all_to_all(grad_mod, COLUMNS, split_axis=0, concat_axis=0, tiled=True).reshape(dq, 1, unit_slots, part)
-    gates = {2: (grad_mod,), 1: (got,)}
-    sums_b = folded_in(b_step, order_b, gates)
-    sums_a = folded_in(a_step, order_a, gates)
-    sums_out = folded_in(out_step, order_a, {len(order_a) - 1: (sums_b[0],), len(order_a) - 2: (sums_b[1],)})
-    block_out = swap(after(block_out, sums_b[0]))
-    grad_back = swap(jnp.concatenate([sums_a[-1], sums_b[-1], sums_out[-1]], axis=1))
-    input_grad = swap(after(after((grad_residual + grad_after).reshape(rows, width), sums_a[1]), sums_b[1]))
-
-    d_down = d_down[:, :lowrank]
+    )
+    grad_mod = grad_mod.reshape(own_slots, 2 * dq, part).transpose(1, 0, 2).reshape(2 * dq, own_slots * part)
 
     def placed(value):
         return lax.dynamic_update_slice_in_dim(jnp.zeros((value.shape[0], width), f32), value, start, 1)
 
-    d_up = d_up[:, :lowrank, :HDIM].transpose(1, 0, 2).reshape(lowrank, inner)
+    d_vec = jnp.concatenate([d_vec_a, d_vec_b], axis=0)
+    d_taps = jnp.concatenate([d_taps_a, d_taps_b], axis=0)
+    d_down = d_down[:lowrank].T
+    d_up = d_up[:lowrank].reshape(lowrank, heads, LANES)[:, :, :HDIM].reshape(lowrank, inner)
     d_taps = d_taps[:, :9, :HDIM].transpose(1, 0, 2).reshape(9, inner)
     d_bias = d_vec[:, 1, :HDIM].reshape(1, inner)
     d_gain = jnp.sum(d_vec[:, 0, :HDIM], axis=0)
     stacked = placed(jnp.concatenate([d_up, d_taps, d_bias], axis=0))
     flat = jnp.concatenate([d_down.reshape(lowrank, width), stacked, jnp.pad(d_gain, (0, width - HDIM))[None]], axis=0)
-    flat = flat + other(flat)
-    for step, bit in enumerate(bits()):
-        flat = after(flat, (sums_a, sums_b)[step % 2][step // 2])
-        flat = flat + flipped(flat, bit)
+    flat_rows = flat.shape[0]
+    flat = flat.reshape(-1)
+    flat = jnp.pad(flat, (0, -flat.shape[0] % (2 * dq))).reshape(2 * dq, -1)
+    packed = jnp.concatenate([grad_mod, flat], axis=1)
+
+    names = bits()
+    sum_b = fold_sum(split_b, order_a, 0, (packed, input_grad))
+    sum_a = fold_sum(split_a, order_a, 1, (packed, input_grad))
+    got = lax.all_to_all(packed, COLUMNS, split_axis=0, concat_axis=0, tiled=True)
+    split_b = fold_split(sum_b, order_a, 1)
+    split_a = fold_split(after(sum_a, sum_b), order_a, 2)
+    sum_b = fold_sum(split_b, order_a, 1, (got,))
+    sum_a = fold_sum(split_a, order_a, 2, (got,))
+    flat = jnp.sum(got[:, own_slots * part :], axis=0)
+    got = jnp.concatenate([got[:, : own_slots * part].reshape(-1), flat])
+    away = lax.ppermute(got, "mp", FLIP)
+    count = 2 * dq * own_slots * part
+    flat = flat + away[count:]
+    got = jnp.where(y == 0, jnp.stack([got[:count], away[:count]]), jnp.stack([away[:count], got[:count]]))
+    got = got.reshape(2, dq, unit_slots, part).transpose(1, 0, 2, 3).reshape(2 * dq, unit_slots, part)
+    folded = jnp.sum(got, axis=1, keepdims=True)
+    first = jnp.arange(unit_slots)[None, :, None] == 0
+    got = jnp.where(big_all[:, None, None], jnp.where(first, folded, 0.0), got).reshape(-1, part)
+    grad_silu = jnp.dot(got, ada_weight.astype(f32).T, precision=lax.Precision.HIGHEST, preferred_element_type=f32)
+    packed = jnp.concatenate(
+        [grad_silu.reshape(2 * dq, unit_slots * width), jnp.broadcast_to(flat[None], (2 * dq, flat.shape[0]))], axis=1
+    )
+    split_b = fold_split(sum_b, order_a, 2)
+    split_a = fold_split(after(sum_a, sum_b), order_a, 3)
+    block_out = swap(after(block_out, sum_b))
+    input_grad = swap(after(input_grad, sum_b))
+    sum_b = fold_sum(split_b, order_a, 2, (packed,))
+    sum_a = fold_sum(split_a, order_a, 3, (packed,))
+    packed = lax.all_to_all(packed, COLUMNS, split_axis=0, concat_axis=0, tiled=True)
+    ada_bias_grad = jnp.sum(got, axis=0)
+    ada_weight_grad = jnp.dot(silu_all.astype(f32).T, got, precision=lax.Precision.HIGHEST, preferred_element_type=f32)
+    sum_b = fold_step(sum_b, order_a, 3)
+    for step in range(4, last):
+        sum_a, sum_b = fold_step(sum_a, order_a, step), fold_step(sum_b, order_a, step)
+    grad_back = swap(jnp.concatenate([sum_a, sum_b, grad_out.astype(f32)], axis=1))
+    flat = packed[:, unit_slots * width :].reshape(-1)[: flat_rows * width].reshape(flat_rows, width)
     down_sum = flat[:lowrank].reshape(width, lowrank)
     up_sum = flat[lowrank : 2 * lowrank]
     taps_sum = flat[2 * lowrank : 2 * lowrank + 9]
     bias_sum = flat[2 * lowrank + 9]
     gain_sum = flat[2 * lowrank + 10, :HDIM]
-
-    away = lax.ppermute(got, "mp", FLIP)
-    got = jnp.where(y == 0, jnp.concatenate([got, away], axis=1), jnp.concatenate([away, got], axis=1))
-    got = got.reshape(2 * dq, unit_slots, part).astype(f32)
-    folded = jnp.sum(got, axis=1, keepdims=True)
-    first = jnp.arange(unit_slots)[None, :, None] == 0
-    got = jnp.where(big_all[:, None, None], jnp.where(first, folded, 0.0), got).reshape(-1, part)
-    ada_bias_grad = jnp.sum(got, axis=0)
-    ada_weight_grad = jnp.dot(silu_all.astype(f32).T, got, precision=lax.Precision.HIGHEST, preferred_element_type=f32)
-    grad_silu = jnp.dot(got, ada_weight.astype(f32).T, precision=lax.Precision.HIGHEST, preferred_element_type=f32)
-    grad_silu = lax.all_to_all(grad_silu, COLUMNS, split_axis=0, concat_axis=0, tiled=True)
-    grad_silu = jnp.sum(grad_silu.reshape(2 * dq, unit_slots, width), axis=0)
+    grad_silu = jnp.sum(packed[:, : unit_slots * width].reshape(2 * dq, unit_slots, width), axis=0)
     own_cond = lax.dynamic_slice_in_dim(condition, (2 * lax.axis_index("dq") + core) * unit_slots, unit_slots, 0)
     gate = jax.nn.sigmoid(own_cond)
     cond_grad = grad_silu * (gate * (1.0 + own_cond * (1.0 - gate)))
-
-    proj_grad = grad_back[:, : 4 * inner].reshape(-1, 4, inner).transpose(1, 0, 2)
+    proj_grad = grad_back[:, : 4 * inner].reshape(-1, 2, 4, inner // 2).transpose(2, 0, 1, 3).reshape(4, -1, inner)
     return (
         block_out, input_grad, cond_grad, ada_weight_grad, ada_bias_grad, proj_grad, down_sum, up_sum, bias_sum,
         gain_sum, taps_sum, grad_back[:, 4 * inner :].T, fc1_grad, fc2_grad,

time: 727 us -> 666 us (0.916)
  Pallas kernels: 189 us -> 167 us
  local copies, waits for them, and re-layouts: 96.1 us -> 80.2 us
  waiting for transfers between devices: 139 us -> 127 us
  other arithmetic: 90.1 us -> 78.8 us
  starting transfers between devices: 82.8 us -> 73.8 us
    ppermute x4 -> x5, waiting for transfers between devices: 9.81 us -> 41.8 us  [across(): return lax.ppermute(x, 'mp', FLIP)]
    ppermute x6, waiting for transfers between devices: 31.7 us -> 0.02 us  [swap(): away = lax.ppermute(x, ('core', 'mp'), [(1, 2), (2, 1)])]
    pallas_call x1, Pallas kernels: 65.1 us -> 42.1 us  [gla_forward(): pl.pallas_call(functools.partial(fwd_kernel, PS, PA, total), grid=(H,), i...]
    ppermute x24 -> x16, waiting for transfers between devices: 68 us -> 50.9 us  [flipped(): lax.ppermute(x, axis, [(i, i ^ 1 << place) for i in range(lax.axis_size(a...]
    slice x25 -> x39, local copies, waits for them, and re-layouts: 16.5 us -> 28.5 us  [after(): marks = sum((f[(0,) * f.ndim].astype(f32) for f in first))]
    select_n x21 -> x14, other arithmetic: 24.7 us -> 14.4 us  [after(): return jnp.where(jnp.isnan(marks), jnp.zeros_like(x), x)]
    ppermute x6, starting transfers between devices: 28.7 us -> 20.4 us  [swap(): away = lax.ppermute(x, ('core', 'mp'), [(1, 2), (2, 1)])]
    ppermute x24 -> x16, starting transfers between devices: 23.8 us -> 17.6 us  [flipped(): lax.ppermute(x, axis, [(i, i ^ 1 << place) for i in range(lax.axis_size(a...]
  transfers between devices with their start and end apart: 51 -> 43, of which waited for: 16 -> 16; matrix products, arithmetic and copies ran while one was open for 30% -> 28% of each run, Pallas kernels for 26% -> 25%
where the time goes in v3:
time: 666 us; the launch traced here: 654 us
  Pallas kernels  167 us (25%)
  waiting for transfers between devices  127 us (19%)
  local copies, waits for them, and re-layouts  80.2 us (12%)
  other arithmetic  78.8 us (12%)
  matrix products  78.6 us (12%)
  starting transfers between devices  73.8 us (11%)
  between operations  49.2 us (7%)
    pallas_call x2, Pallas kernels, gla_backward(): pl.pallas_call(functools.partial(bwd_kernel, PS, PA, total), grid=(count,...  76.9 us
    ppermute x16, waiting for transfers between devices, flipped(): lax.ppermute(x, axis, [(i, i ^ 1 << place) for i in range(lax.axis_size(a...  50.9 us
    dot_general x9, matrix products, contract(): lax.dot_general(a, b, (((i,), (j,)), ((), ())), preferred_element_type=f32)  50.2 us
    pallas_call x1, Pallas kernels, gla_forward(): pl.pallas_call(functools.partial(fwd_kernel, PS, PA, total), grid=(H,), i...  42.1 us
    ppermute x5, waiting for transfers between devices, across(): return lax.ppermute(x, 'mp', FLIP)  41.8 us
    slice x39, local copies, waits for them, and re-layouts, after(): marks = sum((f[(0,) * f.ndim].astype(f32) for f in first))  28.5 us
    unnamed x207, local copies, waits for them, and re-layouts  26.1 us
    ppermute x6, starting transfers between devices, swap(): away = lax.ppermute(x, ('core', 'mp'), [(1, 2), (2, 1)])  20.4 us
  transfers between devices with their start and end apart: 43, of which 16 were waited for; matrix products, arithmetic and copies ran while one was open for 28% of the time, Pallas kernels for 25%

profile of v3, /device:TPU:1, one launch (start us, length us, event | category | flops | bytes accessed | tf_op | source)
XLA Modules:
  0.0 654.5 jit_solution(16048170572090038113)
XLA Ops:
  9.3 4.5 collective-permute-start.1
  15.8 3.6 collective-permute-start
  20.2 2.4 collective-permute-start.4
  26.6 3.9 all-to-all-start
  31.1 2.3 collective-permute-start.2
  35.3 6.3 collective-permute-done.2
  44.7 2.8 gather_fusion
  50.3 2.4 broadcast_select_fusion.3
  55.3 3.0 collective-permute-done.3
  60.9 7.5 %all-to-all-start.1 = ((f32[16,2,432]{2,1,0:T(2,128)}), f32[16,2,432]{2,1,0:T(2,128)S(1)}, u32[]{:S(2)}, u32[]{:S(2)}) async-start(f32[16,2,432]{2,1,0:T(2,128)} %bitcast.14), calls=%async_computation.1 | async-start | bytes 131072 | tf_op jit(solution)/shard_map/all_to_all | solution.py:680
  68.6 5.8 all-to-all-done.1
  85.1 12.0 %collective-permute-done.9 = bf16[2,2,72,1152]{3,2,0,1:T(8,128)(2,1)S(1)} collective-permute-done((bf16[2,2,72,1152]{3,2,0,1:T(8,128)(2,1)S(1)}, bf16[2,2,72,1152]{3,2,0,1:T(8,128)(2,1)S(1)}, u32[]{:S(2)}, u32[]{:S(2)}) %collective-permute-start.9) | collective-permute-done | bytes 663584 | tf_op jit(solution)/shard_map/ppermute | solution.py:567
  102.7 2.8 collective-permute-start.7
  113.4 26.8 %collective-permute-done.14 = f32[2,1152]{1,0:T(2,128)} collective-permute-done((f32[2,1152]{1,0:T(2,128)S(1)}, f32[2,1152]{1,0:T(2,128)}, u32[]{:S(2)}, u32[]{:S(2)}) %collective-permute-start.14) | collective-permute-done | bytes 9248 | tf_op jit(solution)/shard_map/ppermute | solution.py:557
  140.3 2.7 fusion.70
  151.5 2.1 select_bitcast_fusion.1
  162.1 2.7 fusion.55
  167.3 16.2 %project.1 = (f32[4,8,1024,128]{3,2,1,0:T(8,128)}, f32[8,1024,128]{2,1,0:T(8,128)}, f32[1024,128]{1,0:T(8,128)}) custom-call(s32[1]{0:T(128)} %bitcast.18.turn_ref, bf16[512,1152]{1,0:T(8,128)(2,1)} %fusion.54.x_ref, bf16[512,1152]{1,0:T(8,128)(2,1)} %collective-permute-done.7.y_ref, bf16[1152,1152]{1,0:T(8,128)(2,1)} %bitcast.256, ...), custom_call_target="tpu_custom_call" | custom-call | flops 13500000256 | bytes 1000000 | tf_op jit(solution)/shard_map/project/pallas_call | solution.py:380
  183.5 42.1 %gla_forward.1 = (bf16[8,1024,128]{2,1,0:T(8,128)(2,1)S(1)}, f32[8,1024,128]{2,1,0:T(8,128)S(1)}, f32[8,8,128,128]{3,2,1,0:T(8,128)S(1)}, f32[8,8,128,128]{3,2,1,0:T(8,128)}) custom-call(s32[1]{0:T(128)S(6)} %select_n.499.big_ref, f32[4,8,1024,128]{3,2,1,0:T(8,128)} %get-tuple-element.36.q_ref.k_ref.v_ref.g_ref, ...), custom_call_target="tpu_custom_call" | custom-call | flops 58500001792 | bytes 1000000 | tf_op jit(solution)/shard_map/gla_forward/pallas_call | solution.py:165
  233.7 3.4 attend.1
  237.6 4.2 collective-permute-done.16
  246.1 2.1 collective-permute-start.17
  248.1 13.3 %all-gather.3.cloned.1.call-done = bf16[1152,4608]{1,0:T(8,128)(2,1)} async-done(((bf16[72,4608]{1,0:T(8,128)(2,1)}), bf16[1152,4608]{1,0:T(8,128)(2,1)}) %all-gather.3.cloned.1.call-update) | async-done | bytes 10616848 | tf_op jit(solution)/shard_map/all_gather | solution.py:710
  261.5 6.9 %multiply_convert_fusion.1 = (bf16[512,2304]{1,0:T(8,128)(2,1)S(1)}, f32[512,2304]{1,0:T(8,128)S(1)}) fusion(bf16[512,1152]{1,0:T(8,128)(2,1)} %fusion.61, bf16[1152,4608]{1,0:T(8,128)(2,1)} %all-gather.3.cloned.1.call-done), kind=kOutput, calls=%fused_computation.31 | convolution fusion | flops 2728525824 | bytes 13565952 | tf_op jit(solution)/shard_map/dot_general | solution.py:728
  268.4 5.9 fusion.6
  274.3 3.2 fusion.32
  278.1 3.2 fusion.24
  283.4 3.8 multiply_convert_fusion
  287.2 5.7 fusion.13
  293.0 4.3 fusion.43
  300.8 7.7 %convolution_convert_fusion = bf16[1152,2304]{1,0:T(8,128)(2,1)} fusion(bf16[512,2304]{1,0:T(8,128)(2,1)S(1)} %get-tuple-element.166, bf16[512,2304]{1,0:T(8,128)(2,1)S(1)} %get-tuple-element.164, pred[]{:T(512)} %bitcast.51, bf16[512,1152]{1,0:T(8,128)(2,1)S(1)} %copy-done.49, bf16[512,1152]{1,0:T(8,128)(2,1)S(1)} %copy-done.52), kind=kOutput, calls=%fused_computation.2 | convolution fusion | flops 5454987264 | bytes 12386305 | tf_op jit(solution)/shard_map/dot_general | solution.py:629
  309.7 10.5 %convolution_convert_fusion.1 = bf16[1152,2304]{1,0:T(8,128)(2,1)} fusion(bf16[512,2304]{1,0:T(8,128)(2,1)} %copy-done.94, bf16[512,2304]{1,0:T(8,128)(2,1)} %copy-done.91, pred[]{:T(512)} %bitcast.51, bf16[512,1152]{1,0:T(8,128)(2,1)} %copy-done.48, bf16[512,1152]{1,0:T(8,128)(2,1)} %fusion.61), kind=kOutput, calls=%fused_computation.3 | convolution fusion | flops 5454987264 | bytes 12386305 | tf_op jit(solution)/shard_map/dot_general | solution.py:629
  322.6 3.4 collective-permute-done.18
  326.0 3.2 multiply_reduce_fusion.2
  333.1 2.5 collective-permute-done.19
  336.6 3.2 convolution_convert_fusion.4
  342.7 3.2 pad_maximum_fusion.2.x_ref
  348.0 4.3 attend_back.1.gm_ref
  354.3 38.7 %gla_backward.2 = (bf16[4,4,1024,128]{3,2,1,0:T(8,128)(2,1)}, f32[4,1024,128]{2,1,0:T(8,128)S(1)}, f32[4,16,128]{2,1,0:T(8,128)S(1)}, f32[4,8,128]{2,1,0:T(8,128)S(1)}) custom-call(s32[1]{0:T(128)} %bitcast.19.big_ref, f32[4,8,1024,128]{3,2,1,0:T(8,128)} %get-tuple-element.36.q_ref.k_ref.v_ref.g_ref, ...), custom_call_target="tpu_custom_call" | custom-call | flops 35999997952 | bytes 1000000 | tf_op jit(solution)/shard_map/gla_backward/pallas_call | solution.py:289
  393.0 3.0 copy-done.10
  397.8 5.8 convolution_convert_fusion.3
  407.2 38.2 %gla_backward.3 = (bf16[4,4,1024,128]{3,2,1,0:T(8,128)(2,1)}, f32[4,1024,128]{2,1,0:T(8,128)S(1)}, f32[4,16,128]{2,1,0:T(8,128)S(1)}, f32[4,8,128]{2,1,0:T(8,128)S(1)}) custom-call(s32[1]{0:T(128)S(6)} %select_n.512.big_ref, f32[4,8,1024,128]{3,2,1,0:T(8,128)} %get-tuple-element.36.q_ref.k_ref.v_ref.g_ref, ...), custom_call_target="tpu_custom_call" | custom-call | flops 35999997952 | bytes 1000000 | tf_op jit(solution)/shard_map/gla_backward/pallas_call | solution.py:289
  450.2 2.2 copy-done.8
  457.1 4.9 convolution_convert_fusion.2
  467.3 20.0 %project_back.1 = (f32[512,1152]{1,0:T(8,128)}, f32[512,1152]{1,0:T(8,128)}, f32[128,1152]{1,0:T(8,128)}, f32[128,1024]{1,0:T(8,128)}) custom-call(s32[1]{0:T(128)S(6)} %select_n.520.turn_ref, bf16[1024,1152]{1,0:T(8,128)(2,1)} %pad_maximum_fusion.2.x_ref, bf16[1024,1152]{1,0:T(8,128)(2,1)} %copy-done.2, bf16[1024,1152]{1,0:T(8,128)(2,1)} %copy-done.3, ...), custom_call_target="tpu_custom_call" | custom-call | flops 1800000000 | bytes 1000000 | tf_op jit(solution)/shard_map/project_back/pallas_call | solution.py:501
  488.0 7.5 %fusion.46 = bf16[512,1152]{1,0:T(8,128)(2,1)} fusion(bf16[512,2304]{1,0:T(8,128)(2,1)S(1)} %copy-done.93, bf16[1152,4608]{1,0:T(8,128)(2,1)} %all-gather.3.cloned.1.call-done, pred[]{:T(512)} %bitcast.51), kind=kOutput, calls=%fused_computation.64 | convolution fusion | flops 2719088640 | bytes 8847872 | tf_op jit(solution)/shard_map/dot_general | solution.py:629
  503.2 3.0 multiply_reduce_fusion
  507.9 2.2 add_add_fusion.3
  512.1 11.2 %collective-permute-done.22 = bf16[512,1152]{1,0:T(8,128)(2,1)} collective-permute-done((bf16[512,1152]{1,0:T(8,128)(2,1)}, bf16[512,1152]{1,0:T(8,128)(2,1)}, u32[]{:S(2)}, u32[]{:S(2)}) %collective-permute-start.22) | collective-permute-done | bytes 1179680 | tf_op jit(solution)/shard_map/ppermute | solution.py:557
  523.3 4.7 fusion.69
  530.2 4.2 collective-permute-done.23
  534.4 2.1 add_convert_fusion
  539.3 6.4 all-to-all-start.2
  548.0 7.0 %all-to-all-done.2 = f32[16,1,3960]{2,1,0:T(1,128)S(1)} async-done(((f32[16,1,3960]{2,1,0:T(1,128)}), f32[16,1,3960]{2,1,0:T(1,128)S(1)}, u32[]{:S(2)}, u32[]{:S(2)}) %all-to-all-start.2) | async-done | bytes 253472 | tf_op jit(solution)/shard_map/all_to_all | solution.py:801
  566.8 4.5 all-to-all-start.3
  572.7 2.3 fusion.90
  579.5 2.4 collective-permute-start.30
  585.0 3.9 collective-permute-start.25
  588.9 3.2 broadcast_select_fusion.1
  594.1 15.3 %collective-permute-done.31 = bf16[2,72,1152]{2,1,0:T(8,128)(2,1)S(1)} collective-permute-done((bf16[2,72,1152]{2,1,0:T(8,128)(2,1)S(1)}, bf16[2,72,1152]{2,1,0:T(8,128)(2,1)S(1)}, u32[]{:S(2)}, u32[]{:S(2)}) %collective-permute-start.31) | collective-permute-done | bytes 331808 | tf_op jit(solution)/shard_map/ppermute | solution.py:567
  610.4 10.1 %collective-permute-done.32 = bf16[72,1152]{1,0:T(8,128)(2,1)S(1)} collective-permute-done((bf16[72,1152]{1,0:T(8,128)(2,1)S(1)}, bf16[72,1152]{1,0:T(8,128)(2,1)S(1)}, u32[]{:S(2)}, u32[]{:S(2)}) %collective-permute-start.32) | collective-permute-done | bytes 165920 | tf_op jit(solution)/shard_map/ppermute | solution.py:567
  621.6 4.5 collective-permute-start.33
  631.3 2.4 broadcast_select_fusion.5
  643.4 4.1 broadcast_select_fusion.4
  (482 shorter events, 145.6 us)
Async XLA Ops:
  7.2 36.8 %copy-start = (bf16[1001,1152]{1,0:T(8,128)(2,1)S(1)}, bf16[1001,1152]{1,0:T(8,128)(2,1)}, u32[]{:S(2)}) copy-start(bf16[1001,1152]{1,0:T(8,128)(2,1)} %param.21) | copy-start | bytes 6918916
  7.2 18.7 %copy-start.87 = (s32[4]{0:T(128)S(1)}, s32[4]{0:T(128)}, u32[]{:S(2)}) copy-start(s32[4]{0:T(128)} %param.23) | copy-start | bytes 52
  7.2 18.7 %copy-start.88 = (s32[4]{0:T(128)S(1)}, s32[4]{0:T(128)}, u32[]{:S(2)}) copy-start(s32[4]{0:T(128)} %param.22) | copy-start | bytes 52
  9.3 10.8 %collective-permute-start.1 = (bf16[72,2304]{1,0:T(8,128)(2,1)S(1)}, bf16[72,2304]{1,0:T(8,128)(2,1)S(1)}, u32[]{:S(2)}, u32[]{:S(2)}) collective-permute-start(bf16[72,2304]{1,0:T(8,128)(2,1)S(1)} %reshape.574), channel_id=1, source_target_pairs={{1,2},{2,1},{5,6},{6,5},{9,10},{10,9},{13,14},{14,13},{17,18},{18,... | collective-permute-start | bytes 995336 | tf_op jit(solution)/shard_map/ppermute | solution.py:539
  13.9 8.7 %collective-permute-start.6 = (bf16[72,576]{1,0:T(8,128)(2,1)S(1)}, bf16[72,576]{1,0:T(8,128)(2,1)}, u32[]{:S(2)}, u32[]{:S(2)}) collective-permute-start(bf16[72,576]{1,0:T(8,128)(2,1)S(1)} %bitcast.288), channel_id=1, source_target_pairs={{1,2},{2,1},{5,6},{6,5},{9,10},{10,9},{13,14},{14,13},{17,18},{18,... | collective-permute-start | bytes 248840 | tf_op jit(solution)/shard_map/ppermute | solution.py:539
  15.8 61.2 %collective-permute-start = (bf16[512,1152]{1,0:T(8,128)(2,1)}, bf16[512,1152]{1,0:T(8,128)(2,1)}, u32[]{:S(2)}, u32[]{:S(2)}) collective-permute-start(bf16[512,1152]{1,0:T(8,128)(2,1)} %param.18), channel_id=1, source_target_pairs={{1,2},{2,1},{5,6},{6,5},{9,10},{10,9},{13,14},{14,13},{17,18},{18,... | collective-permute-start | bytes 3538952 | tf_op jit(solution)/shard_map/ppermute | solution.py:539
  20.2 10.3 %collective-permute-start.4 = (bf16[72,1152]{1,0:T(8,128)(2,1)S(1)}, bf16[72,1152]{1,0:T(8,128)(2,1)S(1)}, u32[]{:S(2)}, u32[]{:S(2)}) collective-permute-start(bf16[72,1152]{1,0:T(8,128)(2,1)S(1)} %slice.286), channel_id=1, source_target_pairs={{0,16},{4,20},{8,24},{12,28},{16,0},{20,4},{24,8},{28,12},{1,17},{... | collective-permute-start | bytes 497672 | tf_op jit(solution)/shard_map/ppermute | solution.py:567
  26.6 16.8 %all-to-all-start = ((s32[16,1,9]{2,1,0:T(1,128)}), s32[16,1,9]{2,1,0:T(1,128)S(1)}, u32[]{:S(2)}, u32[]{:S(2)}) async-start(s32[16,1,9]{2,1,0:T(1,128)} %broadcast_in_dim.146), calls=%async_computation | async-start | bytes 16384 | tf_op jit(solution)/shard_map/all_to_all | solution.py:661
  31.1 10.5 %collective-permute-start.2 = (bf16[72,1152]{1,0:T(8,128)(2,1)S(1)}, bf16[72,1152]{1,0:T(8,128)(2,1)S(1)}, u32[]{:S(2)}, u32[]{:S(2)}) collective-permute-start(bf16[72,1152]{1,0:T(8,128)(2,1)S(1)} %get-tuple-element.149), channel_id=1, source_target_pairs={{0,16},{4,20},{8,24},{12,28},{16,0},{20,4},{24,8},{28,12},{1,17},{... | collective-permute-start | bytes 497672 | tf_op jit(solution)/shard_map/ppermute | solution.py:567
  34.1 19.5 %collective-permute-start.5 = (bf16[2,72,1152]{2,1,0:T(8,128)(2,1)}, bf16[2,72,1152]{2,1,0:T(8,128)(2,1)}, u32[]{:S(2)}, u32[]{:S(2)}) collective-permute-start(bf16[2,72,1152]{2,1,0:T(8,128)(2,1)} %pad_maximum_fusion.7), channel_id=1, source_target_pairs={{0,8},{4,12},{8,0},{12,4},{16,24},{20,28},{24,16},{28,20},{1,9},{5... | collective-permute-start | bytes 995336 | tf_op jit(solution)/shard_map/ppermute | solution.py:567
  49.6 8.6 %collective-permute-start.3 = (bf16[2,72,1152]{2,1,0:T(8,128)(2,1)S(1)}, bf16[2,72,1152]{2,1,0:T(8,128)(2,1)S(1)}, u32[]{:S(2)}, u32[]{:S(2)}) collective-permute-start(bf16[2,72,1152]{2,1,0:T(8,128)(2,1)S(1)} %pad_maximum_fusion.6), channel_id=1, source_target_pairs={{0,8},{4,12},{8,0},{12,4},{16,24},{20,28},{24,16},{28,20},{1,9},{5... | collective-permute-start | bytes 995336 | tf_op jit(solution)/shard_map/ppermute | solution.py:567
  52.7 27.1 %collective-permute-start.8 = (bf16[512,1152]{1,0:T(8,128)(2,1)}, bf16[512,1152]{1,0:T(8,128)(2,1)}, u32[]{:S(2)}, u32[]{:S(2)}) collective-permute-start(bf16[512,1152]{1,0:T(8,128)(2,1)} %broadcast_select_fusion.3), channel_id=1, source_target_pairs={{0,1},{1,0},{2,3},{3,2},{4,5},{5,4},{6,7},{7,6},{8,9},{9,8},{10,11... | collective-permute-start | bytes 3538952 | tf_op jit(solution)/shard_map/ppermute | solution.py:557
  54.7 29.0 %copy-start.34 = (bf16[2,1,72,1152]{3,2,0,1:T(8,128)(2,1)}, bf16[2,1,72,1152]{3,2,0,1:T(8,128)(2,1)S(1)}, u32[]{:S(2)}) copy-start(bf16[2,1,72,1152]{3,2,0,1:T(8,128)(2,1)S(1)} %get-tuple-element.141) | copy-start | bytes 995332
  54.7 29.0 %copy-start.36 = (bf16[2,1,72,1152]{3,2,0,1:T(8,128)(2,1)}, bf16[2,1,72,1152]{3,2,0,1:T(8,128)(2,1)S(1)}, u32[]{:S(2)}) copy-start(bf16[2,1,72,1152]{3,2,0,1:T(8,128)(2,1)S(1)} %get-tuple-element.142) | copy-start | bytes 995332
  60.9 13.5 %all-to-all-start.1 = ((f32[16,2,432]{2,1,0:T(2,128)}), f32[16,2,432]{2,1,0:T(2,128)S(1)}, u32[]{:S(2)}, u32[]{:S(2)}) async-start(f32[16,2,432]{2,1,0:T(2,128)} %bitcast.14), calls=%async_computation.1 | async-start | bytes 131072 | tf_op jit(solution)/shard_map/all_to_all | solution.py:680
  68.4 162.4 %all-gather.5.cloned.1.call-start = ((), (), s32[]{:S(2)}) async-start(), calls=%async_computation.8 | async-start | bytes 1566720 | tf_op jit(solution)/shard_map/all_gather | solution.py:660
  68.5 71.8 %collective-permute-start.11 = (bf16[512,1152]{1,0:T(8,128)(2,1)}, bf16[512,1152]{1,0:T(8,128)(2,1)}, u32[]{:S(2)}, u32[]{:S(2)}) collective-permute-start(bf16[512,1152]{1,0:T(8,128)(2,1)} %param.19), channel_id=1, source_target_pairs={{0,2},{2,0},{1,3},{3,1},{4,6},{6,4},{5,7},{7,5},{8,10},{10,8},{9,1... | collective-permute-start | bytes 3538952 | tf_op jit(solution)/shard_map/ppermute | solution.py:544
  77.0 22.7 %copy-start.60 = (f32[2,1152]{1,0:T(2,128)}, f32[2,1152]{1,0:T(2,128)S(1)}, u32[]{:S(2)}) copy-start(f32[2,1152]{1,0:T(2,128)S(1)} %get-tuple-element.157) | copy-start | bytes 27652
  77.0 85.1 %copy-start.65 = (f32[2,1152]{1,0:T(2,128)}, f32[2,1152]{1,0:T(2,128)S(1)}, u32[]{:S(2)}) copy-start(f32[2,1152]{1,0:T(2,128)S(1)} %get-tuple-element.155) | copy-start | bytes 27652
  78.7 163.1 %copy-start.18 = (bf16[512,1152]{1,0:T(8,128)(2,1)}, bf16[512,1152]{1,0:T(8,128)(2,1)S(1)}, u32[]{:S(2)}) copy-start(bf16[512,1152]{1,0:T(8,128)(2,1)S(1)} %get-tuple-element.122) | copy-start | bytes 3538948
  82.3 14.8 %collective-permute-start.9 = (bf16[2,2,72,1152]{3,2,0,1:T(8,128)(2,1)S(1)}, bf16[2,2,72,1152]{3,2,0,1:T(8,128)(2,1)S(1)}, u32[]{:S(2)}, u32[]{:S(2)}) collective-permute-start(bf16[2,2,72,1152]{3,2,0,1:T(8,128)(2,1)S(1)} %maximum_select_fusion.6), channel_id=1, source_target_pairs={{0,1},{1,0},{2,3},{3,2},{4,5},{5,4},{6,7},{7,6},{8,9},{9,8},{10,11... | collective-permute-start | bytes 1990664 | tf_op jit(solution)/shard_map/ppermute | solution.py:567
  83.3 16.5 %copy-start.62 = (f32[512]{0:T(512)}, f32[512]{0:T(512)S(1)}, u32[]{:S(2)}) copy-start(f32[512]{0:T(512)S(1)} %broadcast_multiply_fusion.1) | copy-start | bytes 6148
  83.7 16.0 %copy-start.71 = (f32[512]{0:T(512)}, f32[512]{0:T(512)S(1)}, u32[]{:S(2)}) copy-start(f32[512]{0:T(512)S(1)} %multiply_reduce_fusion.4) | copy-start | bytes 6148
  83.8 23.0 %collective-permute-start.12 = (bf16[2,2,72,1152]{3,2,0,1:T(8,128)(2,1)S(1)}, bf16[2,2,72,1152]{3,2,0,1:T(8,128)(2,1)S(1)}, u32[]{:S(2)}, u32[]{:S(2)}) collective-permute-start(bf16[2,2,72,1152]{3,2,0,1:T(8,128)(2,1)S(1)} %maximum_select_fusion.7), channel_id=1, source_target_pairs={{0,4},{4,0},{8,12},{12,8},{16,20},{20,16},{24,28},{28,24},{1,5},{5... | collective-permute-start | bytes 1990664 | tf_op jit(solution)/shard_map/ppermute | solution.py:567
  98.6 50.0 %collective-permute-start.10 = (bf16[2,2,2,72,1152]{4,3,0,1,2:T(8,128)(2,1)}, bf16[2,2,2,72,1152]{4,3,0,1,2:T(8,128)(2,1)}, u32[]{:S(2)}, u32[]{:S(2)}) collective-permute-start(bf16[2,2,2,72,1152]{4,3,0,1,2:T(8,128)(2,1)} %maximum_select_fusion.4), channel_id=1, source_target_pairs={{0,4},{4,0},{8,12},{12,8},{16,20},{20,16},{24,28},{28,24},{1,5},{5... | collective-permute-start | bytes 3981320 | tf_op jit(solution)/shard_map/ppermute | solution.py:567
  102.7 40.9 %collective-permute-start.7 = (bf16[512,1152]{1,0:T(8,128)(2,1)}, bf16[512,1152]{1,0:T(8,128)(2,1)}, u32[]{:S(2)}, u32[]{:S(2)}) collective-permute-start(bf16[512,1152]{1,0:T(8,128)(2,1)} %fusion.54.x_ref), channel_id=1, source_target_pairs={{0,2},{2,0},{1,3},{3,1},{4,6},{6,4},{5,7},{7,5},{8,10},{10,8},{9,1... | collective-permute-start | bytes 3538952 | tf_op jit(solution)/shard_map/ppermute | solution.py:544
  108.3 43.1 %collective-permute-start.13 = (bf16[2,2,2,72,1152]{4,3,0,1,2:T(8,128)(2,1)}, bf16[2,2,2,72,1152]{4,3,0,1,2:T(8,128)(2,1)}, u32[]{:S(2)}, u32[]{:S(2)}) collective-permute-start(bf16[2,2,2,72,1152]{4,3,0,1,2:T(8,128)(2,1)} %maximum_select_fusion.5), channel_id=1, source_target_pairs={{0,1},{1,0},{2,3},{3,2},{4,5},{5,4},{6,7},{7,6},{8,9},{9,8},{10,11... | collective-permute-start | bytes 3981320 | tf_op jit(solution)/shard_map/ppermute | solution.py:567
  109.7 30.6 %collective-permute-start.14 = (f32[2,1152]{1,0:T(2,128)S(1)}, f32[2,1152]{1,0:T(2,128)}, u32[]{:S(2)}, u32[]{:S(2)}) collective-permute-start(f32[2,1152]{1,0:T(2,128)S(1)} %get-tuple-element.155), channel_id=1, source_target_pairs={{0,1},{1,0},{2,3},{3,2},{4,5},{5,4},{6,7},{7,6},{8,9},{9,8},{10,11... | collective-permute-start | bytes 27656 | tf_op jit(solution)/shard_map/ppermute | solution.py:557
  110.3 32.6 %copy-start.80 = (f32[1,8,128]{2,1,0:T(8,128)}, f32[1,8,128]{2,1,0:T(8,128)S(1)}, u32[]{:S(2)}) copy-start(f32[1,8,128]{2,1,0:T(8,128)S(1)} %pad_convert_fusion) | copy-start | bytes 12292
  112.8 30.2 %copy-start.55 = (bf16[16,8,8,128]{3,1,2,0:T(8,128)(2,1)}, bf16[16,8,8,128]{3,1,2,0:T(8,128)(2,1)S(1)}, u32[]{:S(2)}) copy-start(bf16[16,8,8,128]{3,1,2,0:T(8,128)(2,1)S(1)} %copy.123) | copy-start | bytes 786436
  113.4 148.1 %all-gather.3.cloned.1.call-start = ((), (), s32[]{:S(2)}) async-start(), calls=%async_computation.7 | async-start | bytes 11280384 | tf_op jit(solution)/shard_map/all_gather | solution.py:710
  158.4 343.8 %reduce-scatter.10.cloned.1.call-start = ((), (), s32[]{:S(2)}) async-start(), calls=%async_computation.11 | async-start | bytes 1566720
  158.5 3.7 collective-permute-start.15
  164.8 18.7 %copy-start.51 = (bf16[512,1152]{1,0:T(8,128)(2,1)}, bf16[512,1152]{1,0:T(8,128)(2,1)S(1)}, u32[]{:S(2)}) copy-start(bf16[512,1152]{1,0:T(8,128)(2,1)S(1)} %get-tuple-element.123) | copy-start | bytes 3538948
  237.2 4.6 collective-permute-start.16
  246.1 37.2 %collective-permute-start.17 = (bf16[512,1152]{1,0:T(8,128)(2,1)}, bf16[512,1152]{1,0:T(8,128)(2,1)S(1)}, u32[]{:S(2)}, u32[]{:S(2)}) collective-permute-start(bf16[512,1152]{1,0:T(8,128)(2,1)} %fusion.61), channel_id=1, source_target_pairs={{0,1},{1,0},{2,3},{3,2},{4,5},{5,4},{6,7},{7,6},{8,9},{9,8},{10,11... | collective-permute-start | bytes 3538952 | tf_op jit(solution)/shard_map/ppermute | solution.py:557
  298.4 27.6 %collective-permute-start.18 = (bf16[512,1152]{1,0:T(8,128)(2,1)}, bf16[512,1152]{1,0:T(8,128)(2,1)S(1)}, u32[]{:S(2)}, u32[]{:S(2)}) collective-permute-start(bf16[512,1152]{1,0:T(8,128)(2,1)} %fusion.43), channel_id=1, source_target_pairs={{0,1},{1,0},{2,3},{3,2},{4,5},{5,4},{6,7},{7,6},{8,9},{9,8},{10,11... | collective-permute-start | bytes 3538952 | tf_op jit(solution)/shard_map/ppermute | solution.py:557
  332.0 3.5 collective-permute-start.19
  339.8 293.9 %reduce-scatter.6.cloned.1.call-start = ((), (), s32[]{:S(2)}) async-start(), calls=%async_computation.9 | async-start | bytes 5640192 | tf_op jit(solution)/shard_map/reduce_scatter | solution.py:746
  340.4 296.6 %reduce-scatter.8.cloned.1.call-start = ((), (), s32[]{:S(2)}) async-start(), calls=%async_computation.10 | async-start | bytes 5640192 | tf_op jit(solution)/shard_map/reduce_scatter | solution.py:744
  404.5 43.5 %collective-permute-start.20 = (bf16[2,2,2,72,1152]{4,3,0,1,2:T(8,128)(2,1)S(1)}, bf16[2,2,2,72,1152]{4,3,0,1,2:T(8,128)(2,1)S(1)}, u32[]{:S(2)}, u32[]{:S(2)}) collective-permute-start(bf16[2,2,2,72,1152]{4,3,0,1,2:T(8,128)(2,1)S(1)} %bitcast.270), channel_id=1, source_target_pairs={{0,4},{4,0},{8,12},{12,8},{16,20},{20,16},{24,28},{28,24},{1,5},{5... | collective-permute-start | bytes 3981320 | tf_op jit(solution)/shard_map/ppermute | solution.py:567
  462.3 25.0 %copy-start.25 = (bf16[2,2,1,2,72,1152]{5,4,3,2,1,0:T(8,128)(2,1)}, bf16[2,2,1,2,72,1152]{5,4,3,2,1,0:T(8,128)(2,1)S(1)}, u32[]{:S(2)}) copy-start(bf16[2,2,1,2,72,1152]{5,4,3,2,1,0:T(8,128)(2,1)S(1)} %get-tuple-element.127) | copy-start | bytes 3981316
  467.3 20.7 %copy-start.93 = (bf16[512,2304]{1,0:T(8,128)(2,1)S(1)}, bf16[512,2304]{1,0:T(8,128)(2,1)}, u32[]{:S(2)}) copy-start(bf16[512,2304]{1,0:T(8,128)(2,1)} %copy-done.92) | copy-start | bytes 7077892
  487.3 15.8 %collective-permute-start.21 = (f32[512,1152]{1,0:T(8,128)}, f32[512,1152]{1,0:T(8,128)}, u32[]{:S(2)}, u32[]{:S(2)}) collective-permute-start(f32[512,1152]{1,0:T(8,128)} %get-tuple-element.50), channel_id=1, source_target_pairs={{0,2},{2,0},{1,3},{3,1},{4,6},{6,4},{5,7},{7,5},{8,10},{10,8},{9,1... | collective-permute-start | bytes 7077896 | tf_op jit(solution)/shard_map/ppermute | solution.py:544
  495.4 27.9 %collective-permute-start.22 = (bf16[512,1152]{1,0:T(8,128)(2,1)}, bf16[512,1152]{1,0:T(8,128)(2,1)}, u32[]{:S(2)}, u32[]{:S(2)}) collective-permute-start(bf16[512,1152]{1,0:T(8,128)(2,1)} %fusion.46), channel_id=1, source_target_pairs={{0,1},{1,0},{2,3},{3,2},{4,5},{5,4},{6,7},{7,6},{8,9},{9,8},{10,11... | collective-permute-start | bytes 3538952 | tf_op jit(solution)/shard_map/ppermute | solution.py:557
  497.6 49.0 %collective-permute-start.28 = (bf16[2,2,72,1152]{3,2,0,1:T(8,128)(2,1)}, bf16[2,2,72,1152]{3,2,0,1:T(8,128)(2,1)}, u32[]{:S(2)}, u32[]{:S(2)}) collective-permute-start(bf16[2,2,72,1152]{3,2,0,1:T(8,128)(2,1)} %get-tuple-element.136), channel_id=1, source_target_pairs={{0,1},{1,0},{2,3},{3,2},{4,5},{5,4},{6,7},{7,6},{8,9},{9,8},{10,11... | collective-permute-start | bytes 1990664 | tf_op jit(solution)/shard_map/ppermute | solution.py:567
  497.8 36.6 %collective-permute-start.23 = (bf16[2,2,2,72,1152]{4,3,0,1,2:T(8,128)(2,1)}, bf16[2,2,2,72,1152]{4,3,0,1,2:T(8,128)(2,1)}, u32[]{:S(2)}, u32[]{:S(2)}) collective-permute-start(bf16[2,2,2,72,1152]{4,3,0,1,2:T(8,128)(2,1)} %bitcast.268), channel_id=1, source_target_pairs={{0,4},{4,0},{8,12},{12,8},{16,20},{20,16},{24,28},{28,24},{1,5},{5... | collective-permute-start | bytes 3981320 | tf_op jit(solution)/shard_map/ppermute | solution.py:567
  507.9 15.4 %copy-start.21 = (f32[512,1152]{1,0:T(8,128)S(1)}, f32[512,1152]{1,0:T(8,128)}, u32[]{:S(2)}) copy-start(f32[512,1152]{1,0:T(8,128)} %copy-done.20) | copy-start | bytes 7077892
  507.9 15.4 %copy-start.29 = (f32[512,1152]{1,0:T(8,128)S(1)}, f32[512,1152]{1,0:T(8,128)}, u32[]{:S(2)}) copy-start(f32[512,1152]{1,0:T(8,128)} %copy-done.28) | copy-start | bytes 7077892
  507.9 15.4 %copy-start.31 = (f32[512,1152]{1,0:T(8,128)S(1)}, f32[512,1152]{1,0:T(8,128)}, u32[]{:S(2)}) copy-start(f32[512,1152]{1,0:T(8,128)} %get-tuple-element.120) | copy-start | bytes 7077892
  507.9 15.4 %copy-start.75 = (f32[2,256]{1,0:T(2,128)S(1)}, f32[2,256]{1,0:T(2,128)}, u32[]{:S(2)}) copy-start(f32[2,256]{1,0:T(2,128)} %get-tuple-element.161) | copy-start | bytes 6148
  539.3 15.7 %all-to-all-start.2 = ((f32[16,1,3960]{2,1,0:T(1,128)}), f32[16,1,3960]{2,1,0:T(1,128)S(1)}, u32[]{:S(2)}, u32[]{:S(2)}) async-start(f32[16,1,3960]{2,1,0:T(1,128)} %all_to_all.25), calls=%async_computation.2 | async-start | bytes 507904 | tf_op jit(solution)/shard_map/all_to_all | solution.py:801
  546.7 15.0 %copy-start.76 = (pred[64]{0:T(512)(128)(4,1)S(1)}, pred[64]{0:T(512)(128)(4,1)}, u32[]{:S(2)}) copy-start(pred[64]{0:T(512)(128)(4,1)} %broadcast_in_dim.167) | copy-start | bytes 196
  546.7 15.0 %copy-start.77 = (pred[64]{0:T(512)(128)(4,1)S(1)}, pred[64]{0:T(512)(128)(4,1)}, u32[]{:S(2)}) copy-start(pred[64]{0:T(512)(128)(4,1)} %broadcast_in_dim.164) | copy-start | bytes 196
  555.3 4.7 collective-permute-start.27
  557.3 21.1 %collective-permute-start.29 = (bf16[2,72,1152]{2,1,0:T(8,128)(2,1)}, bf16[2,72,1152]{2,1,0:T(8,128)(2,1)}, u32[]{:S(2)}, u32[]{:S(2)}) collective-permute-start(bf16[2,72,1152]{2,1,0:T(8,128)(2,1)} %dynamic-slice_bitcast_fusion.4), channel_id=1, source_target_pairs={{0,8},{4,12},{8,0},{12,4},{16,24},{20,28},{24,16},{28,20},{1,9},{5... | collective-permute-start | bytes 995336 | tf_op jit(solution)/shard_map/ppermute | solution.py:567
  557.8 17.3 %collective-permute-start.24 = (bf16[2,2,72,1152]{3,2,0,1:T(8,128)(2,1)}, bf16[2,2,72,1152]{3,2,0,1:T(8,128)(2,1)}, u32[]{:S(2)}, u32[]{:S(2)}) collective-permute-start(bf16[2,2,72,1152]{3,2,0,1:T(8,128)(2,1)} %dynamic-slice_bitcast_fusion), channel_id=1, source_target_pairs={{0,1},{1,0},{2,3},{3,2},{4,5},{5,4},{6,7},{7,6},{8,9},{9,8},{10,11... | collective-permute-start | bytes 1990664 | tf_op jit(solution)/shard_map/ppermute | solution.py:567
  566.8 59.3 %all-to-all-start.3 = ((f32[16,1,7704]{2,1,0:T(1,128)}), f32[16,1,7704]{2,1,0:T(1,128)S(1)}, u32[]{:S(2)}, u32[]{:S(2)}) async-start(f32[16,1,7704]{2,1,0:T(1,128)} %all_to_all.28), calls=%async_computation.3 | async-start | bytes 999424 | tf_op jit(solution)/shard_map/all_to_all | solution.py:826
  579.5 30.9 %collective-permute-start.30 = (bf16[72,1152]{1,0:T(8,128)(2,1)S(1)}, bf16[72,1152]{1,0:T(8,128)(2,1)S(1)}, u32[]{:S(2)}, u32[]{:S(2)}) collective-permute-start(bf16[72,1152]{1,0:T(8,128)(2,1)S(1)} %dynamic-slice_bitcast_fusion.6), channel_id=1, source_target_pairs={{0,16},{4,20},{8,24},{12,28},{16,0},{20,4},{24,8},{28,12},{1,17},{... | collective-permute-start | bytes 497672 | tf_op jit(solution)/shard_map/ppermute | solution.py:567
  581.9 27.5 %collective-permute-start.31 = (bf16[2,72,1152]{2,1,0:T(8,128)(2,1)S(1)}, bf16[2,72,1152]{2,1,0:T(8,128)(2,1)S(1)}, u32[]{:S(2)}, u32[]{:S(2)}) collective-permute-start(bf16[2,72,1152]{2,1,0:T(8,128)(2,1)S(1)} %dynamic-slice_bitcast_fusion.3), channel_id=1, source_target_pairs={{0,8},{4,12},{8,0},{12,4},{16,24},{20,28},{24,16},{28,20},{1,9},{5... | collective-permute-start | bytes 995336 | tf_op jit(solution)/shard_map/ppermute | solution.py:567
  585.0 46.4 %collective-permute-start.25 = (bf16[512,1152]{1,0:T(8,128)(2,1)S(1)}, bf16[512,1152]{1,0:T(8,128)(2,1)}, u32[]{:S(2)}, u32[]{:S(2)}) collective-permute-start(bf16[512,1152]{1,0:T(8,128)(2,1)S(1)} %fusion.74), channel_id=1, source_target_pairs={{1,2},{2,1},{5,6},{6,5},{9,10},{10,9},{13,14},{14,13},{17,18},{18,... | collective-permute-start | bytes 3538952 | tf_op jit(solution)/shard_map/ppermute | solution.py:539
  592.1 51.3 %collective-permute-start.26 = (f32[512,1152]{1,0:T(8,128)}, f32[512,1152]{1,0:T(8,128)}, u32[]{:S(2)}, u32[]{:S(2)}) collective-permute-start(f32[512,1152]{1,0:T(8,128)} %broadcast_select_fusion.1), channel_id=1, source_target_pairs={{1,2},{2,1},{5,6},{6,5},{9,10},{10,9},{13,14},{14,13},{17,18},{18,... | collective-permute-start | bytes 7077896 | tf_op jit(solution)/shard_map/ppermute | solution.py:539
  609.5 11.0 %collective-permute-start.32 = (bf16[72,1152]{1,0:T(8,128)(2,1)S(1)}, bf16[72,1152]{1,0:T(8,128)(2,1)S(1)}, u32[]{:S(2)}, u32[]{:S(2)}) collective-permute-start(bf16[72,1152]{1,0:T(8,128)(2,1)S(1)} %dynamic-slice_bitcast_fusion.5), channel_id=1, source_target_pairs={{0,16},{4,20},{8,24},{12,28},{16,0},{20,4},{24,8},{28,12},{1,17},{... | collective-permute-start | bytes 497672 | tf_op jit(solution)/shard_map/ppermute | solution.py:567
  621.6 17.2 %collective-permute-start.33 = (f32[72,2880]{1,0:T(8,128)}, f32[72,2880]{1,0:T(8,128)}, u32[]{:S(2)}, u32[]{:S(2)}) collective-permute-start(f32[72,2880]{1,0:T(8,128)} %pad_maximum_fusion.4), channel_id=1, source_target_pairs={{1,2},{2,1},{5,6},{6,5},{9,10},{10,9},{13,14},{14,13},{17,18},{18,... | collective-permute-start | bytes 2488328 | tf_op jit(solution)/shard_map/ppermute | solution.py:539
  (74 other events, 369.0 us)
Sparse Core Ops, SparseCore 0:
  113.5 55.5 all-gather.4
  171.9 89.5 all-gather.2
  339.9 114.4 reduce-scatter.9
  458.8 87.3 reduce-scatter.5
  550.6 86.2 reduce-scatter.7

commit v4 on v3

--- a/solution.py
+++ b/solution.py
@@ -820,7 +820,7 @@
     split_b = fold_split(sum_b, order_a, 2)
     split_a = fold_split(after(sum_a, sum_b), order_a, 3)
     block_out = swap(after(block_out, sum_b))
-    input_grad = swap(after(input_grad, sum_b))
+    input_grad = swap(after(input_grad, sum_b).astype(bf16)).astype(f32)
     sum_b = fold_sum(split_b, order_a, 2, (packed,))
     sum_a = fold_sum(split_a, order_a, 3, (packed,))
     packed = lax.all_to_all(packed, COLUMNS, split_axis=0, concat_axis=0, tiled=True)
@@ -829,7 +829,7 @@
     sum_b = fold_step(sum_b, order_a, 3)
     for step in range(4, last):
         sum_a, sum_b = fold_step(sum_a, order_a, step), fold_step(sum_b, order_a, step)
-    grad_back = swap(jnp.concatenate([sum_a, sum_b, grad_out.astype(f32)], axis=1))
+    grad_back = swap(jnp.concatenate([sum_a, sum_b, grad_out.astype(f32)], axis=1).astype(bf16)).astype(f32)
     flat = packed[:, unit_slots * width :].reshape(-1)[: flat_rows * width].reshape(flat_rows, width)
     down_sum = flat[:lowrank].reshape(width, lowrank)
     up_sum = flat[lowrank : 2 * lowrank]

time: 666 us -> 665 us (level)
  waiting for transfers between devices: 127 us -> 134 us
    select_n x14 -> x13, other arithmetic: 14.4 us -> 11.3 us  [after(): return jnp.where(jnp.isnan(marks), jnp.zeros_like(x), x)]
    unnamed x207 -> x201, local copies, waits for them, and re-layouts: 26.1 us -> 27 us
  transfers between devices with their start and end apart: 43 -> 43, of which waited for: 16 -> 17; matrix products, arithmetic and copies ran while one was open for 28% -> 27% of each run, Pallas kernels for 25% -> 25%
where the time goes in v4:
time: 665 us; the launch traced here: 654 us
  Pallas kernels  166 us (25%)
  waiting for transfers between devices  134 us (20%)
  local copies, waits for them, and re-layouts  79.8 us (12%)
  matrix products  77.9 us (12%)
  starting transfers between devices  74.5 us (11%)
  other arithmetic  72.4 us (11%)
  between operations  49.4 us (7%)
    pallas_call x2, Pallas kernels, gla_backward(): pl.pallas_call(functools.partial(bwd_kernel, PS, PA, total), grid=(count,...  76.5 us
    ppermute x16, waiting for transfers between devices, flipped(): lax.ppermute(x, axis, [(i, i ^ 1 << place) for i in range(lax.axis_size(a...  55.4 us
    dot_general x9, matrix products, contract(): lax.dot_general(a, b, (((i,), (j,)), ((), ())), preferred_element_type=f32)  49.5 us
    ppermute x5, waiting for transfers between devices, across(): return lax.ppermute(x, 'mp', FLIP)  44 us
    pallas_call x1, Pallas kernels, gla_forward(): pl.pallas_call(functools.partial(fwd_kernel, PS, PA, total), grid=(H,), i...  41.9 us
    slice x39, local copies, waits for them, and re-layouts, after(): marks = sum((f[(0,) * f.ndim].astype(f32) for f in first))  27.1 us
    unnamed x201, local copies, waits for them, and re-layouts  27 us
    ppermute x6, starting transfers between devices, swap(): away = lax.ppermute(x, ('core', 'mp'), [(1, 2), (2, 1)])  22.7 us
  transfers between devices with their start and end apart: 43, of which 17 were waited for; matrix products, arithmetic and copies ran while one was open for 27% of the time, Pallas kernels for 25%

profile of v4, /device:TPU:1, one launch (start us, length us, event | category | flops | bytes accessed | tf_op | source)
XLA Modules:
  0.0 653.8 jit_solution(9823714611831616938)
XLA Ops:
  9.3 4.5 collective-permute-start.1
  15.8 3.6 collective-permute-start
  20.2 2.4 collective-permute-start.4
  26.6 3.9 all-to-all-start
  31.1 2.3 collective-permute-start.2
  35.3 6.3 collective-permute-done.2
  44.7 2.8 gather_fusion
  50.3 2.4 broadcast_select_fusion.2
  55.3 3.0 collective-permute-done.3
  60.9 7.5 %all-to-all-start.1 = ((f32[16,2,432]{2,1,0:T(2,128)}), f32[16,2,432]{2,1,0:T(2,128)S(1)}, u32[]{:S(2)}, u32[]{:S(2)}) async-start(f32[16,2,432]{2,1,0:T(2,128)} %bitcast.14), calls=%async_computation.1 | async-start | bytes 131072 | tf_op jit(solution)/shard_map/all_to_all | solution.py:680
  68.6 5.8 all-to-all-done.1
  85.1 12.0 %collective-permute-done.9 = bf16[2,2,72,1152]{3,2,0,1:T(8,128)(2,1)S(1)} collective-permute-done((bf16[2,2,72,1152]{3,2,0,1:T(8,128)(2,1)S(1)}, bf16[2,2,72,1152]{3,2,0,1:T(8,128)(2,1)S(1)}, u32[]{:S(2)}, u32[]{:S(2)}) %collective-permute-start.9) | collective-permute-done | bytes 663584 | tf_op jit(solution)/shard_map/ppermute | solution.py:567
  102.7 2.8 collective-permute-start.7
  113.5 26.8 %collective-permute-done.14 = f32[2,1152]{1,0:T(2,128)} collective-permute-done((f32[2,1152]{1,0:T(2,128)S(1)}, f32[2,1152]{1,0:T(2,128)}, u32[]{:S(2)}, u32[]{:S(2)}) %collective-permute-start.14) | collective-permute-done | bytes 9248 | tf_op jit(solution)/shard_map/ppermute | solution.py:557
  140.3 2.7 fusion.70
  151.6 2.1 select_bitcast_fusion.1
  162.3 2.7 fusion.55
  167.5 16.2 %project.1 = (f32[4,8,1024,128]{3,2,1,0:T(8,128)}, f32[8,1024,128]{2,1,0:T(8,128)}, f32[1024,128]{1,0:T(8,128)}) custom-call(s32[1]{0:T(128)} %bitcast.18.turn_ref, bf16[512,1152]{1,0:T(8,128)(2,1)} %fusion.54.x_ref, bf16[512,1152]{1,0:T(8,128)(2,1)} %collective-permute-done.7.y_ref, bf16[1152,1152]{1,0:T(8,128)(2,1)} %bitcast.256, ...), custom_call_target="tpu_custom_call" | custom-call | flops 13500000256 | bytes 1000000 | tf_op jit(solution)/shard_map/project/pallas_call | solution.py:380
  183.7 41.9 %gla_forward.1 = (bf16[8,1024,128]{2,1,0:T(8,128)(2,1)S(1)}, f32[8,1024,128]{2,1,0:T(8,128)S(1)}, f32[8,8,128,128]{3,2,1,0:T(8,128)S(1)}, f32[8,8,128,128]{3,2,1,0:T(8,128)}) custom-call(s32[1]{0:T(128)S(6)} %select_n.499.big_ref, f32[4,8,1024,128]{3,2,1,0:T(8,128)} %get-tuple-element.36.q_ref.k_ref.v_ref.g_ref, ...), custom_call_target="tpu_custom_call" | custom-call | flops 58500001792 | bytes 1000000 | tf_op jit(solution)/shard_map/gla_forward/pallas_call | solution.py:165
  228.9 2.0 copy-done.14
  233.8 3.4 attend.1
  237.7 4.2 collective-permute-done.16
  246.1 2.1 collective-permute-start.17
  248.3 13.3 %all-gather.3.cloned.1.call-done = bf16[1152,4608]{1,0:T(8,128)(2,1)} async-done(((bf16[72,4608]{1,0:T(8,128)(2,1)}), bf16[1152,4608]{1,0:T(8,128)(2,1)}) %all-gather.3.cloned.1.call-update) | async-done | bytes 10616848 | tf_op jit(solution)/shard_map/all_gather | solution.py:710
  261.6 6.9 %multiply_convert_fusion.1 = (bf16[512,2304]{1,0:T(8,128)(2,1)S(1)}, f32[512,2304]{1,0:T(8,128)S(1)}) fusion(bf16[512,1152]{1,0:T(8,128)(2,1)} %fusion.61, bf16[1152,4608]{1,0:T(8,128)(2,1)} %all-gather.3.cloned.1.call-done), kind=kOutput, calls=%fused_computation.31 | convolution fusion | flops 2728525824 | bytes 13565952 | tf_op jit(solution)/shard_map/dot_general | solution.py:728
  268.5 5.9 fusion.6
  274.3 3.2 fusion.32
  278.1 3.2 fusion.24
  283.4 3.8 multiply_convert_fusion
  287.3 5.7 fusion.13
  293.1 4.3 fusion.43
  301.1 7.7 %convolution_convert_fusion = bf16[1152,2304]{1,0:T(8,128)(2,1)} fusion(bf16[512,2304]{1,0:T(8,128)(2,1)S(1)} %get-tuple-element.166, bf16[512,2304]{1,0:T(8,128)(2,1)S(1)} %get-tuple-element.164, pred[]{:T(512)} %bitcast.51, bf16[512,1152]{1,0:T(8,128)(2,1)S(1)} %copy-done.53, bf16[512,1152]{1,0:T(8,128)(2,1)S(1)} %copy-done.56), kind=kOutput, calls=%fused_computation.2 | convolution fusion | flops 5454987264 | bytes 12386305 | tf_op jit(solution)/shard_map/dot_general | solution.py:629
  309.9 10.4 %convolution_convert_fusion.1 = bf16[1152,2304]{1,0:T(8,128)(2,1)} fusion(bf16[512,2304]{1,0:T(8,128)(2,1)} %copy-done.91, bf16[512,2304]{1,0:T(8,128)(2,1)} %copy-done.88, pred[]{:T(512)} %bitcast.51, bf16[512,1152]{1,0:T(8,128)(2,1)} %copy-done.52, bf16[512,1152]{1,0:T(8,128)(2,1)} %fusion.61), kind=kOutput, calls=%fused_computation.3 | convolution fusion | flops 5454987264 | bytes 12386305 | tf_op jit(solution)/shard_map/dot_general | solution.py:629
  322.8 3.2 collective-permute-done.18
  326.1 3.2 multiply_reduce_fusion.2
  333.2 2.5 collective-permute-done.19
  336.7 3.2 convolution_convert_fusion.4
  341.7 3.2 pad_maximum_fusion.2.x_ref
  345.0 2.0 pad_maximum_fusion.3.g_ref
  347.2 4.3 attend_back.1.gm_ref
  353.4 38.5 %gla_backward.2 = (bf16[4,4,1024,128]{3,2,1,0:T(8,128)(2,1)}, f32[4,1024,128]{2,1,0:T(8,128)S(1)}, f32[4,16,128]{2,1,0:T(8,128)S(1)}, f32[4,8,128]{2,1,0:T(8,128)S(1)}) custom-call(s32[1]{0:T(128)} %bitcast.19.big_ref, f32[4,8,1024,128]{3,2,1,0:T(8,128)} %get-tuple-element.36.q_ref.k_ref.v_ref.g_ref, ...), custom_call_target="tpu_custom_call" | custom-call | flops 35999997952 | bytes 1000000 | tf_op jit(solution)/shard_map/gla_backward/pallas_call | solution.py:289
  391.9 3.0 copy-done.10
  396.7 5.8 convolution_convert_fusion.3
  406.1 38.0 %gla_backward.3 = (bf16[4,4,1024,128]{3,2,1,0:T(8,128)(2,1)}, f32[4,1024,128]{2,1,0:T(8,128)S(1)}, f32[4,16,128]{2,1,0:T(8,128)S(1)}, f32[4,8,128]{2,1,0:T(8,128)S(1)}) custom-call(s32[1]{0:T(128)S(6)} %select_n.512.big_ref, f32[4,8,1024,128]{3,2,1,0:T(8,128)} %get-tuple-element.36.q_ref.k_ref.v_ref.g_ref, ...), custom_call_target="tpu_custom_call" | custom-call | flops 35999997952 | bytes 1000000 | tf_op jit(solution)/shard_map/gla_backward/pallas_call | solution.py:289
  448.9 2.2 copy-done.8
  455.8 4.9 convolution_convert_fusion.2
  466.0 20.0 %project_back.1 = (f32[512,1152]{1,0:T(8,128)}, f32[512,1152]{1,0:T(8,128)}, f32[128,1152]{1,0:T(8,128)}, f32[128,1024]{1,0:T(8,128)}) custom-call(s32[1]{0:T(128)S(6)} %select_n.520.turn_ref, bf16[1024,1152]{1,0:T(8,128)(2,1)} %pad_maximum_fusion.2.x_ref, bf16[1024,1152]{1,0:T(8,128)(2,1)} %copy-done.2, bf16[1024,1152]{1,0:T(8,128)(2,1)} %copy-done.3, ...), custom_call_target="tpu_custom_call" | custom-call | flops 1800000000 | bytes 1000000 | tf_op jit(solution)/shard_map/project_back/pallas_call | solution.py:501
  486.8 6.8 %fusion.46 = bf16[512,1152]{1,0:T(8,128)(2,1)} fusion(bf16[512,2304]{1,0:T(8,128)(2,1)S(1)} %copy-done.90, bf16[1152,4608]{1,0:T(8,128)(2,1)} %all-gather.3.cloned.1.call-done, pred[]{:T(512)} %bitcast.51), kind=kOutput, calls=%fused_computation.64 | convolution fusion | flops 2719088640 | bytes 8847872 | tf_op jit(solution)/shard_map/dot_general | solution.py:629
  500.0 3.0 multiply_reduce_fusion
  507.9 13.6 %collective-permute-done.22 = bf16[512,1152]{1,0:T(8,128)(2,1)} collective-permute-done((bf16[512,1152]{1,0:T(8,128)(2,1)}, bf16[512,1152]{1,0:T(8,128)(2,1)}, u32[]{:S(2)}, u32[]{:S(2)}) %collective-permute-start.22) | collective-permute-done | bytes 1179680 | tf_op jit(solution)/shard_map/ppermute | solution.py:557
  521.5 4.7 fusion.69
  528.3 5.7 collective-permute-done.23
  534.0 2.1 add_convert_fusion
  538.9 5.7 all-to-all-start.2
  546.9 7.0 %all-to-all-done.2 = f32[16,1,3960]{2,1,0:T(1,128)S(1)} async-done(((f32[16,1,3960]{2,1,0:T(1,128)}), f32[16,1,3960]{2,1,0:T(1,128)S(1)}, u32[]{:S(2)}, u32[]{:S(2)}) %all-to-all-start.2) | async-done | bytes 253472 | tf_op jit(solution)/shard_map/all_to_all | solution.py:801
  559.4 2.0 fusion.93
  564.5 4.6 all-to-all-start.3
  569.9 2.3 fusion.92
  581.6 3.9 collective-permute-start.26
  589.3 10.6 %collective-permute-done.31 = bf16[2,72,1152]{2,1,0:T(8,128)(2,1)S(1)} collective-permute-done((bf16[2,72,1152]{2,1,0:T(8,128)(2,1)S(1)}, bf16[2,72,1152]{2,1,0:T(8,128)(2,1)S(1)}, u32[]{:S(2)}, u32[]{:S(2)}) %collective-permute-start.31) | collective-permute-done | bytes 331808 | tf_op jit(solution)/shard_map/ppermute | solution.py:567
  600.3 16.8 %collective-permute-done.32 = bf16[72,1152]{1,0:T(8,128)(2,1)S(1)} collective-permute-done((bf16[72,1152]{1,0:T(8,128)(2,1)S(1)}, bf16[72,1152]{1,0:T(8,128)(2,1)S(1)}, u32[]{:S(2)}, u32[]{:S(2)}) %collective-permute-start.32) | collective-permute-done | bytes 165920 | tf_op jit(solution)/shard_map/ppermute | solution.py:567
  618.2 6.7 %collective-permute-start.33 = (bf16[72,2880]{1,0:T(8,128)(2,1)S(1)}, bf16[72,2880]{1,0:T(8,128)(2,1)}, u32[]{:S(2)}, u32[]{:S(2)}) collective-permute-start(bf16[72,2880]{1,0:T(8,128)(2,1)S(1)} %pad_maximum_fusion.5), channel_id=1, source_target_pairs={{1,2},{2,1},{5,6},{6,5},{9,10},{10,9},{13,14},{14,13},{17,18},{18,... | collective-permute-start | bytes 1244168 | tf_op jit(solution)/shard_map/ppermute | solution.py:539
  637.5 2.4 broadcast_select_fusion.3
  639.9 3.1 select_convert_fusion.1
  (475 shorter events, 141.2 us)
Async XLA Ops:
  7.2 36.8 %copy-start = (bf16[1001,1152]{1,0:T(8,128)(2,1)S(1)}, bf16[1001,1152]{1,0:T(8,128)(2,1)}, u32[]{:S(2)}) copy-start(bf16[1001,1152]{1,0:T(8,128)(2,1)} %param.21) | copy-start | bytes 6918916
  7.2 12.9 %copy-start.82 = (bf16[432]{0:T(512)(128)(2,1)S(1)}, bf16[432]{0:T(512)(128)(2,1)}, u32[]{:S(2)}) copy-start(bf16[432]{0:T(512)(128)(2,1)} %param.26) | copy-start | bytes 2596
  7.2 18.7 %copy-start.84 = (s32[4]{0:T(128)S(1)}, s32[4]{0:T(128)}, u32[]{:S(2)}) copy-start(s32[4]{0:T(128)} %param.23) | copy-start | bytes 52
  7.2 18.7 %copy-start.85 = (s32[4]{0:T(128)S(1)}, s32[4]{0:T(128)}, u32[]{:S(2)}) copy-start(s32[4]{0:T(128)} %param.22) | copy-start | bytes 52
  9.3 10.8 %collective-permute-start.1 = (bf16[72,2304]{1,0:T(8,128)(2,1)S(1)}, bf16[72,2304]{1,0:T(8,128)(2,1)S(1)}, u32[]{:S(2)}, u32[]{:S(2)}) collective-permute-start(bf16[72,2304]{1,0:T(8,128)(2,1)S(1)} %reshape.574), channel_id=1, source_target_pairs={{1,2},{2,1},{5,6},{6,5},{9,10},{10,9},{13,14},{14,13},{17,18},{18,... | collective-permute-start | bytes 995336 | tf_op jit(solution)/shard_map/ppermute | solution.py:539
  13.9 8.7 %collective-permute-start.6 = (bf16[72,576]{1,0:T(8,128)(2,1)S(1)}, bf16[72,576]{1,0:T(8,128)(2,1)}, u32[]{:S(2)}, u32[]{:S(2)}) collective-permute-start(bf16[72,576]{1,0:T(8,128)(2,1)S(1)} %bitcast.288), channel_id=1, source_target_pairs={{1,2},{2,1},{5,6},{6,5},{9,10},{10,9},{13,14},{14,13},{17,18},{18,... | collective-permute-start | bytes 248840 | tf_op jit(solution)/shard_map/ppermute | solution.py:539
  15.8 61.2 %collective-permute-start = (bf16[512,1152]{1,0:T(8,128)(2,1)}, bf16[512,1152]{1,0:T(8,128)(2,1)}, u32[]{:S(2)}, u32[]{:S(2)}) collective-permute-start(bf16[512,1152]{1,0:T(8,128)(2,1)} %param.18), channel_id=1, source_target_pairs={{1,2},{2,1},{5,6},{6,5},{9,10},{10,9},{13,14},{14,13},{17,18},{18,... | collective-permute-start | bytes 3538952 | tf_op jit(solution)/shard_map/ppermute | solution.py:539
  20.2 10.3 %collective-permute-start.4 = (bf16[72,1152]{1,0:T(8,128)(2,1)S(1)}, bf16[72,1152]{1,0:T(8,128)(2,1)S(1)}, u32[]{:S(2)}, u32[]{:S(2)}) collective-permute-start(bf16[72,1152]{1,0:T(8,128)(2,1)S(1)} %slice.286), channel_id=1, source_target_pairs={{0,16},{4,20},{8,24},{12,28},{16,0},{20,4},{24,8},{28,12},{1,17},{... | collective-permute-start | bytes 497672 | tf_op jit(solution)/shard_map/ppermute | solution.py:567
  26.6 16.8 %all-to-all-start = ((s32[16,1,9]{2,1,0:T(1,128)}), s32[16,1,9]{2,1,0:T(1,128)S(1)}, u32[]{:S(2)}, u32[]{:S(2)}) async-start(s32[16,1,9]{2,1,0:T(1,128)} %broadcast_in_dim.146), calls=%async_computation | async-start | bytes 16384 | tf_op jit(solution)/shard_map/all_to_all | solution.py:661
  31.1 10.5 %collective-permute-start.2 = (bf16[72,1152]{1,0:T(8,128)(2,1)S(1)}, bf16[72,1152]{1,0:T(8,128)(2,1)S(1)}, u32[]{:S(2)}, u32[]{:S(2)}) collective-permute-start(bf16[72,1152]{1,0:T(8,128)(2,1)S(1)} %get-tuple-element.149), channel_id=1, source_target_pairs={{0,16},{4,20},{8,24},{12,28},{16,0},{20,4},{24,8},{28,12},{1,17},{... | collective-permute-start | bytes 497672 | tf_op jit(solution)/shard_map/ppermute | solution.py:567
  34.1 19.5 %collective-permute-start.5 = (bf16[2,72,1152]{2,1,0:T(8,128)(2,1)}, bf16[2,72,1152]{2,1,0:T(8,128)(2,1)}, u32[]{:S(2)}, u32[]{:S(2)}) collective-permute-start(bf16[2,72,1152]{2,1,0:T(8,128)(2,1)} %pad_maximum_fusion.7), channel_id=1, source_target_pairs={{0,8},{4,12},{8,0},{12,4},{16,24},{20,28},{24,16},{28,20},{1,9},{5... | collective-permute-start | bytes 995336 | tf_op jit(solution)/shard_map/ppermute | solution.py:567
  49.6 8.6 %collective-permute-start.3 = (bf16[2,72,1152]{2,1,0:T(8,128)(2,1)S(1)}, bf16[2,72,1152]{2,1,0:T(8,128)(2,1)S(1)}, u32[]{:S(2)}, u32[]{:S(2)}) collective-permute-start(bf16[2,72,1152]{2,1,0:T(8,128)(2,1)S(1)} %pad_maximum_fusion.6), channel_id=1, source_target_pairs={{0,8},{4,12},{8,0},{12,4},{16,24},{20,28},{24,16},{28,20},{1,9},{5... | collective-permute-start | bytes 995336 | tf_op jit(solution)/shard_map/ppermute | solution.py:567
  52.7 27.1 %collective-permute-start.8 = (bf16[512,1152]{1,0:T(8,128)(2,1)}, bf16[512,1152]{1,0:T(8,128)(2,1)}, u32[]{:S(2)}, u32[]{:S(2)}) collective-permute-start(bf16[512,1152]{1,0:T(8,128)(2,1)} %broadcast_select_fusion.2), channel_id=1, source_target_pairs={{0,1},{1,0},{2,3},{3,2},{4,5},{5,4},{6,7},{7,6},{8,9},{9,8},{10,11... | collective-permute-start | bytes 3538952 | tf_op jit(solution)/shard_map/ppermute | solution.py:557
  54.7 29.0 %copy-start.38 = (bf16[2,1,72,1152]{3,2,0,1:T(8,128)(2,1)}, bf16[2,1,72,1152]{3,2,0,1:T(8,128)(2,1)S(1)}, u32[]{:S(2)}) copy-start(bf16[2,1,72,1152]{3,2,0,1:T(8,128)(2,1)S(1)} %get-tuple-element.141) | copy-start | bytes 995332
  54.7 29.0 %copy-start.40 = (bf16[2,1,72,1152]{3,2,0,1:T(8,128)(2,1)}, bf16[2,1,72,1152]{3,2,0,1:T(8,128)(2,1)S(1)}, u32[]{:S(2)}) copy-start(bf16[2,1,72,1152]{3,2,0,1:T(8,128)(2,1)S(1)} %get-tuple-element.142) | copy-start | bytes 995332
  60.9 13.5 %all-to-all-start.1 = ((f32[16,2,432]{2,1,0:T(2,128)}), f32[16,2,432]{2,1,0:T(2,128)S(1)}, u32[]{:S(2)}, u32[]{:S(2)}) async-start(f32[16,2,432]{2,1,0:T(2,128)} %bitcast.14), calls=%async_computation.1 | async-start | bytes 131072 | tf_op jit(solution)/shard_map/all_to_all | solution.py:680
  68.4 162.5 %all-gather.5.cloned.1.call-start = ((), (), s32[]{:S(2)}) async-start(), calls=%async_computation.8 | async-start | bytes 1566720 | tf_op jit(solution)/shard_map/all_gather | solution.py:660
  68.5 71.8 %collective-permute-start.11 = (bf16[512,1152]{1,0:T(8,128)(2,1)}, bf16[512,1152]{1,0:T(8,128)(2,1)}, u32[]{:S(2)}, u32[]{:S(2)}) collective-permute-start(bf16[512,1152]{1,0:T(8,128)(2,1)} %param.19), channel_id=1, source_target_pairs={{0,2},{2,0},{1,3},{3,1},{4,6},{6,4},{5,7},{7,5},{8,10},{10,8},{9,1... | collective-permute-start | bytes 3538952 | tf_op jit(solution)/shard_map/ppermute | solution.py:544
  77.0 22.7 %copy-start.62 = (f32[2,1152]{1,0:T(2,128)}, f32[2,1152]{1,0:T(2,128)S(1)}, u32[]{:S(2)}) copy-start(f32[2,1152]{1,0:T(2,128)S(1)} %get-tuple-element.157) | copy-start | bytes 27652
  77.0 85.3 %copy-start.67 = (f32[2,1152]{1,0:T(2,128)}, f32[2,1152]{1,0:T(2,128)S(1)}, u32[]{:S(2)}) copy-start(f32[2,1152]{1,0:T(2,128)S(1)} %get-tuple-element.155) | copy-start | bytes 27652
  78.7 163.1 %copy-start.18 = (bf16[512,1152]{1,0:T(8,128)(2,1)}, bf16[512,1152]{1,0:T(8,128)(2,1)S(1)}, u32[]{:S(2)}) copy-start(bf16[512,1152]{1,0:T(8,128)(2,1)S(1)} %get-tuple-element.122) | copy-start | bytes 3538948
  82.3 14.8 %collective-permute-start.9 = (bf16[2,2,72,1152]{3,2,0,1:T(8,128)(2,1)S(1)}, bf16[2,2,72,1152]{3,2,0,1:T(8,128)(2,1)S(1)}, u32[]{:S(2)}, u32[]{:S(2)}) collective-permute-start(bf16[2,2,72,1152]{3,2,0,1:T(8,128)(2,1)S(1)} %maximum_select_fusion.6), channel_id=1, source_target_pairs={{0,1},{1,0},{2,3},{3,2},{4,5},{5,4},{6,7},{7,6},{8,9},{9,8},{10,11... | collective-permute-start | bytes 1990664 | tf_op jit(solution)/shard_map/ppermute | solution.py:567
  83.2 16.5 %copy-start.64 = (f32[512]{0:T(512)}, f32[512]{0:T(512)S(1)}, u32[]{:S(2)}) copy-start(f32[512]{0:T(512)S(1)} %broadcast_multiply_fusion.1) | copy-start | bytes 6148
  83.7 16.0 %copy-start.73 = (f32[512]{0:T(512)}, f32[512]{0:T(512)S(1)}, u32[]{:S(2)}) copy-start(f32[512]{0:T(512)S(1)} %multiply_reduce_fusion.4) | copy-start | bytes 6148
  83.8 23.1 %collective-permute-start.12 = (bf16[2,2,72,1152]{3,2,0,1:T(8,128)(2,1)S(1)}, bf16[2,2,72,1152]{3,2,0,1:T(8,128)(2,1)S(1)}, u32[]{:S(2)}, u32[]{:S(2)}) collective-permute-start(bf16[2,2,72,1152]{3,2,0,1:T(8,128)(2,1)S(1)} %maximum_select_fusion.7), channel_id=1, source_target_pairs={{0,4},{4,0},{8,12},{12,8},{16,20},{20,16},{24,28},{28,24},{1,5},{5... | collective-permute-start | bytes 1990664 | tf_op jit(solution)/shard_map/ppermute | solution.py:567
  98.5 50.2 %collective-permute-start.10 = (bf16[2,2,2,72,1152]{4,3,0,1,2:T(8,128)(2,1)}, bf16[2,2,2,72,1152]{4,3,0,1,2:T(8,128)(2,1)}, u32[]{:S(2)}, u32[]{:S(2)}) collective-permute-start(bf16[2,2,2,72,1152]{4,3,0,1,2:T(8,128)(2,1)} %maximum_select_fusion.4), channel_id=1, source_target_pairs={{0,4},{4,0},{8,12},{12,8},{16,20},{20,16},{24,28},{28,24},{1,5},{5... | collective-permute-start | bytes 3981320 | tf_op jit(solution)/shard_map/ppermute | solution.py:567
  102.7 40.9 %collective-permute-start.7 = (bf16[512,1152]{1,0:T(8,128)(2,1)}, bf16[512,1152]{1,0:T(8,128)(2,1)}, u32[]{:S(2)}, u32[]{:S(2)}) collective-permute-start(bf16[512,1152]{1,0:T(8,128)(2,1)} %fusion.54.x_ref), channel_id=1, source_target_pairs={{0,2},{2,0},{1,3},{3,1},{4,6},{6,4},{5,7},{7,5},{8,10},{10,8},{9,1... | collective-permute-start | bytes 3538952 | tf_op jit(solution)/shard_map/ppermute | solution.py:544
  108.3 43.3 %collective-permute-start.13 = (bf16[2,2,2,72,1152]{4,3,0,1,2:T(8,128)(2,1)}, bf16[2,2,2,72,1152]{4,3,0,1,2:T(8,128)(2,1)}, u32[]{:S(2)}, u32[]{:S(2)}) collective-permute-start(bf16[2,2,2,72,1152]{4,3,0,1,2:T(8,128)(2,1)} %maximum_select_fusion.5), channel_id=1, source_target_pairs={{0,1},{1,0},{2,3},{3,2},{4,5},{5,4},{6,7},{7,6},{8,9},{9,8},{10,11... | collective-permute-start | bytes 3981320 | tf_op jit(solution)/shard_map/ppermute | solution.py:567
  109.7 30.5 %collective-permute-start.14 = (f32[2,1152]{1,0:T(2,128)S(1)}, f32[2,1152]{1,0:T(2,128)}, u32[]{:S(2)}, u32[]{:S(2)}) collective-permute-start(f32[2,1152]{1,0:T(2,128)S(1)} %get-tuple-element.155), channel_id=1, source_target_pairs={{0,1},{1,0},{2,3},{3,2},{4,5},{5,4},{6,7},{7,6},{8,9},{9,8},{10,11... | collective-permute-start | bytes 27656 | tf_op jit(solution)/shard_map/ppermute | solution.py:557
  110.4 32.6 %copy-start.79 = (f32[1,8,128]{2,1,0:T(8,128)}, f32[1,8,128]{2,1,0:T(8,128)S(1)}, u32[]{:S(2)}) copy-start(f32[1,8,128]{2,1,0:T(8,128)S(1)} %pad_convert_fusion) | copy-start | bytes 12292
  112.9 30.1 %copy-start.57 = (bf16[16,8,8,128]{3,1,2,0:T(8,128)(2,1)}, bf16[16,8,8,128]{3,1,2,0:T(8,128)(2,1)S(1)}, u32[]{:S(2)}) copy-start(bf16[16,8,8,128]{3,1,2,0:T(8,128)(2,1)S(1)} %copy.123) | copy-start | bytes 786436
  113.5 148.1 %all-gather.3.cloned.1.call-start = ((), (), s32[]{:S(2)}) async-start(), calls=%async_computation.7 | async-start | bytes 11280384 | tf_op jit(solution)/shard_map/all_gather | solution.py:710
  158.5 458.6 %reduce-scatter.10.cloned.1.call-start = ((), (), s32[]{:S(2)}) async-start(), calls=%async_computation.11 | async-start | bytes 1566720
  158.6 3.7 collective-permute-start.15
  165.0 18.7 %copy-start.55 = (bf16[512,1152]{1,0:T(8,128)(2,1)}, bf16[512,1152]{1,0:T(8,128)(2,1)S(1)}, u32[]{:S(2)}) copy-start(bf16[512,1152]{1,0:T(8,128)(2,1)S(1)} %get-tuple-element.123) | copy-start | bytes 3538948
  237.3 4.6 collective-permute-start.16
  246.1 37.2 %collective-permute-start.17 = (bf16[512,1152]{1,0:T(8,128)(2,1)}, bf16[512,1152]{1,0:T(8,128)(2,1)S(1)}, u32[]{:S(2)}, u32[]{:S(2)}) collective-permute-start(bf16[512,1152]{1,0:T(8,128)(2,1)} %fusion.61), channel_id=1, source_target_pairs={{0,1},{1,0},{2,3},{3,2},{4,5},{5,4},{6,7},{7,6},{8,9},{9,8},{10,11... | collective-permute-start | bytes 3538952 | tf_op jit(solution)/shard_map/ppermute | solution.py:557
  287.3 13.8 %copy-start.89 = (bf16[512,2304]{1,0:T(8,128)(2,1)}, bf16[512,2304]{1,0:T(8,128)(2,1)S(1)}, u32[]{:S(2)}) copy-start(bf16[512,2304]{1,0:T(8,128)(2,1)S(1)} %get-tuple-element.166) | copy-start | bytes 7077892
  298.5 27.5 %collective-permute-start.18 = (bf16[512,1152]{1,0:T(8,128)(2,1)}, bf16[512,1152]{1,0:T(8,128)(2,1)S(1)}, u32[]{:S(2)}, u32[]{:S(2)}) collective-permute-start(bf16[512,1152]{1,0:T(8,128)(2,1)} %fusion.43), channel_id=1, source_target_pairs={{0,1},{1,0},{2,3},{3,2},{4,5},{5,4},{6,7},{7,6},{8,9},{9,8},{10,11... | collective-permute-start | bytes 3538952 | tf_op jit(solution)/shard_map/ppermute | solution.py:557
  332.1 3.5 collective-permute-start.19
  340.0 303.1 %reduce-scatter.8.cloned.1.call-start = ((), (), s32[]{:S(2)}) async-start(), calls=%async_computation.10 | async-start | bytes 5640192 | tf_op jit(solution)/shard_map/reduce_scatter | solution.py:744
  340.6 304.4 %reduce-scatter.6.cloned.1.call-start = ((), (), s32[]{:S(2)}) async-start(), calls=%async_computation.9 | async-start | bytes 5640192 | tf_op jit(solution)/shard_map/reduce_scatter | solution.py:746
  403.3 43.4 %collective-permute-start.20 = (bf16[2,2,2,72,1152]{4,3,0,1,2:T(8,128)(2,1)S(1)}, bf16[2,2,2,72,1152]{4,3,0,1,2:T(8,128)(2,1)S(1)}, u32[]{:S(2)}, u32[]{:S(2)}) collective-permute-start(bf16[2,2,2,72,1152]{4,3,0,1,2:T(8,128)(2,1)S(1)} %bitcast.270), channel_id=1, source_target_pairs={{0,4},{4,0},{8,12},{12,8},{16,20},{20,16},{24,28},{28,24},{1,5},{5... | collective-permute-start | bytes 3981320 | tf_op jit(solution)/shard_map/ppermute | solution.py:567
  461.0 25.0 %copy-start.28 = (bf16[2,2,1,2,72,1152]{5,4,3,2,1,0:T(8,128)(2,1)}, bf16[2,2,1,2,72,1152]{5,4,3,2,1,0:T(8,128)(2,1)S(1)}, u32[]{:S(2)}) copy-start(bf16[2,2,1,2,72,1152]{5,4,3,2,1,0:T(8,128)(2,1)S(1)} %get-tuple-element.127) | copy-start | bytes 3981316
  466.0 20.8 %copy-start.90 = (bf16[512,2304]{1,0:T(8,128)(2,1)S(1)}, bf16[512,2304]{1,0:T(8,128)(2,1)}, u32[]{:S(2)}) copy-start(bf16[512,2304]{1,0:T(8,128)(2,1)} %copy-done.89) | copy-start | bytes 7077892
  485.9 14.1 %collective-permute-start.21 = (f32[512,1152]{1,0:T(8,128)}, f32[512,1152]{1,0:T(8,128)}, u32[]{:S(2)}, u32[]{:S(2)}) collective-permute-start(f32[512,1152]{1,0:T(8,128)} %get-tuple-element.50), channel_id=1, source_target_pairs={{0,2},{2,0},{1,3},{3,1},{4,6},{6,4},{5,7},{7,5},{8,10},{10,8},{9,1... | collective-permute-start | bytes 7077896 | tf_op jit(solution)/shard_map/ppermute | solution.py:544
  493.5 27.9 %collective-permute-start.22 = (bf16[512,1152]{1,0:T(8,128)(2,1)}, bf16[512,1152]{1,0:T(8,128)(2,1)}, u32[]{:S(2)}, u32[]{:S(2)}) collective-permute-start(bf16[512,1152]{1,0:T(8,128)(2,1)} %fusion.46), channel_id=1, source_target_pairs={{0,1},{1,0},{2,3},{3,2},{4,5},{5,4},{6,7},{7,6},{8,9},{9,8},{10,11... | collective-permute-start | bytes 3538952 | tf_op jit(solution)/shard_map/ppermute | solution.py:557
  495.3 50.2 %collective-permute-start.28 = (bf16[2,2,72,1152]{3,2,0,1:T(8,128)(2,1)}, bf16[2,2,72,1152]{3,2,0,1:T(8,128)(2,1)}, u32[]{:S(2)}, u32[]{:S(2)}) collective-permute-start(bf16[2,2,72,1152]{3,2,0,1:T(8,128)(2,1)} %get-tuple-element.136), channel_id=1, source_target_pairs={{0,1},{1,0},{2,3},{3,2},{4,5},{5,4},{6,7},{7,6},{8,9},{9,8},{10,11... | collective-permute-start | bytes 1990664 | tf_op jit(solution)/shard_map/ppermute | solution.py:567
  495.4 38.6 %collective-permute-start.23 = (bf16[2,2,2,72,1152]{4,3,0,1,2:T(8,128)(2,1)}, bf16[2,2,2,72,1152]{4,3,0,1,2:T(8,128)(2,1)}, u32[]{:S(2)}, u32[]{:S(2)}) collective-permute-start(bf16[2,2,2,72,1152]{4,3,0,1,2:T(8,128)(2,1)} %bitcast.268), channel_id=1, source_target_pairs={{0,4},{4,0},{8,12},{12,8},{16,20},{20,16},{24,28},{28,24},{1,5},{5... | collective-permute-start | bytes 3981320 | tf_op jit(solution)/shard_map/ppermute | solution.py:567
  504.8 16.7 %copy-start.21 = (f32[512,1152]{1,0:T(8,128)S(1)}, f32[512,1152]{1,0:T(8,128)}, u32[]{:S(2)}) copy-start(f32[512,1152]{1,0:T(8,128)} %copy-done.20) | copy-start | bytes 7077892
  504.8 16.7 %copy-start.32 = (f32[512,1152]{1,0:T(8,128)S(1)}, f32[512,1152]{1,0:T(8,128)}, u32[]{:S(2)}) copy-start(f32[512,1152]{1,0:T(8,128)} %copy-done.31) | copy-start | bytes 7077892
  504.8 16.7 %copy-start.34 = (f32[512,1152]{1,0:T(8,128)S(1)}, f32[512,1152]{1,0:T(8,128)}, u32[]{:S(2)}) copy-start(f32[512,1152]{1,0:T(8,128)} %get-tuple-element.120) | copy-start | bytes 7077892
  538.9 14.9 %all-to-all-start.2 = ((f32[16,1,3960]{2,1,0:T(1,128)}), f32[16,1,3960]{2,1,0:T(1,128)S(1)}, u32[]{:S(2)}, u32[]{:S(2)}) async-start(f32[16,1,3960]{2,1,0:T(1,128)} %all_to_all.25), calls=%async_computation.2 | async-start | bytes 507904 | tf_op jit(solution)/shard_map/all_to_all | solution.py:801
  554.2 4.8 collective-permute-start.27
  556.2 20.1 %collective-permute-start.29 = (bf16[2,72,1152]{2,1,0:T(8,128)(2,1)}, bf16[2,72,1152]{2,1,0:T(8,128)(2,1)}, u32[]{:S(2)}, u32[]{:S(2)}) collective-permute-start(bf16[2,72,1152]{2,1,0:T(8,128)(2,1)} %dynamic-slice_bitcast_fusion.4), channel_id=1, source_target_pairs={{0,8},{4,12},{8,0},{12,4},{16,24},{20,28},{24,16},{28,20},{1,9},{5... | collective-permute-start | bytes 995336 | tf_op jit(solution)/shard_map/ppermute | solution.py:567
  556.7 16.4 %collective-permute-start.24 = (bf16[2,2,72,1152]{3,2,0,1:T(8,128)(2,1)}, bf16[2,2,72,1152]{3,2,0,1:T(8,128)(2,1)}, u32[]{:S(2)}, u32[]{:S(2)}) collective-permute-start(bf16[2,2,72,1152]{3,2,0,1:T(8,128)(2,1)} %dynamic-slice_bitcast_fusion), channel_id=1, source_target_pairs={{0,1},{1,0},{2,3},{3,2},{4,5},{5,4},{6,7},{7,6},{8,9},{9,8},{10,11... | collective-permute-start | bytes 1990664 | tf_op jit(solution)/shard_map/ppermute | solution.py:567
  564.5 60.4 %all-to-all-start.3 = ((f32[16,1,7704]{2,1,0:T(1,128)}), f32[16,1,7704]{2,1,0:T(1,128)S(1)}, u32[]{:S(2)}, u32[]{:S(2)}) async-start(f32[16,1,7704]{2,1,0:T(1,128)} %all_to_all.28), calls=%async_computation.3 | async-start | bytes 999424 | tf_op jit(solution)/shard_map/all_to_all | solution.py:826
  577.6 22.6 %collective-permute-start.30 = (bf16[72,1152]{1,0:T(8,128)(2,1)S(1)}, bf16[72,1152]{1,0:T(8,128)(2,1)S(1)}, u32[]{:S(2)}, u32[]{:S(2)}) collective-permute-start(bf16[72,1152]{1,0:T(8,128)(2,1)S(1)} %dynamic-slice_bitcast_fusion.6), channel_id=1, source_target_pairs={{0,16},{4,20},{8,24},{12,28},{16,0},{20,4},{24,8},{28,12},{1,17},{... | collective-permute-start | bytes 497672 | tf_op jit(solution)/shard_map/ppermute | solution.py:567
  579.2 20.8 %collective-permute-start.31 = (bf16[2,72,1152]{2,1,0:T(8,128)(2,1)S(1)}, bf16[2,72,1152]{2,1,0:T(8,128)(2,1)S(1)}, u32[]{:S(2)}, u32[]{:S(2)}) collective-permute-start(bf16[2,72,1152]{2,1,0:T(8,128)(2,1)S(1)} %dynamic-slice_bitcast_fusion.3), channel_id=1, source_target_pairs={{0,8},{4,12},{8,0},{12,4},{16,24},{20,28},{24,16},{28,20},{1,9},{5... | collective-permute-start | bytes 995336 | tf_op jit(solution)/shard_map/ppermute | solution.py:567
  581.6 58.3 %collective-permute-start.26 = (bf16[512,1152]{1,0:T(8,128)(2,1)}, bf16[512,1152]{1,0:T(8,128)(2,1)}, u32[]{:S(2)}, u32[]{:S(2)}) collective-permute-start(bf16[512,1152]{1,0:T(8,128)(2,1)} %select_convert_fusion), channel_id=1, source_target_pairs={{1,2},{2,1},{5,6},{6,5},{9,10},{10,9},{13,14},{14,13},{17,18},{18,... | collective-permute-start | bytes 3538952 | tf_op jit(solution)/shard_map/ppermute | solution.py:539
  587.4 50.1 %collective-permute-start.25 = (bf16[512,1152]{1,0:T(8,128)(2,1)S(1)}, bf16[512,1152]{1,0:T(8,128)(2,1)}, u32[]{:S(2)}, u32[]{:S(2)}) collective-permute-start(bf16[512,1152]{1,0:T(8,128)(2,1)S(1)} %fusion.74), channel_id=1, source_target_pairs={{1,2},{2,1},{5,6},{6,5},{9,10},{10,9},{13,14},{14,13},{17,18},{18,... | collective-permute-start | bytes 3538952 | tf_op jit(solution)/shard_map/ppermute | solution.py:539
  600.1 17.0 %collective-permute-start.32 = (bf16[72,1152]{1,0:T(8,128)(2,1)S(1)}, bf16[72,1152]{1,0:T(8,128)(2,1)S(1)}, u32[]{:S(2)}, u32[]{:S(2)}) collective-permute-start(bf16[72,1152]{1,0:T(8,128)(2,1)S(1)} %dynamic-slice_bitcast_fusion.5), channel_id=1, source_target_pairs={{0,16},{4,20},{8,24},{12,28},{16,0},{20,4},{24,8},{28,12},{1,17},{... | collective-permute-start | bytes 497672 | tf_op jit(solution)/shard_map/ppermute | solution.py:567
  617.2 13.9 %copy-start.58 = (bf16[72,576]{1,0:T(8,128)(2,1)S(1)}, bf16[72,576]{1,0:T(8,128)(2,1)}, u32[]{:S(2)}) copy-start(bf16[72,576]{1,0:T(8,128)(2,1)} %reduce-scatter.10.cloned.1.call-done) | copy-start | bytes 248836
  618.2 12.9 %collective-permute-start.33 = (bf16[72,2880]{1,0:T(8,128)(2,1)S(1)}, bf16[72,2880]{1,0:T(8,128)(2,1)}, u32[]{:S(2)}, u32[]{:S(2)}) collective-permute-start(bf16[72,2880]{1,0:T(8,128)(2,1)S(1)} %pad_maximum_fusion.5), channel_id=1, source_target_pairs={{1,2},{2,1},{5,6},{6,5},{9,10},{10,9},{13,14},{14,13},{17,18},{18,... | collective-permute-start | bytes 1244168 | tf_op jit(solution)/shard_map/ppermute | solution.py:539
  (71 other events, 323.8 us)
Sparse Core Ops, SparseCore 0:
  113.6 55.5 all-gather.4
  172.0 89.5 all-gather.2
  340.0 114.6 reduce-scatter.9
  459.2 88.0 reduce-scatter.7
  551.7 88.0 reduce-scatter.5
